TPU v7x, 32 devices: a whole 2x2x4 slice. The times are simulated.
32 devices in a mesh: frame: 8 (over y, x, core), head: 4 (over z).
Axes of the slice: x: 2, y: 2, z: 4, core: 2. Of those that a mesh axis runs over, the one named last changes fastest.
Arguments:
- queries: bfloat16 [1792, 3072], P('frame', 'head'), may hold values from -24 to 24
- key_rows: bfloat16 [1792, 3072], P('frame', 'head'), may hold values from -24 to 24
- value_rows: bfloat16 [1792, 3072], P('frame', 'head'), may hold values from -5 to 5
- ref_keys: bfloat16 [8, 1024, 3072], P('frame', None, 'head'), may hold values from -5 to 5
- ref_values: bfloat16 [8, 1024, 3072], P('frame', None, 'head'), may hold values from -5 to 5
- key_lists: int32 [8, 8], P('frame'), may hold values from 0 to 7, as said below
- list_counts: int32 [8], P('frame'), may hold values from 1 to 7, as said below
- owner_index: int32 [1], replicated, may hold values from 0 to 7
- out_weight: bfloat16 [3072, 3072], P('head'), may hold values from -1.5 to 1.5
- residual: bfloat16 [1792, 3072], P('frame', 'head'), may hold values from -3 to 3
- gate_scale: float32 [3072], P('head'), may hold values from 0.5 to 2
Outputs:
- block_out: bfloat16 [1792, 3072], P('frame', 'head')
Inputs may be any that keep to these rules, and one draw needn't show every extreme that they name: `key_lists`: the first list_counts[f] entries of row f are distinct frames other than f, each within 4 frames of f; the remaining entries equal f. `list_counts`: some frame lists every frame within 4 of it.
All inputs are finite; a program needn't handle non-finite values.
Results may differ from a plain program's by a relative error of at most 0.02.
Values may be sent and summed in bfloat16 or wider, within the bound.
No kernel may reach another device: no remote copies, remote signals or barrier semaphores. Data moves between devices by JAX's collectives and lax.ppermute only.
A program may use at most 64 MiB of HBM per device.

v0:
```python
import math

import jax
import jax.numpy as jnp
from jax import lax
from jax.sharding import PartitionSpec as P

HD = 128
REACH = 4


def broadcast(block, axis, source):
    block = jnp.where(lax.axis_index(axis) == source, block, jnp.zeros_like(block))
    return lax.psum(block, axis)


def from_behind(block, axis, distance):
    devices = range(lax.axis_size(axis))
    route = [(i - distance, i) for i in devices if i - distance in devices]
    return lax.ppermute(block, axis, route)


def absorb(carried, query_heads, key_block, value_block, allowed):
    running_max, running_sum, weighted = carried
    head_count = query_heads.shape[1]
    key_heads = key_block.reshape(key_block.shape[0], head_count, HD)
    value_heads = value_block.reshape(value_block.shape[0], head_count, HD)
    scores = jnp.einsum(
        "qhd,khd->hqk", query_heads, key_heads, preferred_element_type=jnp.float32
    ) * (1.0 / math.sqrt(HD))
    if allowed is not None:
        scores = jnp.where(allowed[None, None, :], scores, -jnp.inf)
    new_max = jnp.maximum(running_max, jnp.max(scores, axis=-1))
    factor = jnp.exp(running_max - new_max)
    weights = jnp.exp(scores - new_max[:, :, None])
    running_sum = running_sum * factor + jnp.sum(weights, axis=-1)
    weighted = weighted * factor.T[:, :, None] + jnp.einsum(
        "hqk,khd->qhd",
        weights.astype(jnp.bfloat16),
        value_heads,
        preferred_element_type=jnp.float32,
    )
    return (new_max, running_sum, weighted)


def frame_block(carried, query_heads, key_block, value_block, begin_row, listed, live_slots):
    frame_of = (begin_row + jnp.arange(key_block.shape[0], dtype=jnp.int32)) // query_heads.shape[0]
    allowed = jnp.any((frame_of[:, None] == listed[None, :]) & live_slots[None, :], axis=1)
    return lax.cond(
        jnp.any(allowed),
        lambda current: absorb(current, query_heads, key_block, value_block, allowed),
        lambda current: current,
        carried,
    )


def per_device(
    queries,
    key_rows,
    value_rows,
    ref_keys,
    ref_values,
    key_lists,
    list_counts,
    owner_index,
    out_weight,
    residual,
    gate_scale,
):
    frame_len = queries.shape[0]
    columns_here = queries.shape[1]
    head_count = columns_here // HD
    query_heads = queries.reshape(frame_len, head_count, HD)
    listed = key_lists[0]
    live_slots = jnp.arange(listed.shape[0], dtype=jnp.int32) < list_counts[0]
    position = lax.axis_index("frame")
    carried = (
        jnp.full((head_count, frame_len), -jnp.inf, jnp.float32),
        jnp.zeros((head_count, frame_len), jnp.float32),
        jnp.zeros((frame_len, head_count, HD), jnp.float32),
    )
    style_keys, style_values = (
        broadcast(ref_keys, "frame", owner_index[0]),
        broadcast(ref_values, "frame", owner_index[0]),
    )
    carried = absorb(carried, query_heads, style_keys[0], style_values[0], None)
    carried = absorb(carried, query_heads, key_rows, value_rows, None)
    for offset in list(range(1, REACH + 1)) + list(range(-REACH, 0)):
        moved_keys, moved_values = from_behind((key_rows, value_rows), "frame", offset)
        carried = frame_block(
            carried,
            query_heads,
            moved_keys,
            moved_values,
            (position - offset) * frame_len,
            listed,
            live_slots,
        )
    running_max, running_sum, weighted = carried
    attended = (
        (weighted / running_sum.T[:, :, None]).astype(jnp.bfloat16).reshape(frame_len, columns_here)
    )
    shares = lax.psum_scatter(
        lax.dot_general(
            out_weight, attended, (((0,), (1,)), ((), ())), preferred_element_type=jnp.float32
        ).astype(jnp.bfloat16),
        "head",
        scatter_dimension=0,
        tiled=True,
    ).astype(jnp.float32)
    return (residual.astype(jnp.float32) + gate_scale[None, :] * shares.T).astype(jnp.bfloat16)


def solution(mesh):
    placed = (
        P("frame", "head"),
        P("frame", "head"),
        P("frame", "head"),
        P("frame", None, "head"),
        P("frame", None, "head"),
        P("frame", None),
        P("frame"),
        P(),
        P("head", None),
        P("frame", "head"),
        P("head"),
    )
    return jax.shard_map(
        per_device, mesh=mesh, in_specs=placed, out_specs=P("frame", "head"), check_vma=False
    )
```

profile of v0, /device:TPU:0, one launch (start us, length us, event | category | flops | bytes accessed | tf_op | source)
XLA Modules:
  0.0 252.8 jit_solution(4590144768342689919)
XLA Ops:
  7.2 1.8 copy.63
  9.1 1.6 copy.70
  10.7 1.4 broadcast_select_fusion
  12.1 2.6 %copy.64 = bf16[1024,6,128]{2,0,1:T(8,128)(2,1)} copy(bf16[1024,6,128]{0,2,1:T(8,128)(2,1)} %bitcast.160) | data formatting | bytes 3145728 | tf_op jit(solution)/shard_map/reshape;squeeze | solution.py:26
  14.7 1.6 copy.71
  16.4 0.9 copy-done.13
  17.4 4.5 %collective-permute-start = (bf16[224,768]{0,1:T(8,128)(2,1)S(1)}, bf16[224,768]{0,1:T(8,128)(2,1)}, u32[]{:S(2)}, u32[]{:S(2)}) collective-permute-start(bf16[224,768]{0,1:T(8,128)(2,1)S(1)} %copy.67), channel_id=1, source_target_pairs={{0,4},{4,8},{8,12},{12,16},{16,20},{20,24},{24,28},{1,5},{5,9},{9,... | collective-permute-start | bytes 1032200 | tf_op jit(solution)/shard_map/ppermute | solution.py:20
  22.0 3.0 %collective-permute-start.2 = (bf16[224,768]{0,1:T(8,128)(2,1)S(1)}, bf16[224,768]{0,1:T(8,128)(2,1)}, u32[]{:S(2)}, u32[]{:S(2)}) collective-permute-start(bf16[224,768]{0,1:T(8,128)(2,1)S(1)} %copy.67), channel_id=1, source_target_pairs={{0,8},{4,12},{8,16},{12,20},{16,24},{20,28},{1,9},{5,13},{9,17},{1... | collective-permute-start | bytes 1032200 | tf_op jit(solution)/shard_map/ppermute | solution.py:20
  25.2 4.0 %collective-permute-start.1 = (bf16[224,768]{0,1:T(8,128)(2,1)S(1)}, bf16[224,768]{0,1:T(8,128)(2,1)}, u32[]{:S(2)}, u32[]{:S(2)}) collective-permute-start(bf16[224,768]{0,1:T(8,128)(2,1)S(1)} %copy.72), channel_id=1, source_target_pairs={{0,4},{4,8},{8,12},{12,16},{16,20},{20,24},{24,28},{1,5},{5,9},{9,... | collective-permute-start | bytes 1032200 | tf_op jit(solution)/shard_map/ppermute | solution.py:20
  29.1 2.7 %collective-permute-start.3 = (bf16[224,768]{0,1:T(8,128)(2,1)S(1)}, bf16[224,768]{0,1:T(8,128)(2,1)}, u32[]{:S(2)}, u32[]{:S(2)}) collective-permute-start(bf16[224,768]{0,1:T(8,128)(2,1)S(1)} %copy.72), channel_id=1, source_target_pairs={{0,8},{4,12},{8,16},{12,20},{16,24},{20,28},{1,9},{5,13},{9,17},{1... | collective-permute-start | bytes 1032200 | tf_op jit(solution)/shard_map/ppermute | solution.py:20
  31.8 1.3 collective-permute-start.4
  34.1 0.9 fusion.92
  40.3 80.5 %all-reduce.3.cloned.1.call-done = (bf16[1024,6,128]{2,0,1:T(8,128)(2,1)}, bf16[1024,6,128]{2,0,1:T(8,128)(2,1)}) async-done(((bf16[1024,6,128]{2,0,1:T(8,128)(2,1)}, bf16[1024,6,128]{2,0,1:T(8,128)(2,1)}), (bf16[1024,6,128]{2,0,1:T(8,128)(2,1)}, bf16[1024,6,128]{2,0,1:T(8,128)(2,1)})) %all-reduce.3.cloned.1.call-update) | async-done | bytes 3145744 | tf_op jit(solution)/shard_map/psum | solution.py:14
  120.8 2.5 %bitcast_reduce_fusion = (f32[6,224]{1,0:T(8,128)S(1)}, f32[6,1024,224]{1,2,0:T(8,128)S(1)}) fusion(bf16[1024,6,128]{2,0,1:T(8,128)(2,1)} %get-tuple-element.347, bf16[224,6,128]{0,2,1:T(8,128)(2,1)S(1)} %bitcast.150), kind=kOutput, calls=%fused_computation.89 | convolution fusion | flops 355072704 | bytes 7427328 | tf_op jit(solution)/shard_map/qhd,khd->hqk/dot_general | solution.py:28
  123.6 3.4 %collective-permute-start.5 = (bf16[224,768]{0,1:T(8,128)(2,1)S(1)}, bf16[224,768]{0,1:T(8,128)(2,1)}, u32[]{:S(2)}, u32[]{:S(2)}) collective-permute-start(bf16[224,768]{0,1:T(8,128)(2,1)S(1)} %copy.72), channel_id=1, source_target_pairs={{0,12},{4,16},{8,20},{12,24},{16,28},{1,13},{5,17},{9,21},{13,25},... | collective-permute-start | bytes 1032200 | tf_op jit(solution)/shard_map/ppermute | solution.py:20
  127.0 1.9 fusion.71
  129.0 2.1 collective-permute-start.6
  131.1 1.3 collective-permute-start.7
  132.4 1.3 collective-permute-start.8
  133.7 1.3 collective-permute-start.9
  135.1 1.3 collective-permute-start.10
  136.4 1.1 fusion.58
  137.5 3.5 %collective-permute-done.6 = bf16[224,768]{0,1:T(8,128)(2,1)S(1)} collective-permute-done((bf16[224,768]{0,1:T(8,128)(2,1)S(1)}, bf16[224,768]{0,1:T(8,128)(2,1)S(1)}, u32[]{:S(2)}, u32[]{:S(2)}) %collective-permute-start.6) | collective-permute-done | bytes 344096 | tf_op jit(solution)/shard_map/ppermute | solution.py:20
  141.0 1.3 collective-permute-start.11
  142.3 7.1 %collective-permute-done.7 = bf16[224,768]{0,1:T(8,128)(2,1)S(1)} collective-permute-done((bf16[224,768]{0,1:T(8,128)(2,1)S(1)}, bf16[224,768]{0,1:T(8,128)(2,1)S(1)}, u32[]{:S(2)}, u32[]{:S(2)}) %collective-permute-start.7) | collective-permute-done | bytes 344096 | tf_op jit(solution)/shard_map/ppermute | solution.py:20
  149.4 1.3 collective-permute-start.12
  150.7 1.3 collective-permute-start.13
  152.0 1.7 collective-permute-done.9
  153.7 1.3 collective-permute-start.14
  155.1 1.3 collective-permute-start.15
  156.4 0.4 fusion.64
  156.9 1.0 copy-done.2
  157.9 1.0 copy-done.10
  159.0 1.0 copy-done.6
  160.1 1.4 conditional.12
  160.8 0.8 fusion.29
  161.6 2.4 conditional.13
  162.3 1.7 fusion.36
  164.0 5.3 %collective-permute-done.13 = bf16[224,768]{0,1:T(8,128)(2,1)} collective-permute-done((bf16[224,768]{0,1:T(8,128)(2,1)S(1)}, bf16[224,768]{0,1:T(8,128)(2,1)}, u32[]{:S(2)}, u32[]{:S(2)}) %collective-permute-start.13) | collective-permute-done | bytes 344096 | tf_op jit(solution)/shard_map/ppermute | solution.py:20
  169.3 3.4 %conditional.14 = ((f32[6,224]{1,0:T(8,128)S(1)}, f32[6,224]{1,0:T(8,128)S(1)}, f32[224,6,128]{2,0,1:T(8,128)S(1)})) conditional(s32[]{:T(128)} %convert_element_type.74, (f32[6,224]{1,0:T(8,128)S(1)}, f32[6,224]{1,0:T(8,128)S(1)}, f32[224,6,128]{2,0,1:T(8,128)S(1)}) %get-tuple-element.458, (pred[224,8]{0,1:T(8,128)(4,1)S(1)}, ...), branch_computations={%region_44.45_spmd, %region_45.49_spmd} | conditional | flops 156597728 | bytes 6109409 | solution.py:49
  169.4 1.4 fusion.103
  171.0 1.7 fusion.43
  172.8 3.5 %conditional.15 = ((f32[6,224]{1,0:T(8,128)S(1)}, f32[224,6,128]{2,0,1:T(8,128)S(1)})) conditional(s32[]{:T(128)} %convert_element_type.73, (f32[6,224]{1,0:T(8,128)S(1)}, f32[224,6,128]{2,0,1:T(8,128)S(1)}) %tuple.63, (pred[224,8]{0,1:T(8,128)(4,1)S(1)}, bf16[224,768]{0,1:T(8,128)(2,1)}, bf16[224,6,128]{0,2,1:T(8,128)(2,1)S(1)}, ...), branch_computations={%region_49.50_spmd, %region_50.54_spmd} | conditional | flops 156597728 | bytes 6098649 | solution.py:49
  172.8 1.4 fusion.104
  174.5 1.7 fusion.50
  176.7 4.7 %fusion.59 = bf16[3072,224]{0,1:T(8,128)(2,1)} fusion(bf16[224,768]{0,1:T(8,128)(2,1)S(1)} %bitcast.170, bf16[768,3072]{1,0:T(8,128)(2,1)} %param.35), kind=kOutput, calls=%fused_computation.94 | convolution fusion | flops 1057652736 | bytes 6438912 | tf_op jit(solution)/shard_map/dot_general | solution.py:104
  181.4 62.7 %reduce-scatter.2.cloned.1.call-done = bf16[768,224]{0,1:T(8,128)(2,1)} async-done(((bf16[3072,224]{0,1:T(8,128)(2,1)}), bf16[768,224]{0,1:T(8,128)(2,1)}) %reduce-scatter.2.cloned.1.call-update) | async-done | bytes 344080 | tf_op jit(solution)/shard_map/reduce_scatter | solution.py:103
  244.2 1.8 fusion.77
  (90 shorter events, 3.9 us)
Async XLA Ops:
  6.5 114.3 %all-reduce.3.cloned.1.call-start = ((), (), s32[]{:S(2)}) async-start(), calls=%async_computation.2 | async-start | bytes 6291456 | tf_op jit(solution)/shard_map/psum | solution.py:14
  7.2 1.9 copy-start
  16.3 1.0 copy-start.13
  16.3 8.7 %copy-start.14 = (bf16[224,768]{1,0:T(8,128)(2,1)S(1)}, bf16[224,768]{1,0:T(8,128)(2,1)}, u32[]{:S(2)}) copy-start(bf16[224,768]{1,0:T(8,128)(2,1)} %param.29) | copy-start | bytes 1032196
  16.3 16.8 %copy-start.15 = (bf16[224,768]{1,0:T(8,128)(2,1)S(1)}, bf16[224,768]{1,0:T(8,128)(2,1)}, u32[]{:S(2)}) copy-start(bf16[224,768]{1,0:T(8,128)(2,1)} %param.27) | copy-start | bytes 1032196
  16.3 17.7 %copy-start.18 = (s32[1,8]{1,0:T(1,128)S(1)}, s32[1,8]{1,0:T(1,128)}, u32[]{:S(2)}) copy-start(s32[1,8]{1,0:T(1,128)} %param.32) | copy-start | bytes 100
  16.3 227.8 %reduce-scatter.2.cloned.1.call-start = ((), (), s32[]{:S(2)}) async-start(), calls=%async_computation.1 | async-start | bytes 1720320 | tf_op jit(solution)/shard_map/reduce_scatter | solution.py:103
  17.4 106.2 %collective-permute-start = (bf16[224,768]{0,1:T(8,128)(2,1)S(1)}, bf16[224,768]{0,1:T(8,128)(2,1)}, u32[]{:S(2)}, u32[]{:S(2)}) collective-permute-start(bf16[224,768]{0,1:T(8,128)(2,1)S(1)} %copy.67), channel_id=1, source_target_pairs={{0,4},{4,8},{8,12},{12,16},{16,20},{20,24},{24,28},{1,5},{5,9},{9,... | collective-permute-start | bytes 1032200 | tf_op jit(solution)/shard_map/ppermute | solution.py:20
  22.0 109.1 %collective-permute-start.2 = (bf16[224,768]{0,1:T(8,128)(2,1)S(1)}, bf16[224,768]{0,1:T(8,128)(2,1)}, u32[]{:S(2)}, u32[]{:S(2)}) collective-permute-start(bf16[224,768]{0,1:T(8,128)(2,1)S(1)} %copy.67), channel_id=1, source_target_pairs={{0,8},{4,12},{8,16},{12,20},{16,24},{20,28},{1,9},{5,13},{9,17},{1... | collective-permute-start | bytes 1032200 | tf_op jit(solution)/shard_map/ppermute | solution.py:20
  25.2 103.8 %collective-permute-start.1 = (bf16[224,768]{0,1:T(8,128)(2,1)S(1)}, bf16[224,768]{0,1:T(8,128)(2,1)}, u32[]{:S(2)}, u32[]{:S(2)}) collective-permute-start(bf16[224,768]{0,1:T(8,128)(2,1)S(1)} %copy.72), channel_id=1, source_target_pairs={{0,4},{4,8},{8,12},{12,16},{16,20},{20,24},{24,28},{1,5},{5,9},{9,... | collective-permute-start | bytes 1032200 | tf_op jit(solution)/shard_map/ppermute | solution.py:20
  29.1 103.3 %collective-permute-start.3 = (bf16[224,768]{0,1:T(8,128)(2,1)S(1)}, bf16[224,768]{0,1:T(8,128)(2,1)}, u32[]{:S(2)}, u32[]{:S(2)}) collective-permute-start(bf16[224,768]{0,1:T(8,128)(2,1)S(1)} %copy.72), channel_id=1, source_target_pairs={{0,8},{4,12},{8,16},{12,20},{16,24},{20,28},{1,9},{5,13},{9,17},{1... | collective-permute-start | bytes 1032200 | tf_op jit(solution)/shard_map/ppermute | solution.py:20
  31.8 101.9 %collective-permute-start.4 = (bf16[224,768]{0,1:T(8,128)(2,1)S(1)}, bf16[224,768]{0,1:T(8,128)(2,1)S(1)}, u32[]{:S(2)}, u32[]{:S(2)}) collective-permute-start(bf16[224,768]{0,1:T(8,128)(2,1)S(1)} %copy.67), channel_id=1, source_target_pairs={{0,12},{4,16},{8,20},{12,24},{16,28},{1,13},{5,17},{9,21},{13,25},... | collective-permute-start | bytes 1032200 | tf_op jit(solution)/shard_map/ppermute | solution.py:20
  120.8 6.2 %copy-start.19 = (bf16[1024,6,128]{2,0,1:T(8,128)(2,1)S(1)}, bf16[1024,6,128]{2,0,1:T(8,128)(2,1)}, u32[]{:S(2)}) copy-start(bf16[1024,6,128]{2,0,1:T(8,128)(2,1)} %get-tuple-element.348) | copy-start | bytes 4718596
  123.6 11.4 %collective-permute-start.5 = (bf16[224,768]{0,1:T(8,128)(2,1)S(1)}, bf16[224,768]{0,1:T(8,128)(2,1)}, u32[]{:S(2)}, u32[]{:S(2)}) collective-permute-start(bf16[224,768]{0,1:T(8,128)(2,1)S(1)} %copy.72), channel_id=1, source_target_pairs={{0,12},{4,16},{8,20},{12,24},{16,28},{1,13},{5,17},{9,21},{13,25},... | collective-permute-start | bytes 1032200 | tf_op jit(solution)/shard_map/ppermute | solution.py:20
  129.0 12.0 %collective-permute-start.6 = (bf16[224,768]{0,1:T(8,128)(2,1)S(1)}, bf16[224,768]{0,1:T(8,128)(2,1)S(1)}, u32[]{:S(2)}, u32[]{:S(2)}) collective-permute-start(bf16[224,768]{0,1:T(8,128)(2,1)S(1)} %copy.67), channel_id=1, source_target_pairs={{0,16},{4,20},{8,24},{12,28},{1,17},{5,21},{9,25},{13,29},{2,18},{... | collective-permute-start | bytes 1032200 | tf_op jit(solution)/shard_map/ppermute | solution.py:20
  131.1 18.3 %collective-permute-start.7 = (bf16[224,768]{0,1:T(8,128)(2,1)S(1)}, bf16[224,768]{0,1:T(8,128)(2,1)S(1)}, u32[]{:S(2)}, u32[]{:S(2)}) collective-permute-start(bf16[224,768]{0,1:T(8,128)(2,1)S(1)} %copy.72), channel_id=1, source_target_pairs={{0,16},{4,20},{8,24},{12,28},{1,17},{5,21},{9,25},{13,29},{2,18},{... | collective-permute-start | bytes 1032200 | tf_op jit(solution)/shard_map/ppermute | solution.py:20
  132.4 18.3 %collective-permute-start.8 = (bf16[224,768]{0,1:T(8,128)(2,1)S(1)}, bf16[224,768]{0,1:T(8,128)(2,1)S(1)}, u32[]{:S(2)}, u32[]{:S(2)}) collective-permute-start(bf16[224,768]{0,1:T(8,128)(2,1)S(1)} %copy.67), channel_id=1, source_target_pairs={{16,0},{20,4},{24,8},{28,12},{17,1},{21,5},{25,9},{29,13},{18,2},{... | collective-permute-start | bytes 1032200 | tf_op jit(solution)/shard_map/ppermute | solution.py:20
  133.7 3.7 %copy-start.1 = (bf16[224,768]{0,1:T(8,128)(2,1)}, bf16[224,768]{0,1:T(8,128)(2,1)S(1)}, u32[]{:S(2)}) copy-start(bf16[224,768]{0,1:T(8,128)(2,1)S(1)} %collective-permute-done.4) | copy-start | bytes 1032196
  133.7 20.0 %collective-permute-start.9 = (bf16[224,768]{0,1:T(8,128)(2,1)S(1)}, bf16[224,768]{0,1:T(8,128)(2,1)S(1)}, u32[]{:S(2)}, u32[]{:S(2)}) collective-permute-start(bf16[224,768]{0,1:T(8,128)(2,1)S(1)} %copy.72), channel_id=1, source_target_pairs={{16,0},{20,4},{24,8},{28,12},{17,1},{21,5},{25,9},{29,13},{18,2},{... | collective-permute-start | bytes 1032200 | tf_op jit(solution)/shard_map/ppermute | solution.py:20
  135.1 20.0 %collective-permute-start.10 = (bf16[224,768]{0,1:T(8,128)(2,1)S(1)}, bf16[224,768]{0,1:T(8,128)(2,1)S(1)}, u32[]{:S(2)}, u32[]{:S(2)}) collective-permute-start(bf16[224,768]{0,1:T(8,128)(2,1)S(1)} %copy.67), channel_id=1, source_target_pairs={{12,0},{16,4},{20,8},{24,12},{28,16},{13,1},{17,5},{21,9},{25,13},... | collective-permute-start | bytes 1032200 | tf_op jit(solution)/shard_map/ppermute | solution.py:20
  141.0 15.8 %copy-start.9 = (bf16[224,768]{0,1:T(8,128)(2,1)}, bf16[224,768]{0,1:T(8,128)(2,1)S(1)}, u32[]{:S(2)}) copy-start(bf16[224,768]{0,1:T(8,128)(2,1)S(1)} %collective-permute-done.6) | copy-start | bytes 1032196
  141.0 20.6 %collective-permute-start.11 = (bf16[224,768]{0,1:T(8,128)(2,1)S(1)}, bf16[224,768]{0,1:T(8,128)(2,1)}, u32[]{:S(2)}, u32[]{:S(2)}) collective-permute-start(bf16[224,768]{0,1:T(8,128)(2,1)S(1)} %copy.72), channel_id=1, source_target_pairs={{12,0},{16,4},{20,8},{24,12},{28,16},{13,1},{17,5},{21,9},{25,13},... | collective-permute-start | bytes 1032200 | tf_op jit(solution)/shard_map/ppermute | solution.py:20
  149.4 7.4 %copy-start.11 = (bf16[224,768]{0,1:T(8,128)(2,1)}, bf16[224,768]{0,1:T(8,128)(2,1)S(1)}, u32[]{:S(2)}) copy-start(bf16[224,768]{0,1:T(8,128)(2,1)S(1)} %collective-permute-done.7) | copy-start | bytes 1032196
  149.4 14.6 %collective-permute-start.12 = (bf16[224,768]{0,1:T(8,128)(2,1)S(1)}, bf16[224,768]{0,1:T(8,128)(2,1)}, u32[]{:S(2)}, u32[]{:S(2)}) collective-permute-start(bf16[224,768]{0,1:T(8,128)(2,1)S(1)} %copy.67), channel_id=1, source_target_pairs={{8,0},{12,4},{16,8},{20,12},{24,16},{28,20},{9,1},{13,5},{17,9},{2... | collective-permute-start | bytes 1032200 | tf_op jit(solution)/shard_map/ppermute | solution.py:20
  150.7 6.1 %copy-start.5 = (bf16[224,768]{0,1:T(8,128)(2,1)}, bf16[224,768]{0,1:T(8,128)(2,1)S(1)}, u32[]{:S(2)}) copy-start(bf16[224,768]{0,1:T(8,128)(2,1)S(1)} %collective-permute-done.8) | copy-start | bytes 1032196
  150.7 18.6 %collective-permute-start.13 = (bf16[224,768]{0,1:T(8,128)(2,1)S(1)}, bf16[224,768]{0,1:T(8,128)(2,1)}, u32[]{:S(2)}, u32[]{:S(2)}) collective-permute-start(bf16[224,768]{0,1:T(8,128)(2,1)S(1)} %copy.72), channel_id=1, source_target_pairs={{8,0},{12,4},{16,8},{20,12},{24,16},{28,20},{9,1},{13,5},{17,9},{2... | collective-permute-start | bytes 1032200 | tf_op jit(solution)/shard_map/ppermute | solution.py:20
  153.7 3.1 %copy-start.7 = (bf16[224,768]{0,1:T(8,128)(2,1)}, bf16[224,768]{0,1:T(8,128)(2,1)S(1)}, u32[]{:S(2)}) copy-start(bf16[224,768]{0,1:T(8,128)(2,1)S(1)} %collective-permute-done.9) | copy-start | bytes 1032196
  153.7 19.0 %collective-permute-start.14 = (bf16[224,768]{0,1:T(8,128)(2,1)S(1)}, bf16[224,768]{0,1:T(8,128)(2,1)}, u32[]{:S(2)}, u32[]{:S(2)}) collective-permute-start(bf16[224,768]{0,1:T(8,128)(2,1)S(1)} %copy.67), channel_id=1, source_target_pairs={{4,0},{8,4},{12,8},{16,12},{20,16},{24,20},{28,24},{5,1},{9,5},{13... | collective-permute-start | bytes 1032200 | tf_op jit(solution)/shard_map/ppermute | solution.py:20
  155.0 1.8 copy-start.3
  155.1 17.7 %collective-permute-start.15 = (bf16[224,768]{0,1:T(8,128)(2,1)S(1)}, bf16[224,768]{0,1:T(8,128)(2,1)}, u32[]{:S(2)}, u32[]{:S(2)}) collective-permute-start(bf16[224,768]{0,1:T(8,128)(2,1)S(1)} %copy.72), channel_id=1, source_target_pairs={{4,0},{8,4},{12,8},{16,12},{20,16},{24,20},{28,24},{5,1},{9,5},{13... | collective-permute-start | bytes 1032200 | tf_op jit(solution)/shard_map/ppermute | solution.py:20
  156.9 1.0 copy-start.2
  157.9 1.0 copy-start.10
  157.9 1.1 copy-start.12
  159.0 1.0 copy-start.6
  159.0 1.1 copy-start.8
  160.1 1.5 copy-start.4
  181.4 62.8 %copy-start.16 = (bf16[224,768]{1,0:T(8,128)(2,1)S(1)}, bf16[224,768]{1,0:T(8,128)(2,1)}, u32[]{:S(2)}) copy-start(bf16[224,768]{1,0:T(8,128)(2,1)} %param.36) | copy-start | bytes 1032196
  181.4 62.8 %copy-start.17 = (f32[768]{0:T(1024)S(1)}, f32[768]{0:T(1024)}, u32[]{:S(2)}) copy-start(f32[768]{0:T(1024)} %param.37) | copy-start | bytes 9220
Sparse Core Ops, SparseCore 0:
  16.4 104.3 all-reduce.2
  181.5 62.5 reduce-scatter.1
where the time goes:
time: 254 us; the launch traced here: 253 us
  waiting for transfers between devices  161 us (63%)
  starting transfers between devices  32.7 us (13%)
  between operations  20.2 us (8%)
  matrix products  19.6 us (8%)
  local copies, waits for them, and re-layouts  12.5 us (5%)
  other arithmetic  6.73 us (3%)
    psum x1, waiting for transfers between devices, broadcast(): return lax.psum(block, axis)  80.5 us
    reduce_scatter x1, waiting for transfers between devices, per_device(): lax.psum_scatter(lax.dot_general(out_weight, attended, (((0,), (1,)), (()...  62.7 us
    ppermute x16, starting transfers between devices, from_behind(): return lax.ppermute(block, axis, route)  32.6 us
    ppermute x16, waiting for transfers between devices, from_behind(): return lax.ppermute(block, axis, route)  17.7 us
    dot_general x6, matrix products, absorb(): jnp.einsum('hqk,khd->qhd', weights.astype(jnp.bfloat16), value_heads, pre...  8.35 us
    unnamed x45, local copies, waits for them, and re-layouts  8.14 us
    dot_general x6, matrix products, absorb(): jnp.einsum('qhd,khd->hqk', query_heads, key_heads, preferred_element_type...  6.54 us
  transfers between devices with their start and end apart: 18, of which 6 were waited for; matrix products, arithmetic and copies ran while one was open for 6% of the time, Pallas kernels for 0%

commit v1 on v0

--- a/solution.py
+++ b/solution.py
@@ -1,12 +1,17 @@
+import functools
 import math
 
 import jax
 import jax.numpy as jnp
 from jax import lax
+from jax.experimental import pallas as pl
+from jax.experimental.pallas import tpu as pltpu
 from jax.sharding import PartitionSpec as P
 
 HD = 128
 REACH = 4
+LOG2E = 1.4426950408889634
+VMEM_LIMIT = 48 * 1024 * 1024
 
 
 def broadcast(block, axis, source):
@@ -54,7 +59,7 @@
     )
 
 
-def per_device(
+def general_device(
     queries,
     key_rows,
     value_rows,
@@ -111,6 +116,321 @@
     return (residual.astype(jnp.float32) + gate_scale[None, :] * shares.T).astype(jnp.bfloat16)
 
 
+CORE, ROW, COLUMN = 1, 2, 4
+PAD = 256
+SLOTS = (0, 2, 4, 6, 1, 3, 5, 7)
+
+
+def swap(block, axis, bit):
+    return lax.ppermute(block, axis, [(i, i ^ bit) for i in range(lax.axis_size(axis))])
+
+
+def halves(width):
+    x = (lax.axis_index("frame") // ROW) % 2
+    mine = pl.multiple_of(x * width, HD)
+    other = pl.multiple_of((1 - x) * width, HD)
+    return mine, other
+
+
+def visible(frame, lists, counts):
+    seen = frame == lax.axis_index("frame")
+    for j in range(lists.shape[1]):
+        seen = seen | ((lists[0, j] == frame) & (j < counts[0]))
+    return seen
+
+
+def split_kernel(lists, counts, q, k, v, kv_keep, kv_send, q_keep, q_send):
+    rows, width = q_keep.shape
+    mine, other = halves(width)
+    kv_send[:rows, :] = k[:, pl.ds(other, width)]
+    kv_send[rows:, :] = v[:, pl.ds(other, width)]
+    kv_keep[:rows, :] = k[:, pl.ds(mine, width)]
+    kv_keep[rows:, :] = v[:, pl.ds(mine, width)]
+    q_keep[...] = q[:, pl.ds(mine, width)]
+    q_send[:rows, :] = q[:, pl.ds(other, width)]
+    lane = lax.broadcasted_iota(jnp.int32, (16, width), 1)
+    flags = jnp.zeros((16, width), jnp.float32)
+    for g in range(lax.axis_size("frame")):
+        flag = jnp.where(visible(g, lists, counts), 1.0, 0.0)
+        flags = jnp.where(lane == g, flag, flags)
+    q_send[rows:, :] = flags.astype(jnp.bfloat16)
+
+
+def pick_kernel(owner, k, v, from_even, from_odd, send_a, send_b, keep, sems):
+    chunk, width = send_a.shape
+    mine, other = halves(width)
+    core = lax.axis_index("frame") % 2
+    owner_core = owner[0] % 2
+
+    def take(src):
+        copies = [
+            pltpu.make_async_copy(
+                src.at[0, pl.ds(0, chunk), pl.ds(other, width)], send_a, sems.at[0]
+            ),
+            pltpu.make_async_copy(
+                src.at[0, pl.ds(chunk, chunk), pl.ds(other, width)], send_b, sems.at[1]
+            ),
+            pltpu.make_async_copy(src.at[0, :, pl.ds(mine, width)], keep, sems.at[2]),
+        ]
+        for copy in copies:
+            copy.start()
+        for copy in copies:
+            copy.wait()
+
+    for at, here, there in ((0, k, from_odd), (1, v, from_even)):
+        pl.when((core == at) & (owner_core == at))(functools.partial(take, here))
+        pl.when((core == at) & (owner_core != at))(functools.partial(take, there))
+
+
+NT = (((1,), (1,)), ((), ()))
+TN = (((0,), (0,)), ((), ()))
+
+
+def absorb_chunk(query, keys, values, biases, state):
+    scale = LOG2E / math.sqrt(HD)
+    scores = [lax.dot_general(k, query, NT, preferred_element_type=jnp.float32) for k in keys]
+    top = None
+    for s, b in zip(scores, biases):
+        t = jnp.max(s, axis=0, keepdims=True) * scale
+        t = t if b is None else t + b
+        top = t if top is None else jnp.maximum(top, t)
+    if state is not None:
+        old_top, old_sum, old_acc = state
+        top = jnp.maximum(old_top, top)
+    total, acc = None, None
+    for s, b, v in zip(scores, biases, values):
+        shift = top if b is None else top - b
+        p = jnp.exp2(s * scale - shift)
+        part = jnp.sum(p, axis=0, keepdims=True)
+        total = part if total is None else total + part
+        o = lax.dot_general(v, p.astype(jnp.bfloat16), TN, preferred_element_type=jnp.float32)
+        acc = o if acc is None else acc + o
+    if state is not None:
+        factor = jnp.exp2(old_top - top)
+        total = total + old_sum * factor
+        acc = acc + old_acc * factor
+    return top, total, acc
+
+
+def frames_kernel(lists, counts, q_keep, q_got, *rest):
+    kv = rest[: len(SLOTS)]
+    acc_out, stat_out, q_pad = rest[len(SLOTS) :]
+    rows, width = q_keep.shape
+    heads = width // HD
+    here = lax.axis_index("frame")
+    q_pad[...] = jnp.zeros_like(q_pad)
+    q_pad[:rows, :] = q_keep[...]
+    q_pad[PAD : PAD + rows, :] = q_got[:rows, :]
+    flags = q_got[rows : rows + 16, :].astype(jnp.float32)
+    lane = lax.broadcasted_iota(jnp.int32, (16, width), 1)
+    side = lax.broadcasted_iota(jnp.int32, (1, 2 * PAD), 1)
+    biases = []
+    for bit in SLOTS:
+        frame = here ^ bit
+        own = jnp.where(visible(frame, lists, counts), 0.0, -jnp.inf)
+        seen = jnp.max(jnp.where(lane == frame, flags, 0.0), keepdims=True)
+        theirs = jnp.where(seen > 0.5, 0.0, -jnp.inf)
+        biases.append(jnp.where(side < PAD, own, theirs))
+    stat_out[...] = jnp.zeros_like(stat_out)
+    for h in range(heads):
+        cols = slice(h * HD, (h + 1) * HD)
+        query = q_pad[:, cols]
+        state = None
+        for s in range(0, len(SLOTS), 2):
+            state = absorb_chunk(
+                query,
+                [kv[s][:rows, cols], kv[s + 1][:rows, cols]],
+                [kv[s][rows:, cols], kv[s + 1][rows:, cols]],
+                biases[s : s + 2],
+                state,
+            )
+        top, total, acc = state
+        stat_out[h : h + 1, :] = top
+        stat_out[heads + h : heads + h + 1, :] = total
+        acc_out[cols, :] = acc
+
+
+def style_kernel(last, q_pad, held, swapped, acc_in, stat_in, *rest):
+    outs, (keys, values) = rest[:2], rest[2:]
+    chunk, width = keys.shape
+    heads = width // HD
+    core = lax.axis_index("frame") % 2
+
+    @pl.when(core == 0)
+    def _():
+        keys[...] = held[...]
+        values[...] = swapped[...]
+
+    @pl.when(core == 1)
+    def _():
+        keys[...] = swapped[...]
+        values[...] = held[...]
+
+    if not last:
+        acc_out, stat_out = outs
+        stat_out[...] = jnp.zeros_like(stat_out)
+    for h in range(heads):
+        cols = slice(h * HD, (h + 1) * HD)
+        state = (stat_in[h : h + 1, :], stat_in[heads + h : heads + h + 1, :], acc_in[cols, :])
+        top, total, acc = absorb_chunk(
+            q_pad[:, cols], [keys[:, cols]], [values[:, cols]], [None], state
+        )
+        if last:
+            own, theirs = outs
+            rows = own.shape[0]
+            done = (acc / total).T.astype(jnp.bfloat16)
+            own[:, cols] = done[:rows, :]
+            theirs[:, cols] = done[PAD : PAD + rows, :]
+        else:
+            stat_out[h : h + 1, :] = top
+            stat_out[heads + h : heads + h + 1, :] = total
+            acc_out[cols, :] = acc
+
+
+def project_kernel(order, own, got, weight, *rest):
+    outs, (blocks, sems) = rest[: len(order)], rest[len(order) :]
+    width = own.shape[1]
+    columns = outs[0].shape[1]
+    mine, other = halves(width)
+    place = lax.axis_index("head")
+    copies = []
+    for i, bit in enumerate(order):
+        start = pl.multiple_of((place ^ bit) * columns, HD)
+        copies.append(
+            pltpu.make_async_copy(weight.at[:, pl.ds(start, columns)], blocks.at[i], sems.at[i])
+        )
+        copies[-1].start()
+    for i, out in enumerate(outs):
+        copies[i].wait()
+        share = jnp.dot(
+            own[...], blocks[i, pl.ds(mine, width), :], preferred_element_type=jnp.float32
+        ) + jnp.dot(got[...], blocks[i, pl.ds(other, width), :], preferred_element_type=jnp.float32)
+        out[...] = share.astype(out.dtype)
+
+
+SMEM = pl.BlockSpec(memory_space=pltpu.SMEM)
+VMEM = pl.BlockSpec(memory_space=pltpu.VMEM)
+ANY = pl.BlockSpec(memory_space=pl.ANY)
+
+
+def call(kernel, in_specs, outs, scratch=(), out_spec=VMEM, flops=0, moved=0, exps=0):
+    shapes = [jax.ShapeDtypeStruct(shape, dtype) for shape, dtype in outs]
+    return pl.pallas_call(
+        kernel,
+        out_shape=shapes,
+        in_specs=in_specs,
+        out_specs=[out_spec] * len(shapes),
+        scratch_shapes=list(scratch),
+        compiler_params=pltpu.CompilerParams(vmem_limit_bytes=VMEM_LIMIT),
+        cost_estimate=pl.CostEstimate(flops=flops, bytes_accessed=moved, transcendentals=exps),
+    )
+
+
+def paired_device(
+    queries,
+    key_rows,
+    value_rows,
+    ref_keys,
+    ref_values,
+    key_lists,
+    list_counts,
+    owner_index,
+    out_weight,
+    residual,
+    gate_scale,
+):
+    bf16, f32 = jnp.bfloat16, jnp.float32
+    rows, columns = queries.shape
+    width = columns // 2
+    heads = width // HD
+    style = ref_keys.shape[1]
+    chunk = style // 2
+    frames, planes = lax.axis_size("frame"), lax.axis_size("head")
+    owner = owner_index[0]
+    here = lax.axis_index("frame")
+
+    even = [(i, i ^ CORE) for i in range(0, frames, 2)]
+    odd = [(i ^ CORE, i) for i in range(0, frames, 2)]
+    from_even = lax.ppermute(ref_values, "frame", even)
+    from_odd = lax.ppermute(ref_keys, "frame", odd)
+
+    kv = (2 * rows, width)
+    kv_keep, kv_send, q_keep, q_send = call(
+        split_kernel,
+        [SMEM, SMEM, VMEM, VMEM, VMEM],
+        [(kv, bf16), (kv, bf16), ((rows, width), bf16), ((rows + 16, width), bf16)],
+        moved=12 * rows * columns,
+    )(key_lists, list_counts, queries, key_rows, value_rows)
+
+    kv_x = swap(kv_send, "frame", ROW)
+    kv_y = swap(kv_keep, "frame", COLUMN)
+    kv_xy = swap(kv_x, "frame", COLUMN)
+
+    part = (chunk, width)
+    send_a, send_b, keep = call(
+        pick_kernel,
+        [SMEM, ANY, ANY, ANY, ANY],
+        [(part, bf16), (part, bf16), ((style, width), bf16)],
+        scratch=[pltpu.SemaphoreType.DMA((3,))],
+        out_spec=ANY,
+        moved=4 * style * columns,
+    )(owner_index, ref_keys, ref_values, from_even, from_odd)
+
+    same_x = (owner // ROW) % 2 == (here // ROW) % 2
+    same_y = (owner // COLUMN) % 2 == (here // COLUMN) % 2
+    held = []
+    for j, sent in enumerate((send_a, send_b)):
+        came = swap(sent, "frame", ROW)
+        chosen = jnp.where(same_x, keep[j * chunk : (j + 1) * chunk], came)
+        came = swap(chosen, "frame", COLUMN)
+        held.append(jnp.where(same_y, chosen, came))
+    q_got = swap(q_send, "frame", ROW)
+
+    near = [kv_keep, kv_x, kv_y, kv_xy]
+    near = near + [swap(block, "frame", CORE) for block in near]
+    state = [((width, 2 * PAD), f32), ((8, 2 * PAD), f32)]
+    pairs = 2 * PAD * width
+    acc, stats, q_pad = call(
+        frames_kernel,
+        [SMEM, SMEM] + [VMEM] * 10,
+        state + [((2 * PAD, width), bf16)],
+        flops=4 * pairs * 8 * rows,
+        exps=2 * PAD * heads * 8 * rows,
+        moved=16 * rows * width * 2,
+    )(key_lists, list_counts, q_keep, q_got, *near)
+
+    scratch = [pltpu.VMEM(part, bf16), pltpu.VMEM(part, bf16)]
+    cost = dict(flops=4 * pairs * chunk, exps=2 * PAD * heads * chunk, moved=8 * chunk * width)
+    acc, stats = call(
+        functools.partial(style_kernel, False), [VMEM] * 5, state, scratch=scratch, **cost
+    )(q_pad, held[0], swap(held[0], "frame", CORE), acc, stats)
+    own, theirs = call(
+        functools.partial(style_kernel, True),
+        [VMEM] * 5,
+        [((rows, width), bf16)] * 2,
+        scratch=scratch,
+        **cost,
+    )(q_pad, held[1], swap(held[1], "frame", CORE), acc, stats)
+    got = swap(theirs, "frame", ROW)
+
+    order = sorted(range(1, planes), key=lambda bit: bit == 1) + [0]
+    shares = call(
+        functools.partial(project_kernel, order),
+        [VMEM, VMEM, ANY],
+        [((rows, columns), bf16)] * (planes - 1) + [((rows, columns), f32)],
+        scratch=[
+            pltpu.VMEM((planes, columns, columns), bf16),
+            pltpu.SemaphoreType.DMA((planes,)),
+        ],
+        flops=2 * rows * columns * columns * planes,
+        moved=2 * columns * columns * planes,
+    )(own, got, out_weight)
+    projected = shares[-1]
+    for bit, share in zip(order, shares[:-1]):
+        projected = projected + swap(share, "head", bit).astype(f32)
+    return (residual.astype(f32) + gate_scale[None, :] * projected).astype(bf16)
+
+
 def solution(mesh):
     placed = (
         P("frame", "head"),
@@ -125,6 +445,22 @@
         P("frame", "head"),
         P("head"),
     )
+
+    def per_device(*args):
+        rows, columns = args[0].shape
+        style = args[3].shape[1]
+        planes = mesh.shape["head"]
+        paired = (
+            mesh.shape["frame"] == 8
+            and planes & (planes - 1) == 0
+            and columns % (2 * HD) == 0
+            and columns // HD <= 8
+            and rows % 16 == 0
+            and rows <= PAD
+            and style % 32 == 0
+        )
+        return (paired_device if paired else general_device)(*args)
+
     return jax.shard_map(
         per_device, mesh=mesh, in_specs=placed, out_specs=P("frame", "head"), check_vma=False
     )

time: 254 us -> 123 us (0.48)
  the two profiles are of different devices: /device:TPU:0 before, /device:TPU:17 now
where the time goes in v1:
time: 123 us; the launch traced here: 121 us
  waiting for transfers between devices  58.2 us (47%)
  starting transfers between devices  39.6 us (32%)
  Pallas kernels  15.3 us (12%)
  local copies, waits for them, and re-layouts  3.98 us (3%)
  other arithmetic  2.14 us (2%)
  between operations  1.47 us (1%)
    ppermute x18, waiting for transfers between devices, swap(): lax.ppermute(block, axis, [(i, i ^ bit) for i in range(lax.axis_size(axis...  55.8 us
    ppermute x18, starting transfers between devices, swap(): lax.ppermute(block, axis, [(i, i ^ bit) for i in range(lax.axis_size(axis...  35.1 us
    pallas_call x1, Pallas kernels, paired_device(): call(frames_kernel, [SMEM, SMEM] + [VMEM] * 10, state + [((2 * PAD, width...  6.52 us
    unnamed x20, local copies, waits for them, and re-layouts  3.98 us
    pallas_call x1, Pallas kernels, paired_device(): call(functools.partial(project_kernel, order), [VMEM, VMEM, ANY], [((rows...  3.94 us
    ppermute x1, starting transfers between devices, paired_device(): from_odd = lax.ppermute(ref_keys, 'frame', odd)  3.23 us
  transfers between devices with their start and end apart: 20, of which 10 were waited for; matrix products, arithmetic and copies ran while one was open for 1% of the time, Pallas kernels for 7%

profile of v1, /device:TPU:17, one launch (start us, length us, event | category | flops | bytes accessed | tf_op | source)
XLA Modules:
  0.0 120.7 jit_solution(10774356457095733369)
XLA Ops:
  0.0 1.3 %collective-permute-start.8 = (bf16[1,1024,768]{2,1,0:T(8,128)(2,1)}, bf16[1,1024,768]{2,1,0:T(8,128)(2,1)S(1)}, u32[]{:S(2)}, u32[]{:S(2)}) collective-permute-start(bf16[1,1024,768]{2,1,0:T(8,128)(2,1)} %v.3), channel_id=1, source_target_pairs={{0,4},{8,12},{16,20},{24,28},{1,5},{9,13},{17,21},{25,29},{2,6},{1... | collective-permute-start | bytes 4718600 | tf_op jit(solution)/shard_map/ppermute | solution.py:354
  1.3 3.2 %collective-permute-start.9 = (bf16[1,1024,768]{2,1,0:T(8,128)(2,1)}, bf16[1,1024,768]{2,1,0:T(8,128)(2,1)S(1)}, u32[]{:S(2)}, u32[]{:S(2)}) collective-permute-start(bf16[1,1024,768]{2,1,0:T(8,128)(2,1)} %k.3), channel_id=1, source_target_pairs={{4,0},{12,8},{20,16},{28,24},{5,1},{13,9},{21,17},{29,25},{6,2},{1... | collective-permute-start | bytes 4718600 | tf_op jit(solution)/shard_map/ppermute | solution.py:355
  5.2 0.3 collective-permute-done.8.from_even
  5.5 2.1 %collective-permute-done.9.from_odd = bf16[1,1024,768]{2,1,0:T(8,128)(2,1)S(1)} collective-permute-done((bf16[1,1024,768]{2,1,0:T(8,128)(2,1)}, bf16[1,1024,768]{2,1,0:T(8,128)(2,1)S(1)}, u32[]{:S(2)}, u32[]{:S(2)}) %collective-permute-start.9) | collective-permute-done | bytes 1572896 | tf_op jit(solution)/shard_map/ppermute | solution.py:355
  7.7 1.1 copy-done.7
  8.8 1.4 %copy-done = bf16[1,1024,768]{2,1,0:T(8,128)(2,1)S(1)} copy-done((bf16[1,1024,768]{2,1,0:T(8,128)(2,1)S(1)}, bf16[1,1024,768]{2,1,0:T(8,128)(2,1)}, u32[]{:S(2)}) %copy-start) | copy-done | bytes 1572888
  10.2 1.4 %copy-done.1 = bf16[1,1024,768]{2,1,0:T(8,128)(2,1)S(1)} copy-done((bf16[1,1024,768]{2,1,0:T(8,128)(2,1)S(1)}, bf16[1,1024,768]{2,1,0:T(8,128)(2,1)}, u32[]{:S(2)}) %copy-start.1) | copy-done | bytes 1572888
  11.6 0.2 shard_map.111
  11.8 1.3 %collective-permute-start.10 = (bf16[512,384]{1,0:T(8,128)(2,1)S(1)}, bf16[512,384]{1,0:T(8,128)(2,1)S(1)}, u32[]{:S(2)}, u32[]{:S(2)}) collective-permute-start(bf16[512,384]{1,0:T(8,128)(2,1)S(1)} %get-tuple-element.29), channel_id=1, source_target_pairs={{0,8},{4,12},{8,0},{12,4},{16,24},{20,28},{24,16},{28,20},{1,9},{5... | collective-permute-start | bytes 1179656 | tf_op jit(solution)/shard_map/ppermute | solution.py:125
  13.1 0.3 collective-permute-start.13
  14.0 0.7 shard_map.109
  14.7 1.3 %collective-permute-start.1 = (bf16[448,384]{1,0:T(8,128)(2,1)S(1)}, bf16[448,384]{1,0:T(8,128)(2,1)S(1)}, u32[]{:S(2)}, u32[]{:S(2)}) collective-permute-start(bf16[448,384]{1,0:T(8,128)(2,1)S(1)} %get-tuple-element.26), channel_id=1, source_target_pairs={{0,8},{4,12},{8,0},{12,4},{16,24},{20,28},{24,16},{28,20},{1,9},{5... | collective-permute-start | bytes 1032200 | tf_op jit(solution)/shard_map/ppermute | solution.py:125
  16.0 4.8 %collective-permute-done.10 = bf16[512,384]{1,0:T(8,128)(2,1)S(1)} collective-permute-done((bf16[512,384]{1,0:T(8,128)(2,1)S(1)}, bf16[512,384]{1,0:T(8,128)(2,1)S(1)}, u32[]{:S(2)}, u32[]{:S(2)}) %collective-permute-start.10) | collective-permute-done | bytes 393248 | tf_op jit(solution)/shard_map/ppermute | solution.py:125
  20.8 8.5 %collective-permute-done.13 = bf16[512,384]{1,0:T(8,128)(2,1)} collective-permute-done((bf16[512,384]{1,0:T(8,128)(2,1)S(1)}, bf16[512,384]{1,0:T(8,128)(2,1)}, u32[]{:S(2)}, u32[]{:S(2)}) %collective-permute-start.13) | collective-permute-done | bytes 393248 | tf_op jit(solution)/shard_map/ppermute | solution.py:125
  29.4 1.1 slice_select_fusion
  30.5 1.3 %collective-permute-start.14 = (bf16[512,384]{1,0:T(8,128)(2,1)S(1)}, bf16[512,384]{1,0:T(8,128)(2,1)}, u32[]{:S(2)}, u32[]{:S(2)}) collective-permute-start(bf16[512,384]{1,0:T(8,128)(2,1)S(1)} %get-tuple-element.41), channel_id=1, source_target_pairs={{0,16},{4,20},{8,24},{12,28},{16,0},{20,4},{24,8},{28,12},{1,17},{... | collective-permute-start | bytes 1179656 | tf_op jit(solution)/shard_map/ppermute | solution.py:125
  31.8 0.2 collective-permute-start.11
  32.0 1.2 %collective-permute-start.2 = (bf16[448,384]{1,0:T(8,128)(2,1)S(1)}, bf16[448,384]{1,0:T(8,128)(2,1)S(1)}, u32[]{:S(2)}, u32[]{:S(2)}) collective-permute-start(bf16[448,384]{1,0:T(8,128)(2,1)S(1)} %get-tuple-element.25.rest_0_), channel_id=1, source_target_pairs={{0,16},{4,20},{8,24},{12,28},{16,0},{20,4},{24,8},{28,12},{1,17},{... | collective-permute-start | bytes 1032200 | tf_op jit(solution)/shard_map/ppermute | solution.py:125
  33.2 3.4 %collective-permute-done.1.rest_1_ = bf16[448,384]{1,0:T(8,128)(2,1)S(1)} collective-permute-done((bf16[448,384]{1,0:T(8,128)(2,1)S(1)}, bf16[448,384]{1,0:T(8,128)(2,1)S(1)}, u32[]{:S(2)}, u32[]{:S(2)}) %collective-permute-start.1) | collective-permute-done | bytes 344096 | tf_op jit(solution)/shard_map/ppermute | solution.py:125
  36.6 1.2 %collective-permute-start.3 = (bf16[448,384]{1,0:T(8,128)(2,1)S(1)}, bf16[448,384]{1,0:T(8,128)(2,1)S(1)}, u32[]{:S(2)}, u32[]{:S(2)}) collective-permute-start(bf16[448,384]{1,0:T(8,128)(2,1)S(1)} %collective-permute-done.1.rest_1_), channel_id=1, source_target_pairs={{0,16},{4,20},{8,24},{12,28},{16,0},{20,4},{24,8},{28,12},{1,17},{... | collective-permute-start | bytes 1032200 | tf_op jit(solution)/shard_map/ppermute | solution.py:125
  37.9 2.9 %collective-permute-start.4 = (bf16[448,384]{1,0:T(8,128)(2,1)S(1)}, bf16[448,384]{1,0:T(8,128)(2,1)S(1)}, u32[]{:S(2)}, u32[]{:S(2)}) collective-permute-start(bf16[448,384]{1,0:T(8,128)(2,1)S(1)} %get-tuple-element.25.rest_0_), channel_id=1, source_target_pairs={{0,4},{4,0},{8,12},{12,8},{16,20},{20,16},{24,28},{28,24},{1,5},{5... | collective-permute-start | bytes 1032200 | tf_op jit(solution)/shard_map/ppermute | solution.py:125
  40.7 0.0 collective-permute-done.14
  40.7 1.2 %collective-permute-start = (bf16[240,384]{1,0:T(8,128)(2,1)S(1)}, bf16[240,384]{1,0:T(8,128)(2,1)S(1)}, u32[]{:S(2)}, u32[]{:S(2)}) collective-permute-start(bf16[240,384]{1,0:T(8,128)(2,1)S(1)} %get-tuple-element.24), channel_id=1, source_target_pairs={{0,8},{4,12},{8,0},{12,4},{16,24},{20,28},{24,16},{28,20},{1,9},{5... | collective-permute-start | bytes 552968 | tf_op jit(solution)/shard_map/ppermute | solution.py:125
  42.0 0.1 broadcast_select_fusion.held
  42.0 3.5 %collective-permute-done.q_got = bf16[240,384]{1,0:T(8,128)(2,1)S(1)} collective-permute-done((bf16[240,384]{1,0:T(8,128)(2,1)S(1)}, bf16[240,384]{1,0:T(8,128)(2,1)S(1)}, u32[]{:S(2)}, u32[]{:S(2)}) %collective-permute-start) | collective-permute-done | bytes 184352 | tf_op jit(solution)/shard_map/ppermute | solution.py:125
  45.5 7.5 %collective-permute-start.5 = (bf16[448,384]{1,0:T(8,128)(2,1)S(1)}, bf16[448,384]{1,0:T(8,128)(2,1)S(1)}, u32[]{:S(2)}, u32[]{:S(2)}) collective-permute-start(bf16[448,384]{1,0:T(8,128)(2,1)S(1)} %collective-permute-done.1.rest_1_), channel_id=1, source_target_pairs={{0,4},{4,0},{8,12},{12,8},{16,20},{20,16},{24,28},{28,24},{1,5},{5... | collective-permute-start | bytes 1032200 | tf_op jit(solution)/shard_map/ppermute | solution.py:125
  53.0 0.0 collective-permute-done.2.rest_2_
  53.0 8.6 %collective-permute-start.6 = (bf16[448,384]{1,0:T(8,128)(2,1)S(1)}, bf16[448,384]{1,0:T(8,128)(2,1)S(1)}, u32[]{:S(2)}, u32[]{:S(2)}) collective-permute-start(bf16[448,384]{1,0:T(8,128)(2,1)S(1)} %collective-permute-done.2.rest_2_), channel_id=1, source_target_pairs={{0,4},{4,0},{8,12},{12,8},{16,20},{20,16},{24,28},{28,24},{1,5},{5... | collective-permute-start | bytes 1032200 | tf_op jit(solution)/shard_map/ppermute | solution.py:125
  61.5 0.0 collective-permute-done.3.rest_3_
  61.5 3.7 %collective-permute-start.7 = (bf16[448,384]{1,0:T(8,128)(2,1)S(1)}, bf16[448,384]{1,0:T(8,128)(2,1)S(1)}, u32[]{:S(2)}, u32[]{:S(2)}) collective-permute-start(bf16[448,384]{1,0:T(8,128)(2,1)S(1)} %collective-permute-done.3.rest_3_), channel_id=1, source_target_pairs={{0,4},{4,0},{8,12},{12,8},{16,20},{20,16},{24,28},{28,24},{1,5},{5... | collective-permute-start | bytes 1032200 | tf_op jit(solution)/shard_map/ppermute | solution.py:125
  65.2 0.0 collective-permute-done.11
  65.2 0.0 collective-permute-start.15
  65.3 0.0 collective-permute-done.4.rest_4_
  65.3 0.6 collective-permute-start.12
  65.9 0.6 collective-permute-done.7.rest_7_
  66.5 6.5 %shard_map.110 = (f32[384,512]{1,0:T(8,128)S(1)}, f32[8,512]{1,0:T(8,128)S(1)}, bf16[512,384]{1,0:T(8,128)(2,1)S(1)}) custom-call(s32[1,8]{1,0:T(1,128)S(1)} %copy-done.5, s32[1]{0:T(128)S(6)} %copy.12.counts, bf16[224,384]{1,0:T(8,128)(2,1)S(1)} %get-tuple-element.23.q_keep, bf16[240,384]{1,0:T(8,128)(2,1)S(1)} %collective-permute-done.q_got, ...), custom_call_target="tpu_custom_call" | custom-call | flops 1409286144 | bytes 2752512 | tf_op jit(solution)/shard_map/pallas_call | solution.py:393
  73.0 0.0 collective-permute-done.15.swapped
  73.0 1.8 %shard_map.112 = (f32[384,512]{1,0:T(8,128)S(1)}, f32[8,512]{1,0:T(8,128)S(1)}) custom-call(bf16[512,384]{1,0:T(8,128)(2,1)S(1)} %get-tuple-element.27.q_pad, bf16[512,384]{1,0:T(8,128)(2,1)S(1)} %broadcast_select_fusion.held, bf16[512,384]{1,0:T(8,128)(2,1)S(1)} %collective-permute-done.15.swapped, f32[384,512]{1,0:T(8,128)S(1)} %get-tuple-element.31.acc_in, ...), custom_call_target="tpu_custom_call" | custom-call | flops 402653184 | bytes 1572864 | tf_op jit(solution)/shard_map/pallas_call | solution.py:404
  74.9 2.1 %shard_map.113 = (bf16[224,384]{1,0:T(8,128)(2,1)S(1)}, bf16[224,384]{1,0:T(8,128)(2,1)S(1)}) custom-call(bf16[512,384]{1,0:T(8,128)(2,1)S(1)} %get-tuple-element.27.q_pad, bf16[512,384]{1,0:T(8,128)(2,1)S(1)} %broadcast_select_fusion.1.held, bf16[512,384]{1,0:T(8,128)(2,1)S(1)} %collective-permute-done.12.swapped, f32[384,512]{1,0:T(8,128)S(1)} %get-tuple-element.33.acc_in, ...), custom_call_target="tpu_custom_call" | custom-call | flops 402653184 | bytes 1572864 | tf_op jit(solution)/shard_map/pallas_call | solution.py:407
  77.0 0.3 collective-permute-start.16
  77.3 5.4 %collective-permute-done.16.got = bf16[224,384]{1,0:T(8,128)(2,1)S(1)} collective-permute-done((bf16[224,384]{1,0:T(8,128)(2,1)S(1)}, bf16[224,384]{1,0:T(8,128)(2,1)S(1)}, u32[]{:S(2)}, u32[]{:S(2)}) %collective-permute-start.16) | collective-permute-done | bytes 172064 | tf_op jit(solution)/shard_map/ppermute | solution.py:125
  82.6 3.9 %shard_map.114 = (bf16[224,768]{1,0:T(8,128)(2,1)S(1)}, bf16[224,768]{1,0:T(8,128)(2,1)S(1)}, bf16[224,768]{1,0:T(8,128)(2,1)S(1)}, f32[224,768]{1,0:T(8,128)S(1)}) custom-call(bf16[224,384]{1,0:T(8,128)(2,1)S(1)} %get-tuple-element.35.own, bf16[224,384]{1,0:T(8,128)(2,1)S(1)} %collective-permute-done.16.got, bf16[768,3072]{1,0:T(8,128)(2,1)} %weight.1), custom_call_target="tpu_custom_call" | custom-call | flops 1056964608 | bytes 4718592 | tf_op jit(solution)/shard_map/pallas_call | solution.py:417
  86.6 0.2 collective-permute-start.17
  86.7 2.4 %collective-permute-start.18 = (bf16[224,768]{1,0:T(8,128)(2,1)S(1)}, bf16[224,768]{1,0:T(8,128)(2,1)S(1)}, u32[]{:S(2)}, u32[]{:S(2)}) collective-permute-start(bf16[224,768]{1,0:T(8,128)(2,1)S(1)} %get-tuple-element.39), channel_id=1, source_target_pairs={{0,3},{1,2},{2,1},{3,0},{4,7},{5,6},{6,5},{7,4},{8,11},{9,10},{10,... | collective-permute-start | bytes 1032200 | tf_op jit(solution)/shard_map/ppermute | solution.py:125
  89.1 1.1 collective-permute-start.19
  90.2 18.1 %collective-permute-done.17 = bf16[224,768]{1,0:T(8,128)(2,1)S(1)} collective-permute-done((bf16[224,768]{1,0:T(8,128)(2,1)S(1)}, bf16[224,768]{1,0:T(8,128)(2,1)S(1)}, u32[]{:S(2)}, u32[]{:S(2)}) %collective-permute-start.17) | collective-permute-done | bytes 344096 | tf_op jit(solution)/shard_map/ppermute | solution.py:125
  108.3 11.4 %collective-permute-done.18 = bf16[224,768]{1,0:T(8,128)(2,1)S(1)} collective-permute-done((bf16[224,768]{1,0:T(8,128)(2,1)S(1)}, bf16[224,768]{1,0:T(8,128)(2,1)S(1)}, u32[]{:S(2)}, u32[]{:S(2)}) %collective-permute-start.18) | collective-permute-done | bytes 344096 | tf_op jit(solution)/shard_map/ppermute | solution.py:125
  119.7 0.9 add_convert_fusion
  (22 shorter events, 0.1 us)
Async XLA Ops:
  0.0 5.5 %collective-permute-start.8 = (bf16[1,1024,768]{2,1,0:T(8,128)(2,1)}, bf16[1,1024,768]{2,1,0:T(8,128)(2,1)S(1)}, u32[]{:S(2)}, u32[]{:S(2)}) collective-permute-start(bf16[1,1024,768]{2,1,0:T(8,128)(2,1)} %v.3), channel_id=1, source_target_pairs={{0,4},{8,12},{16,20},{24,28},{1,5},{9,13},{17,21},{25,29},{2,6},{1... | collective-permute-start | bytes 4718600 | tf_op jit(solution)/shard_map/ppermute | solution.py:354
  1.3 6.4 %collective-permute-start.9 = (bf16[1,1024,768]{2,1,0:T(8,128)(2,1)}, bf16[1,1024,768]{2,1,0:T(8,128)(2,1)S(1)}, u32[]{:S(2)}, u32[]{:S(2)}) collective-permute-start(bf16[1,1024,768]{2,1,0:T(8,128)(2,1)} %k.3), channel_id=1, source_target_pairs={{4,0},{12,8},{20,16},{28,24},{5,1},{13,9},{21,17},{29,25},{6,2},{1... | collective-permute-start | bytes 4718600 | tf_op jit(solution)/shard_map/ppermute | solution.py:355
  4.5 9.5 %copy-start.5 = (s32[1,8]{1,0:T(1,128)S(1)}, s32[1,8]{1,0:T(1,128)}, u32[]{:S(2)}) copy-start(s32[1,8]{1,0:T(1,128)} %lists.3) | copy-start | bytes 100
  5.5 2.2 %copy-start.6 = (bf16[1,1024,768]{2,1,0:T(8,128)(2,1)}, bf16[1,1024,768]{2,1,0:T(8,128)(2,1)S(1)}, u32[]{:S(2)}) copy-start(bf16[1,1024,768]{2,1,0:T(8,128)(2,1)S(1)} %collective-permute-done.8.from_even) | copy-start | bytes 4718596
  7.7 1.1 copy-start.7
  8.8 1.4 %copy-start = (bf16[1,1024,768]{2,1,0:T(8,128)(2,1)S(1)}, bf16[1,1024,768]{2,1,0:T(8,128)(2,1)}, u32[]{:S(2)}) copy-start(bf16[1,1024,768]{2,1,0:T(8,128)(2,1)} %k.3) | copy-start | bytes 4718596
  10.2 1.4 %copy-start.1 = (bf16[1,1024,768]{2,1,0:T(8,128)(2,1)S(1)}, bf16[1,1024,768]{2,1,0:T(8,128)(2,1)}, u32[]{:S(2)}) copy-start(bf16[1,1024,768]{2,1,0:T(8,128)(2,1)} %v.3) | copy-start | bytes 4718596
  11.6 2.4 %copy-start.2 = (bf16[224,768]{1,0:T(8,128)(2,1)S(1)}, bf16[224,768]{1,0:T(8,128)(2,1)}, u32[]{:S(2)}) copy-start(bf16[224,768]{1,0:T(8,128)(2,1)} %q.1) | copy-start | bytes 1032196
  11.6 2.4 %copy-start.3 = (bf16[224,768]{1,0:T(8,128)(2,1)S(1)}, bf16[224,768]{1,0:T(8,128)(2,1)}, u32[]{:S(2)}) copy-start(bf16[224,768]{1,0:T(8,128)(2,1)} %k.2) | copy-start | bytes 1032196
  11.6 2.4 %copy-start.4 = (bf16[224,768]{1,0:T(8,128)(2,1)S(1)}, bf16[224,768]{1,0:T(8,128)(2,1)}, u32[]{:S(2)}) copy-start(bf16[224,768]{1,0:T(8,128)(2,1)} %v.2) | copy-start | bytes 1032196
  11.8 9.0 %collective-permute-start.10 = (bf16[512,384]{1,0:T(8,128)(2,1)S(1)}, bf16[512,384]{1,0:T(8,128)(2,1)S(1)}, u32[]{:S(2)}, u32[]{:S(2)}) collective-permute-start(bf16[512,384]{1,0:T(8,128)(2,1)S(1)} %get-tuple-element.29), channel_id=1, source_target_pairs={{0,8},{4,12},{8,0},{12,4},{16,24},{20,28},{24,16},{28,20},{1,9},{5... | collective-permute-start | bytes 1179656 | tf_op jit(solution)/shard_map/ppermute | solution.py:125
  13.1 16.3 %collective-permute-start.13 = (bf16[512,384]{1,0:T(8,128)(2,1)S(1)}, bf16[512,384]{1,0:T(8,128)(2,1)}, u32[]{:S(2)}, u32[]{:S(2)}) collective-permute-start(bf16[512,384]{1,0:T(8,128)(2,1)S(1)} %get-tuple-element.30), channel_id=1, source_target_pairs={{0,8},{4,12},{8,0},{12,4},{16,24},{20,28},{24,16},{28,20},{1,9},{5... | collective-permute-start | bytes 1179656 | tf_op jit(solution)/shard_map/ppermute | solution.py:125
  14.7 21.9 %collective-permute-start.1 = (bf16[448,384]{1,0:T(8,128)(2,1)S(1)}, bf16[448,384]{1,0:T(8,128)(2,1)S(1)}, u32[]{:S(2)}, u32[]{:S(2)}) collective-permute-start(bf16[448,384]{1,0:T(8,128)(2,1)S(1)} %get-tuple-element.26), channel_id=1, source_target_pairs={{0,8},{4,12},{8,0},{12,4},{16,24},{20,28},{24,16},{28,20},{1,9},{5... | collective-permute-start | bytes 1032200 | tf_op jit(solution)/shard_map/ppermute | solution.py:125
  30.5 10.3 %collective-permute-start.14 = (bf16[512,384]{1,0:T(8,128)(2,1)S(1)}, bf16[512,384]{1,0:T(8,128)(2,1)}, u32[]{:S(2)}, u32[]{:S(2)}) collective-permute-start(bf16[512,384]{1,0:T(8,128)(2,1)S(1)} %get-tuple-element.41), channel_id=1, source_target_pairs={{0,16},{4,20},{8,24},{12,28},{16,0},{20,4},{24,8},{28,12},{1,17},{... | collective-permute-start | bytes 1179656 | tf_op jit(solution)/shard_map/ppermute | solution.py:125
  31.8 33.5 %collective-permute-start.11 = (bf16[512,384]{1,0:T(8,128)(2,1)S(1)}, bf16[512,384]{1,0:T(8,128)(2,1)S(1)}, u32[]{:S(2)}, u32[]{:S(2)}) collective-permute-start(bf16[512,384]{1,0:T(8,128)(2,1)S(1)} %get-tuple-element.42), channel_id=1, source_target_pairs={{0,16},{4,20},{8,24},{12,28},{16,0},{20,4},{24,8},{28,12},{1,17},{... | collective-permute-start | bytes 1179656 | tf_op jit(solution)/shard_map/ppermute | solution.py:125
  32.0 21.0 %collective-permute-start.2 = (bf16[448,384]{1,0:T(8,128)(2,1)S(1)}, bf16[448,384]{1,0:T(8,128)(2,1)S(1)}, u32[]{:S(2)}, u32[]{:S(2)}) collective-permute-start(bf16[448,384]{1,0:T(8,128)(2,1)S(1)} %get-tuple-element.25.rest_0_), channel_id=1, source_target_pairs={{0,16},{4,20},{8,24},{12,28},{16,0},{20,4},{24,8},{28,12},{1,17},{... | collective-permute-start | bytes 1032200 | tf_op jit(solution)/shard_map/ppermute | solution.py:125
  36.6 24.9 %collective-permute-start.3 = (bf16[448,384]{1,0:T(8,128)(2,1)S(1)}, bf16[448,384]{1,0:T(8,128)(2,1)S(1)}, u32[]{:S(2)}, u32[]{:S(2)}) collective-permute-start(bf16[448,384]{1,0:T(8,128)(2,1)S(1)} %collective-permute-done.1.rest_1_), channel_id=1, source_target_pairs={{0,16},{4,20},{8,24},{12,28},{16,0},{20,4},{24,8},{28,12},{1,17},{... | collective-permute-start | bytes 1032200 | tf_op jit(solution)/shard_map/ppermute | solution.py:125
  37.9 27.4 %collective-permute-start.4 = (bf16[448,384]{1,0:T(8,128)(2,1)S(1)}, bf16[448,384]{1,0:T(8,128)(2,1)S(1)}, u32[]{:S(2)}, u32[]{:S(2)}) collective-permute-start(bf16[448,384]{1,0:T(8,128)(2,1)S(1)} %get-tuple-element.25.rest_0_), channel_id=1, source_target_pairs={{0,4},{4,0},{8,12},{12,8},{16,20},{20,16},{24,28},{28,24},{1,5},{5... | collective-permute-start | bytes 1032200 | tf_op jit(solution)/shard_map/ppermute | solution.py:125
  40.7 4.8 %collective-permute-start = (bf16[240,384]{1,0:T(8,128)(2,1)S(1)}, bf16[240,384]{1,0:T(8,128)(2,1)S(1)}, u32[]{:S(2)}, u32[]{:S(2)}) collective-permute-start(bf16[240,384]{1,0:T(8,128)(2,1)S(1)} %get-tuple-element.24), channel_id=1, source_target_pairs={{0,8},{4,12},{8,0},{12,4},{16,24},{20,28},{24,16},{28,20},{1,9},{5... | collective-permute-start | bytes 552968 | tf_op jit(solution)/shard_map/ppermute | solution.py:125
  45.5 20.3 %collective-permute-start.5 = (bf16[448,384]{1,0:T(8,128)(2,1)S(1)}, bf16[448,384]{1,0:T(8,128)(2,1)S(1)}, u32[]{:S(2)}, u32[]{:S(2)}) collective-permute-start(bf16[448,384]{1,0:T(8,128)(2,1)S(1)} %collective-permute-done.1.rest_1_), channel_id=1, source_target_pairs={{0,4},{4,0},{8,12},{12,8},{16,20},{20,16},{24,28},{28,24},{1,5},{5... | collective-permute-start | bytes 1032200 | tf_op jit(solution)/shard_map/ppermute | solution.py:125
  53.0 12.9 %collective-permute-start.6 = (bf16[448,384]{1,0:T(8,128)(2,1)S(1)}, bf16[448,384]{1,0:T(8,128)(2,1)S(1)}, u32[]{:S(2)}, u32[]{:S(2)}) collective-permute-start(bf16[448,384]{1,0:T(8,128)(2,1)S(1)} %collective-permute-done.2.rest_2_), channel_id=1, source_target_pairs={{0,4},{4,0},{8,12},{12,8},{16,20},{20,16},{24,28},{28,24},{1,5},{5... | collective-permute-start | bytes 1032200 | tf_op jit(solution)/shard_map/ppermute | solution.py:125
  61.5 5.0 %collective-permute-start.7 = (bf16[448,384]{1,0:T(8,128)(2,1)S(1)}, bf16[448,384]{1,0:T(8,128)(2,1)S(1)}, u32[]{:S(2)}, u32[]{:S(2)}) collective-permute-start(bf16[448,384]{1,0:T(8,128)(2,1)S(1)} %collective-permute-done.3.rest_3_), channel_id=1, source_target_pairs={{0,4},{4,0},{8,12},{12,8},{16,20},{20,16},{24,28},{28,24},{1,5},{5... | collective-permute-start | bytes 1032200 | tf_op jit(solution)/shard_map/ppermute | solution.py:125
  65.2 7.8 %collective-permute-start.15 = (bf16[512,384]{1,0:T(8,128)(2,1)S(1)}, bf16[512,384]{1,0:T(8,128)(2,1)S(1)}, u32[]{:S(2)}, u32[]{:S(2)}) collective-permute-start(bf16[512,384]{1,0:T(8,128)(2,1)S(1)} %broadcast_select_fusion.held), channel_id=1, source_target_pairs={{0,4},{4,0},{8,12},{12,8},{16,20},{20,16},{24,28},{28,24},{1,5},{5... | collective-permute-start | bytes 1179656 | tf_op jit(solution)/shard_map/ppermute | solution.py:125
  65.3 9.6 %collective-permute-start.12 = (bf16[512,384]{1,0:T(8,128)(2,1)S(1)}, bf16[512,384]{1,0:T(8,128)(2,1)S(1)}, u32[]{:S(2)}, u32[]{:S(2)}) collective-permute-start(bf16[512,384]{1,0:T(8,128)(2,1)S(1)} %broadcast_select_fusion.1.held), channel_id=1, source_target_pairs={{0,4},{4,0},{8,12},{12,8},{16,20},{20,16},{24,28},{28,24},{1,5},{5... | collective-permute-start | bytes 1179656 | tf_op jit(solution)/shard_map/ppermute | solution.py:125
  77.0 5.6 %collective-permute-start.16 = (bf16[224,384]{1,0:T(8,128)(2,1)S(1)}, bf16[224,384]{1,0:T(8,128)(2,1)S(1)}, u32[]{:S(2)}, u32[]{:S(2)}) collective-permute-start(bf16[224,384]{1,0:T(8,128)(2,1)S(1)} %get-tuple-element.36), channel_id=1, source_target_pairs={{0,8},{4,12},{8,0},{12,4},{16,24},{20,28},{24,16},{28,20},{1,9},{5... | collective-permute-start | bytes 516104 | tf_op jit(solution)/shard_map/ppermute | solution.py:125
  82.6 37.1 %copy-start.8 = (bf16[224,768]{1,0:T(8,128)(2,1)S(1)}, bf16[224,768]{1,0:T(8,128)(2,1)}, u32[]{:S(2)}) copy-start(bf16[224,768]{1,0:T(8,128)(2,1)} %param.20) | copy-start | bytes 1032196
  82.6 37.1 %copy-start.9 = (f32[768]{0:T(1024)S(1)}, f32[768]{0:T(1024)}, u32[]{:S(2)}) copy-start(f32[768]{0:T(1024)} %param.21) | copy-start | bytes 9220
  86.6 21.7 %collective-permute-start.17 = (bf16[224,768]{1,0:T(8,128)(2,1)S(1)}, bf16[224,768]{1,0:T(8,128)(2,1)S(1)}, u32[]{:S(2)}, u32[]{:S(2)}) collective-permute-start(bf16[224,768]{1,0:T(8,128)(2,1)S(1)} %get-tuple-element.38), channel_id=1, source_target_pairs={{0,2},{1,3},{2,0},{3,1},{4,6},{5,7},{6,4},{7,5},{8,10},{9,11},{10,... | collective-permute-start | bytes 1032200 | tf_op jit(solution)/shard_map/ppermute | solution.py:125
  86.7 33.0 %collective-permute-start.18 = (bf16[224,768]{1,0:T(8,128)(2,1)S(1)}, bf16[224,768]{1,0:T(8,128)(2,1)S(1)}, u32[]{:S(2)}, u32[]{:S(2)}) collective-permute-start(bf16[224,768]{1,0:T(8,128)(2,1)S(1)} %get-tuple-element.39), channel_id=1, source_target_pairs={{0,3},{1,2},{2,1},{3,0},{4,7},{5,6},{6,5},{7,4},{8,11},{9,10},{10,... | collective-permute-start | bytes 1032200 | tf_op jit(solution)/shard_map/ppermute | solution.py:125
  89.1 30.6 %collective-permute-start.19 = (bf16[224,768]{1,0:T(8,128)(2,1)S(1)}, bf16[224,768]{1,0:T(8,128)(2,1)S(1)}, u32[]{:S(2)}, u32[]{:S(2)}) collective-permute-start(bf16[224,768]{1,0:T(8,128)(2,1)S(1)} %get-tuple-element.40), channel_id=1, source_target_pairs={{0,1},{1,0},{2,3},{3,2},{4,5},{5,4},{6,7},{7,6},{8,9},{9,8},{10,11... | collective-permute-start | bytes 1032200 | tf_op jit(solution)/shard_map/ppermute | solution.py:125

commit v2 on v0

--- a/solution.py
+++ b/solution.py
@@ -1,12 +1,17 @@
+import functools
 import math
 
 import jax
 import jax.numpy as jnp
 from jax import lax
+from jax.experimental import pallas as pl
+from jax.experimental.pallas import tpu as pltpu
 from jax.sharding import PartitionSpec as P
 
 HD = 128
 REACH = 4
+LOG2E = 1.4426950408889634
+VMEM_LIMIT = 24 * 1024 * 1024
 
 
 def broadcast(block, axis, source):
@@ -54,7 +59,7 @@
     )
 
 
-def per_device(
+def general_device(
     queries,
     key_rows,
     value_rows,
@@ -111,6 +116,394 @@
     return (residual.astype(jnp.float32) + gate_scale[None, :] * shares.T).astype(jnp.bfloat16)
 
 
+CORE, ROW, COLUMN = 1, 2, 4
+PAD = 256
+SLOTS = (0, 2, 4, 6, 1, 3, 5, 7)
+
+
+def swap(block, axis, bit, name):
+    with jax.named_scope(name):
+        return lax.ppermute(block, axis, [(i, i ^ bit) for i in range(lax.axis_size(axis))])
+
+
+def halves(width):
+    x = (lax.axis_index("frame") // ROW) % 2
+    mine = pl.multiple_of(x * width, HD)
+    other = pl.multiple_of((1 - x) * width, HD)
+    return mine, other
+
+
+def visible(frame, lists, counts):
+    seen = frame == lax.axis_index("frame")
+    for j in range(lists.shape[1]):
+        seen = seen | ((lists[0, j] == frame) & (j < counts[0]))
+    return seen
+
+
+def split_kernel(k, v, keep, send, sems):
+    rows, width = keep.shape[0], keep.shape[1] // 2
+    mine, other = halves(width)
+    left, right = pl.ds(0, width), pl.ds(width, width)
+    move(
+        sems,
+        (k.at[:, pl.ds(other, width)], send.at[:, left]),
+        (v.at[:, pl.ds(other, width)], send.at[:, right]),
+        (k.at[:, pl.ds(mine, width)], keep.at[:, left]),
+        (v.at[:, pl.ds(mine, width)], keep.at[:, right]),
+    )
+
+
+def query_kernel(lists, counts, q, after, keep, send, sems):
+    rows, width = keep.shape
+    mine, other = halves(width)
+    lane = lax.broadcasted_iota(jnp.int32, (16, width), 1)
+    flags = jnp.zeros((16, width), jnp.float32)
+    for g in range(lax.axis_size("frame")):
+        flag = jnp.where(visible(g, lists, counts), 1.0, 0.0)
+        flags = jnp.where(lane == g, flag, flags)
+    send[rows:, :] = flags.astype(jnp.bfloat16)
+    move(
+        sems,
+        (q.at[:, pl.ds(mine, width)], keep),
+        (q.at[:, pl.ds(other, width)], send.at[pl.ds(0, rows)]),
+    )
+
+
+def from_owner(owner, k, v, from_even, from_odd, take):
+    core = lax.axis_index("frame") % 2
+    owner_core = owner[0] % 2
+    for at, here, there in ((0, k, from_odd), (1, v, from_even)):
+        pl.when((core == at) & (owner_core == at))(functools.partial(take, here))
+        pl.when((core == at) & (owner_core != at))(functools.partial(take, there))
+
+
+def move(sems, *pairs):
+    copies = [pltpu.make_async_copy(src, dst, sems.at[i]) for i, (src, dst) in enumerate(pairs)]
+    for copy in copies:
+        copy.start()
+    for copy in copies:
+        copy.wait()
+
+
+def pick_kernel(owner, k, v, from_even, from_odd, send_a, send_b, keep, sems):
+    first, width = send_a.shape
+    second = send_b.shape[0]
+    mine, other = halves(width)
+
+    def take(src):
+        move(
+            sems,
+            (src.at[0, pl.ds(0, first), pl.ds(other, width)], send_a),
+            (src.at[0, pl.ds(first, second), pl.ds(other, width)], send_b),
+            (src.at[0, :, pl.ds(mine, width)], keep),
+        )
+
+    from_owner(owner, k, v, from_even, from_odd, take)
+
+
+def after_kernel(*refs):
+    pass
+
+
+def choose_kernel(bit, begin, owner, here, came, *rest):
+    out, sems = rest[-2:]
+    own = (owner[0] // bit) % 2 == (lax.axis_index("frame") // bit) % 2
+
+    @pl.when(own)
+    def _():
+        move(sems, (here.at[pl.ds(begin, out.shape[0])], out))
+
+    @pl.when(jnp.logical_not(own))
+    def _():
+        move(sems, (came, out))
+
+
+NT = (((1,), (1,)), ((), ()))
+TN = (((0,), (0,)), ((), ()))
+
+
+def absorb_chunk(query, keys, values, biases, state):
+    scale = LOG2E / math.sqrt(HD)
+    scores = [lax.dot_general(k, query, NT, preferred_element_type=jnp.float32) for k in keys]
+    top = None
+    for s, b in zip(scores, biases):
+        t = jnp.max(s, axis=0, keepdims=True) * scale
+        t = t if b is None else t + b
+        top = t if top is None else jnp.maximum(top, t)
+    if state is not None:
+        old_top, old_sum, old_acc = state
+        top = jnp.maximum(old_top, top)
+    total, acc = None, None
+    for s, b, v in zip(scores, biases, values):
+        shift = top if b is None else top - b
+        p = jnp.exp2(s * scale - shift)
+        part = jnp.sum(p, axis=0, keepdims=True)
+        total = part if total is None else total + part
+        o = lax.dot_general(v, p.astype(jnp.bfloat16), TN, preferred_element_type=jnp.float32)
+        acc = o if acc is None else acc + o
+    if state is not None:
+        factor = jnp.exp2(old_top - top)
+        total = total + old_sum * factor
+        acc = acc + old_acc * factor
+    return top, total, acc
+
+
+def frames_kernel(remote, lists, counts, q, *rest):
+    kv = rest[: len(SLOTS)]
+    acc_out, stat_out, padded = rest[len(SLOTS) :]
+    rows, width = kv[0].shape[0], kv[0].shape[1] // 2
+    heads = width // HD
+    here = lax.axis_index("frame")
+    padded[...] = jnp.zeros_like(padded)
+    padded[:rows, :] = q[:rows, :]
+    if remote:
+        flags = q[rows : rows + 16, :].astype(jnp.float32)
+        lane = lax.broadcasted_iota(jnp.int32, (16, width), 1)
+    biases = []
+    for bit in SLOTS:
+        frame = here ^ bit
+        if remote:
+            seen = jnp.max(jnp.where(lane == frame, flags, 0.0), keepdims=True)
+            bias = jnp.where(seen > 0.5, 0.0, -jnp.inf)
+        else:
+            bias = jnp.where(visible(frame, lists, counts), 0.0, -jnp.inf)
+        biases.append(jnp.broadcast_to(bias, (1, PAD)))
+    stat_out[...] = jnp.zeros_like(stat_out)
+    for h in range(heads):
+        keys = slice(h * HD, (h + 1) * HD)
+        values = slice(width + h * HD, width + (h + 1) * HD)
+        state = None
+        for s in range(0, len(SLOTS), 2):
+            pair = kv[s : s + 2]
+            state = absorb_chunk(
+                padded[:, keys],
+                [block[:, keys] for block in pair],
+                [block[:, values] for block in pair],
+                biases[s : s + 2],
+                state,
+            )
+        top, total, acc = state
+        stat_out[h : h + 1, :] = top
+        stat_out[heads + h : heads + h + 1, :] = total
+        acc_out[keys, :] = acc
+
+
+def style_kernel(last, rows, q, held, swapped, acc_in, stat_in, *rest):
+    outs, (keys, values, padded) = rest[:-3], rest[-3:]
+    chunk, width = keys.shape
+    heads = width // HD
+    core = lax.axis_index("frame") % 2
+    padded[...] = jnp.zeros_like(padded)
+    padded[:rows, :] = q[:rows, :]
+
+    @pl.when(core == 0)
+    def _():
+        keys[...] = held[...]
+        values[...] = swapped[...]
+
+    @pl.when(core == 1)
+    def _():
+        keys[...] = swapped[...]
+        values[...] = held[...]
+
+    if not last:
+        acc_out, stat_out = outs
+        stat_out[...] = jnp.zeros_like(stat_out)
+    for h in range(heads):
+        cols = slice(h * HD, (h + 1) * HD)
+        state = (stat_in[h : h + 1, :], stat_in[heads + h : heads + h + 1, :], acc_in[cols, :])
+        top, total, acc = absorb_chunk(
+            padded[:, cols], [keys[:, cols]], [values[:, cols]], [None], state
+        )
+        if last:
+            outs[0][:, cols] = (acc / total).T.astype(jnp.bfloat16)[:rows, :]
+        else:
+            stat_out[h : h + 1, :] = top
+            stat_out[heads + h : heads + h + 1, :] = total
+            acc_out[cols, :] = acc
+
+
+def project_kernel(bit, own, got, weight, *rest):
+    came, out = rest[:-1], rest[-1]
+    width, columns = own.shape[1], out.shape[1]
+    mine, other = halves(width)
+    start = pl.multiple_of((lax.axis_index("head") ^ bit) * columns, HD)
+    share = jnp.dot(
+        own[...],
+        weight[pl.ds(mine, width), pl.ds(start, columns)],
+        preferred_element_type=jnp.float32,
+    ) + jnp.dot(
+        got[...],
+        weight[pl.ds(other, width), pl.ds(start, columns)],
+        preferred_element_type=jnp.float32,
+    )
+    for block in came:
+        share = share + block[...].astype(jnp.float32)
+    out[...] = share.astype(out.dtype)
+
+
+SMEM = pl.BlockSpec(memory_space=pltpu.SMEM)
+VMEM = pl.BlockSpec(memory_space=pltpu.VMEM)
+ANY = pl.BlockSpec(memory_space=pl.ANY)
+
+
+def call(kernel, in_specs, outs, scratch=(), out_spec=VMEM, flops=0, moved=0, exps=0):
+    shapes = [jax.ShapeDtypeStruct(shape, dtype) for shape, dtype in outs]
+    return pl.pallas_call(
+        kernel,
+        out_shape=shapes,
+        in_specs=in_specs,
+        out_specs=[out_spec] * len(shapes),
+        scratch_shapes=list(scratch),
+        compiler_params=pltpu.CompilerParams(vmem_limit_bytes=VMEM_LIMIT),
+        cost_estimate=pl.CostEstimate(flops=1, bytes_accessed=1, transcendentals=0),
+    )
+
+
+def dma(count):
+    return pltpu.SemaphoreType.DMA((count,))
+
+
+def later(block, *after):
+    return pl.pallas_call(
+        after_kernel,
+        out_shape=jax.ShapeDtypeStruct(block.shape, block.dtype),
+        in_specs=[ANY] * (1 + len(after)),
+        out_specs=ANY,
+        input_output_aliases={0: 0},
+    )(block, *after)
+
+
+def paired_device(
+    queries,
+    key_rows,
+    value_rows,
+    ref_keys,
+    ref_values,
+    key_lists,
+    list_counts,
+    owner_index,
+    out_weight,
+    residual,
+    gate_scale,
+):
+    bf16, f32 = jnp.bfloat16, jnp.float32
+    rows, columns = queries.shape
+    width = columns // 2
+    heads = width // HD
+    style = ref_keys.shape[1]
+    frames = lax.axis_size("frame")
+
+    even = [(i, i ^ CORE) for i in range(0, frames, 2)]
+    odd = [(i ^ CORE, i) for i in range(0, frames, 2)]
+    with jax.named_scope("core_style"):
+        from_even = lax.ppermute(ref_values, "frame", even)
+        from_odd = lax.ppermute(ref_keys, "frame", odd)
+
+    kv = ((rows, 2 * width), bf16)
+    kv_keep, kv_send = call(
+        split_kernel, [ANY] * 2, [kv, kv], scratch=[dma(4)], moved=8 * rows * columns
+    )(key_rows, value_rows)
+    kv_x = swap(kv_send, "frame", ROW, "x_kv")
+    kv_y = swap(kv_keep, "frame", COLUMN, "y_kv")
+    kv_xy = swap(kv_x, "frame", COLUMN, "xy_kv")
+
+    second = style // 2
+    first = style - second
+    parts = [((first, width), bf16), ((second, width), bf16)]
+    send_a, send_b, keep = call(
+        pick_kernel,
+        [SMEM] + [ANY] * 4,
+        parts + [((style, width), bf16)],
+        scratch=[dma(3)],
+        moved=8 * style * width,
+    )(owner_index, ref_keys, ref_values, from_even, from_odd)
+    send_b = later(send_b, kv_x)
+
+    def choose(part, bit, begin, here, came, *after):
+        return call(
+            functools.partial(choose_kernel, bit, begin),
+            [SMEM] + [ANY] * (2 + len(after)),
+            [part],
+            scratch=[dma(1)],
+            moved=4 * part[0][0] * width,
+        )(owner_index, here, came, *after)[0]
+
+    x_came = [swap(sent, "frame", ROW, f"x_style_{j}") for j, sent in enumerate((send_a, send_b))]
+    q_keep, q_send = call(
+        query_kernel,
+        [SMEM, SMEM, ANY, ANY],
+        [((rows, width), bf16), ((rows + 16, width), bf16)],
+        scratch=[dma(2)],
+        moved=4 * rows * columns,
+    )(key_lists, list_counts, queries, x_came[0])
+    q_got = swap(q_send, "frame", ROW, "x_q")
+
+    near = [kv_keep, kv_x, kv_y, kv_xy]
+    near = near + [swap(block, "frame", CORE, f"c_kv_{n}") for n, block in enumerate(near)]
+    padded = pltpu.VMEM((PAD, width), bf16)
+    state = [((width, PAD), f32), ((8, PAD), f32)]
+
+    def frames_of(remote, q):
+        return call(
+            functools.partial(frames_kernel, remote),
+            [SMEM, SMEM] + [VMEM] * 9,
+            state,
+            scratch=[padded],
+            flops=4 * PAD * width * 8 * rows,
+            exps=PAD * heads * 8 * rows,
+            moved=16 * rows * width * 2,
+        )(key_lists, list_counts, q, *near)
+
+    chosen = [
+        choose(parts[j], ROW, j * first, keep, x_came[j], *after)
+        for j, after in enumerate(((kv_x, kv_y), (kv_xy,)))
+    ]
+    y_came = [swap(block, "frame", COLUMN, f"y_style_{j}") for j, block in enumerate(chosen)]
+
+    def finish(j, *after):
+        held = choose(parts[j], COLUMN, 0, chosen[j], y_came[j], *after)
+        return held, swap(held, "frame", CORE, f"c_style_{j}")
+
+    def style_of(last, j, q, blocks, held_state):
+        part = parts[j]
+        count = part[0][0]
+        return call(
+            functools.partial(style_kernel, last, rows),
+            [VMEM] * 5,
+            [((rows, width), bf16)] if last else state,
+            scratch=[pltpu.VMEM(*part), pltpu.VMEM(*part), padded],
+            flops=4 * PAD * width * count,
+            exps=PAD * heads * count,
+            moved=8 * count * width,
+        )(q, *blocks, *held_state)
+
+    own_state = frames_of(False, q_keep)
+    blocks = finish(0, chosen[1], q_got, own_state[1])
+    their_state = frames_of(True, q_got)
+    own_state = style_of(False, 0, q_keep, blocks, own_state)
+    their_state = style_of(False, 0, q_got, blocks, their_state)
+    blocks = finish(1, own_state[1], their_state[1])
+    (theirs,) = style_of(True, 1, q_got, blocks, their_state)
+    got = swap(theirs, "frame", ROW, "x_back")
+    (own,) = style_of(True, 1, q_keep, blocks, own_state)
+
+    def project(bit, dtype, *came):
+        return call(
+            functools.partial(project_kernel, bit),
+            [VMEM] * (3 + len(came)),
+            [((rows, columns), dtype)],
+            flops=2 * rows * columns * columns,
+            moved=2 * columns * columns,
+        )(own, got, out_weight, *came)[0]
+
+    relay = swap(project(3, bf16), "head", 1, "z_relay")
+    near_share = swap(project(1, bf16), "head", 1, "z_near")
+    far_share = swap(project(2, bf16, relay), "head", 2, "z_far")
+    projected = project(0, f32) + near_share.astype(f32) + far_share.astype(f32)
+    return (residual.astype(f32) + gate_scale[None, :] * projected).astype(bf16)
+
+
 def solution(mesh):
     placed = (
         P("frame", "head"),
@@ -125,6 +518,21 @@
         P("frame", "head"),
         P("head"),
     )
+
+    def per_device(*args):
+        rows, columns = args[0].shape
+        style = args[3].shape[1]
+        paired = (
+            mesh.shape["frame"] == 8
+            and mesh.shape["head"] == 4
+            and columns % (2 * HD) == 0
+            and columns // HD <= 8
+            and rows % 16 == 0
+            and rows <= PAD
+            and style % 256 == 0
+        )
+        return (paired_device if paired else general_device)(*args)
+
     return jax.shard_map(
         per_device, mesh=mesh, in_specs=placed, out_specs=P("frame", "head"), check_vma=False
     )

time: 254 us -> 92 us (0.36)
  waiting for transfers between devices: 161 us -> 37.6 us
  Pallas kernels: 0 us -> 19.8 us
  matrix products: 19.6 us -> 0 us
  between operations: 20.2 us -> 1.62 us
  local copies, waits for them, and re-layouts: 12.5 us -> 5.54 us
  starting transfers between devices: 32.7 us -> 26.2 us
  other arithmetic: 6.73 us -> 0.9 us
    psum x1 -> x0, waiting for transfers between devices: 80.5 us -> none  [broadcast(): return lax.psum(block, axis)]
    reduce_scatter x1 -> x0, waiting for transfers between devices: 62.7 us -> none  [per_device(): lax.psum_scatter(lax.dot_general(out_weight, attended, (((0,), (1,)), (()...]
    ppermute x16 -> x20, waiting for transfers between devices: 17.7 us -> 37.6 us  [the longest x18 37.6 us: swap(): lax.ppermute(block, axis, [(i, i ^ bit) for i in range(lax.axis_size(axis...]
    pallas_call x0 -> x18, Pallas kernels: none -> 19.8 us  [the longest x2 9.7 us: frames_of(): call(functools.partial(frames_kernel, remote), [SMEM, SMEM] + [VMEM] * 9,...]
    dot_general x13 -> x0, matrix products: 19.6 us -> none  [the longest x6 8.35 us: absorb(): jnp.einsum('hqk,khd->qhd', weights.astype(jnp.bfloat16), value_heads, pre...]
    ppermute x16 -> x20, starting transfers between devices: 32.6 us -> 26.2 us  [the longest x18 22.5 us: swap(): lax.ppermute(block, axis, [(i, i ^ bit) for i in range(lax.axis_size(axis...]
    another operation x2 -> x0, local copies, waits for them, and re-layouts: 4.2 us -> none  [the longest x1 2.59 us: absorb(): key_heads = key_block.reshape(key_block.shape[0], head_count, HD)]
    unnamed x45 -> x22, local copies, waits for them, and re-layouts: 8.14 us -> 5.54 us
  transfers between devices with their start and end apart: 18 -> 20, of which waited for: 6 -> 10; matrix products, arithmetic and copies ran while one was open for 6% -> 0% of each run, Pallas kernels for 0% -> 19%
where the time goes in v2:
time: 92 us; the launch traced here: 91.7 us
  waiting for transfers between devices  37.6 us (41%)
  starting transfers between devices  26.2 us (28%)
  Pallas kernels  19.8 us (22%)
  local copies, waits for them, and re-layouts  5.54 us (6%)
  between operations  1.62 us (2%)
    ppermute x18, waiting for transfers between devices, swap(): lax.ppermute(block, axis, [(i, i ^ bit) for i in range(lax.axis_size(axis...  37.6 us
    ppermute x18, starting transfers between devices, swap(): lax.ppermute(block, axis, [(i, i ^ bit) for i in range(lax.axis_size(axis...  22.5 us
    pallas_call x2, Pallas kernels, frames_of(): call(functools.partial(frames_kernel, remote), [SMEM, SMEM] + [VMEM] * 9,...  9.7 us
    pallas_call x4, Pallas kernels, style_of(): call(functools.partial(style_kernel, last, rows), [VMEM] * 5, [((rows, wi...  6.23 us
    unnamed x22, local copies, waits for them, and re-layouts  5.54 us
    ppermute x1, starting transfers between devices, paired_device(): from_even = lax.ppermute(ref_values, 'frame', even)  2.45 us
    pallas_call x4, Pallas kernels, project(): call(functools.partial(project_kernel, bit), [VMEM] * (3 + len(came)), [(...  2.06 us
  transfers between devices with their start and end apart: 20, of which 10 were waited for; matrix products, arithmetic and copies ran while one was open for 0% of the time, Pallas kernels for 19%

profile of v2, /device:TPU:0, one launch (start us, length us, event | category | flops | bytes accessed | tf_op | source)
XLA Modules:
  0.0 91.7 jit_solution(12069923731963316175)
XLA Ops:
  0.0 2.4 %collective-permute-start = (bf16[1,1024,768]{2,1,0:T(8,128)(2,1)}, bf16[1,1024,768]{2,1,0:T(8,128)(2,1)S(1)}, u32[]{:S(2)}, u32[]{:S(2)}) collective-permute-start(bf16[1,1024,768]{2,1,0:T(8,128)(2,1)} %v.2), channel_id=1, source_target_pairs={{0,4},{8,12},{16,20},{24,28},{1,5},{9,13},{17,21},{25,29},{2,6},{1... | collective-permute-start | bytes 4718600 | tf_op jit(solution)/shard_map/core_style/ppermute | solution.py:400
  2.5 1.3 %collective-permute-start.1 = (bf16[1,1024,768]{2,1,0:T(8,128)(2,1)}, bf16[1,1024,768]{2,1,0:T(8,128)(2,1)S(1)}, u32[]{:S(2)}, u32[]{:S(2)}) collective-permute-start(bf16[1,1024,768]{2,1,0:T(8,128)(2,1)} %k.2), channel_id=1, source_target_pairs={{4,0},{12,8},{20,16},{28,24},{5,1},{13,9},{21,17},{29,25},{6,2},{1... | collective-permute-start | bytes 4718600 | tf_op jit(solution)/shard_map/core_style/ppermute | solution.py:401
  3.8 1.0 %copy-done.3 = bf16[224,768]{1,0:T(8,128)(2,1)S(1)} copy-done((bf16[224,768]{1,0:T(8,128)(2,1)S(1)}, bf16[224,768]{1,0:T(8,128)(2,1)}, u32[]{:S(2)}) %copy-start.3) | copy-done | bytes 344088
  4.7 1.0 %copy-done.4 = bf16[224,768]{1,0:T(8,128)(2,1)S(1)} copy-done((bf16[224,768]{1,0:T(8,128)(2,1)S(1)}, bf16[224,768]{1,0:T(8,128)(2,1)}, u32[]{:S(2)}) %copy-start.4) | copy-done | bytes 344088
  5.8 2.4 %collective-permute-start.3 = (bf16[224,768]{1,0:T(8,128)(2,1)S(1)}, bf16[224,768]{1,0:T(8,128)(2,1)}, u32[]{:S(2)}, u32[]{:S(2)}) collective-permute-start(bf16[224,768]{1,0:T(8,128)(2,1)S(1)} %get-tuple-element.24), channel_id=1, source_target_pairs={{0,8},{4,12},{8,0},{12,4},{16,24},{20,28},{24,16},{28,20},{1,9},{5... | collective-permute-start | bytes 1032200 | tf_op jit(solution)/shard_map/x_kv/ppermute | solution.py:126
  8.9 1.4 %copy-done = bf16[1,1024,768]{2,1,0:T(8,128)(2,1)S(1)} copy-done((bf16[1,1024,768]{2,1,0:T(8,128)(2,1)S(1)}, bf16[1,1024,768]{2,1,0:T(8,128)(2,1)}, u32[]{:S(2)}) %copy-start) | copy-done | bytes 1572888
  10.3 1.4 %copy-done.1 = bf16[1,1024,768]{2,1,0:T(8,128)(2,1)S(1)} copy-done((bf16[1,1024,768]{2,1,0:T(8,128)(2,1)S(1)}, bf16[1,1024,768]{2,1,0:T(8,128)(2,1)}, u32[]{:S(2)}) %copy-start.1) | copy-done | bytes 1572888
  11.7 0.2 shard_map.109
  11.9 0.7 copy-done.2
  12.7 1.4 %collective-permute-start.2 = (bf16[512,384]{1,0:T(8,128)(2,1)S(1)}, bf16[512,384]{1,0:T(8,128)(2,1)S(1)}, u32[]{:S(2)}, u32[]{:S(2)}) collective-permute-start(bf16[512,384]{1,0:T(8,128)(2,1)S(1)} %get-tuple-element.20), channel_id=1, source_target_pairs={{0,8},{4,12},{8,0},{12,4},{16,24},{20,28},{24,16},{28,20},{1,9},{5... | collective-permute-start | bytes 1179656 | tf_op jit(solution)/shard_map/x_style_0/ppermute | solution.py:126
  14.1 1.5 %collective-permute-start.7 = (bf16[224,768]{1,0:T(8,128)(2,1)S(1)}, bf16[224,768]{1,0:T(8,128)(2,1)S(1)}, u32[]{:S(2)}, u32[]{:S(2)}) collective-permute-start(bf16[224,768]{1,0:T(8,128)(2,1)S(1)} %get-tuple-element.25.rest_0_), channel_id=1, source_target_pairs={{0,16},{4,20},{8,24},{12,28},{16,0},{20,4},{24,8},{28,12},{1,17},{... | collective-permute-start | bytes 1032200 | tf_op jit(solution)/shard_map/y_kv/ppermute | solution.py:126
  15.6 1.2 %collective-permute-done.3.refs_1_.rest_0_.rest_1_ = bf16[224,768]{1,0:T(8,128)(2,1)} collective-permute-done((bf16[224,768]{1,0:T(8,128)(2,1)S(1)}, bf16[224,768]{1,0:T(8,128)(2,1)}, u32[]{:S(2)}, u32[]{:S(2)}) %collective-permute-start.3) | collective-permute-done | bytes 344096 | tf_op jit(solution)/shard_map/x_kv/ppermute | solution.py:126
  16.8 2.3 %collective-permute-start.5 = (bf16[224,768]{1,0:T(8,128)(2,1)}, bf16[224,768]{1,0:T(8,128)(2,1)S(1)}, u32[]{:S(2)}, u32[]{:S(2)}) collective-permute-start(bf16[224,768]{1,0:T(8,128)(2,1)} %collective-permute-done.3.refs_1_.rest_0_.rest_1_), channel_id=1, source_target_pairs={{0,16},{4,20},{8,24},{12,28},{16,0},{20,4},{24,8},{28,12},{1,17},{... | collective-permute-start | bytes 1032200 | tf_op jit(solution)/shard_map/xy_kv/ppermute | solution.py:126
  19.0 1.5 %collective-permute-start.4 = (bf16[512,384]{1,0:T(8,128)(2,1)}, bf16[512,384]{1,0:T(8,128)(2,1)S(1)}, u32[]{:S(2)}, u32[]{:S(2)}) collective-permute-start(bf16[512,384]{1,0:T(8,128)(2,1)} %shard_map.112), channel_id=1, source_target_pairs={{0,8},{4,12},{8,0},{12,4},{16,24},{20,28},{24,16},{28,20},{1,9},{5... | collective-permute-start | bytes 1179656 | tf_op jit(solution)/shard_map/x_style_1/ppermute | solution.py:126
  20.5 4.5 %collective-permute-done.7.rest_1_.rest_2_ = bf16[224,768]{1,0:T(8,128)(2,1)S(1)} collective-permute-done((bf16[224,768]{1,0:T(8,128)(2,1)S(1)}, bf16[224,768]{1,0:T(8,128)(2,1)S(1)}, u32[]{:S(2)}, u32[]{:S(2)}) %collective-permute-start.7) | collective-permute-done | bytes 344096 | tf_op jit(solution)/shard_map/y_kv/ppermute | solution.py:126
  25.1 0.2 shard_map.114.here
  25.3 2.3 %collective-permute-start.8 = (bf16[512,384]{1,0:T(8,128)(2,1)S(1)}, bf16[512,384]{1,0:T(8,128)(2,1)S(1)}, u32[]{:S(2)}, u32[]{:S(2)}) collective-permute-start(bf16[512,384]{1,0:T(8,128)(2,1)S(1)} %shard_map.114.here), channel_id=1, source_target_pairs={{0,16},{4,20},{8,24},{12,28},{16,0},{20,4},{24,8},{28,12},{1,17},{... | collective-permute-start | bytes 1179656 | tf_op jit(solution)/shard_map/y_style_0/ppermute | solution.py:126
  27.6 0.3 collective-permute-start.11
  28.0 0.2 collective-permute-start.12
  28.1 4.3 %collective-permute-done.5.rest_0_.rest_3_ = bf16[224,768]{1,0:T(8,128)(2,1)S(1)} collective-permute-done((bf16[224,768]{1,0:T(8,128)(2,1)}, bf16[224,768]{1,0:T(8,128)(2,1)S(1)}, u32[]{:S(2)}, u32[]{:S(2)}) %collective-permute-start.5) | collective-permute-done | bytes 344096 | tf_op jit(solution)/shard_map/xy_kv/ppermute | solution.py:126
  33.1 0.7 shard_map.110
  33.8 2.0 %collective-permute-start.9 = (bf16[240,384]{1,0:T(8,128)(2,1)S(1)}, bf16[240,384]{1,0:T(8,128)(2,1)S(1)}, u32[]{:S(2)}, u32[]{:S(2)}) collective-permute-start(bf16[240,384]{1,0:T(8,128)(2,1)S(1)} %get-tuple-element.26), channel_id=1, source_target_pairs={{0,8},{4,12},{8,0},{12,4},{16,24},{20,28},{24,16},{28,20},{1,9},{5... | collective-permute-start | bytes 552968 | tf_op jit(solution)/shard_map/x_q/ppermute | solution.py:126
  35.8 0.2 shard_map.113.rest_0_.here
  36.0 4.9 %shard_map.115 = (f32[384,256]{1,0:T(8,128)S(1)}, f32[8,256]{1,0:T(8,128)S(1)}) custom-call(s32[1,8]{1,0:T(1,128)S(1)} %copy-done.6, s32[1]{0:T(128)S(6)} %copy.14.counts, bf16[224,384]{1,0:T(8,128)(2,1)S(1)} %get-tuple-element.21.q, bf16[224,768]{1,0:T(8,128)(2,1)S(1)} %get-tuple-element.25.rest_0_, ...), custom_call_target="tpu_custom_call" | custom-call | flops 1 | bytes 1 | tf_op jit(solution)/shard_map/pallas_call | solution.py:448
  41.0 0.2 shard_map.116.held
  41.2 0.1 collective-permute-start.14
  41.4 1.7 %collective-permute-start.6 = (bf16[512,384]{1,0:T(8,128)(2,1)S(1)}, bf16[512,384]{1,0:T(8,128)(2,1)S(1)}, u32[]{:S(2)}, u32[]{:S(2)}) collective-permute-start(bf16[512,384]{1,0:T(8,128)(2,1)S(1)} %shard_map.113.rest_0_.here), channel_id=1, source_target_pairs={{0,16},{4,20},{8,24},{12,28},{16,0},{20,4},{24,8},{28,12},{1,17},{... | collective-permute-start | bytes 1179656 | tf_op jit(solution)/shard_map/y_style_1/ppermute | solution.py:126
  43.1 4.8 %shard_map.118 = (f32[384,256]{1,0:T(8,128)S(1)}, f32[8,256]{1,0:T(8,128)S(1)}) custom-call(s32[1,8]{1,0:T(1,128)S(1)} %copy-done.6, s32[1]{0:T(128)S(6)} %copy.14.counts, bf16[240,384]{1,0:T(8,128)(2,1)S(1)} %collective-permute-done.9.rest_1_.q, bf16[224,768]{1,0:T(8,128)(2,1)S(1)} %get-tuple-element.25.rest_0_, ...), custom_call_target="tpu_custom_call" | custom-call | flops 1 | bytes 1 | tf_op jit(solution)/shard_map/pallas_call | solution.py:448
  47.9 1.5 %shard_map.117 = (f32[384,256]{1,0:T(8,128)S(1)}, f32[8,256]{1,0:T(8,128)S(1)}) custom-call(bf16[224,384]{1,0:T(8,128)(2,1)S(1)} %get-tuple-element.21.q, bf16[512,384]{1,0:T(8,128)(2,1)S(1)} %shard_map.116.held, bf16[512,384]{1,0:T(8,128)(2,1)S(1)} %collective-permute-done.14.swapped, f32[384,256]{1,0:T(8,128)S(1)} %get-tuple-element.28.acc_in, ...), custom_call_target="tpu_custom_call" | custom-call | flops 1 | bytes 1 | tf_op jit(solution)/shard_map/pallas_call | solution.py:471
  49.3 1.5 %shard_map.119 = (f32[384,256]{1,0:T(8,128)S(1)}, f32[8,256]{1,0:T(8,128)S(1)}) custom-call(bf16[240,384]{1,0:T(8,128)(2,1)S(1)} %collective-permute-done.9.rest_1_.q, bf16[512,384]{1,0:T(8,128)(2,1)S(1)} %shard_map.116.held, bf16[512,384]{1,0:T(8,128)(2,1)S(1)} %collective-permute-done.14.swapped, f32[384,256]{1,0:T(8,128)S(1)} %get-tuple-element.30.acc_in, ...), custom_call_target="tpu_custom_call" | custom-call | flops 1 | bytes 1 | tf_op jit(solution)/shard_map/pallas_call | solution.py:471
  50.8 2.0 %collective-permute-done.6.came = bf16[512,384]{1,0:T(8,128)(2,1)S(1)} collective-permute-done((bf16[512,384]{1,0:T(8,128)(2,1)S(1)}, bf16[512,384]{1,0:T(8,128)(2,1)S(1)}, u32[]{:S(2)}, u32[]{:S(2)}) %collective-permute-start.6) | collective-permute-done | bytes 393248 | tf_op jit(solution)/shard_map/y_style_1/ppermute | solution.py:126
  52.8 0.2 shard_map.120.held
  53.1 1.7 %collective-permute-done.15.swapped = bf16[512,384]{1,0:T(8,128)(2,1)S(1)} collective-permute-done((bf16[512,384]{1,0:T(8,128)(2,1)S(1)}, bf16[512,384]{1,0:T(8,128)(2,1)S(1)}, u32[]{:S(2)}, u32[]{:S(2)}) %collective-permute-start.15) | collective-permute-done | bytes 393248 | tf_op jit(solution)/shard_map/c_style_1/ppermute | solution.py:126
  54.8 1.7 %shard_map.122 = bf16[224,384]{1,0:T(8,128)(2,1)S(1)} custom-call(bf16[240,384]{1,0:T(8,128)(2,1)S(1)} %collective-permute-done.9.rest_1_.q, bf16[512,384]{1,0:T(8,128)(2,1)S(1)} %shard_map.120.held, bf16[512,384]{1,0:T(8,128)(2,1)S(1)} %collective-permute-done.15.swapped, f32[384,256]{1,0:T(8,128)S(1)} %get-tuple-element.34.acc_in, ...), custom_call_target="tpu_custom_call" | custom-call | flops 1 | bytes 1 | tf_op jit(solution)/shard_map/pallas_call | solution.py:471
  56.6 1.7 %collective-permute-start.16 = (bf16[224,384]{1,0:T(8,128)(2,1)S(1)}, bf16[224,384]{1,0:T(8,128)(2,1)S(1)}, u32[]{:S(2)}, u32[]{:S(2)}) collective-permute-start(bf16[224,384]{1,0:T(8,128)(2,1)S(1)} %shard_map.122), channel_id=1, source_target_pairs={{0,8},{4,12},{8,0},{12,4},{16,24},{20,28},{24,16},{28,20},{1,9},{5... | collective-permute-start | bytes 516104 | tf_op jit(solution)/shard_map/x_back/ppermute | solution.py:126
  58.3 1.5 %shard_map.121.own = bf16[224,384]{1,0:T(8,128)(2,1)S(1)} custom-call(bf16[224,384]{1,0:T(8,128)(2,1)S(1)} %get-tuple-element.21.q, bf16[512,384]{1,0:T(8,128)(2,1)S(1)} %shard_map.120.held, bf16[512,384]{1,0:T(8,128)(2,1)S(1)} %collective-permute-done.15.swapped, f32[384,256]{1,0:T(8,128)S(1)} %get-tuple-element.33.acc_in, ...), custom_call_target="tpu_custom_call" | custom-call | flops 1 | bytes 1 | tf_op jit(solution)/shard_map/pallas_call | solution.py:471
  59.8 3.2 %collective-permute-done.16.got = bf16[224,384]{1,0:T(8,128)(2,1)S(1)} collective-permute-done((bf16[224,384]{1,0:T(8,128)(2,1)S(1)}, bf16[224,384]{1,0:T(8,128)(2,1)S(1)}, u32[]{:S(2)}, u32[]{:S(2)}) %collective-permute-start.16) | collective-permute-done | bytes 172064 | tf_op jit(solution)/shard_map/x_back/ppermute | solution.py:126
  63.0 0.5 shard_map.125
  63.6 1.8 %collective-permute-start.18 = (bf16[224,768]{1,0:T(8,128)(2,1)S(1)}, bf16[224,768]{1,0:T(8,128)(2,1)S(1)}, u32[]{:S(2)}, u32[]{:S(2)}) collective-permute-start(bf16[224,768]{1,0:T(8,128)(2,1)S(1)} %shard_map.125), channel_id=1, source_target_pairs={{0,1},{1,0},{2,3},{3,2},{4,5},{5,4},{6,7},{7,6},{8,9},{9,8},{10,11... | collective-permute-start | bytes 1032200 | tf_op jit(solution)/shard_map/z_relay/ppermute | solution.py:126
  65.4 0.5 shard_map.124
  65.9 0.3 collective-permute-start.17
  66.2 8.4 %collective-permute-done.18.rest_0_ = bf16[224,768]{1,0:T(8,128)(2,1)S(1)} collective-permute-done((bf16[224,768]{1,0:T(8,128)(2,1)S(1)}, bf16[224,768]{1,0:T(8,128)(2,1)S(1)}, u32[]{:S(2)}, u32[]{:S(2)}) %collective-permute-start.18) | collective-permute-done | bytes 344096 | tf_op jit(solution)/shard_map/z_relay/ppermute | solution.py:126
  74.6 0.5 shard_map.126
  75.2 2.8 %collective-permute-start.19 = (bf16[224,768]{1,0:T(8,128)(2,1)S(1)}, bf16[224,768]{1,0:T(8,128)(2,1)S(1)}, u32[]{:S(2)}, u32[]{:S(2)}) collective-permute-start(bf16[224,768]{1,0:T(8,128)(2,1)S(1)} %shard_map.126), channel_id=1, source_target_pairs={{0,2},{1,3},{2,0},{3,1},{4,6},{5,7},{6,4},{7,5},{8,10},{9,11},{10,... | collective-permute-start | bytes 1032200 | tf_op jit(solution)/shard_map/z_far/ppermute | solution.py:126
  78.0 0.5 shard_map.123
  78.5 8.3 %collective-permute-done.17 = bf16[224,768]{1,0:T(8,128)(2,1)S(1)} collective-permute-done((bf16[224,768]{1,0:T(8,128)(2,1)S(1)}, bf16[224,768]{1,0:T(8,128)(2,1)S(1)}, u32[]{:S(2)}, u32[]{:S(2)}) %collective-permute-start.17) | collective-permute-done | bytes 344096 | tf_op jit(solution)/shard_map/z_near/ppermute | solution.py:126
  86.9 3.9 %collective-permute-done.19 = bf16[224,768]{1,0:T(8,128)(2,1)S(1)} collective-permute-done((bf16[224,768]{1,0:T(8,128)(2,1)S(1)}, bf16[224,768]{1,0:T(8,128)(2,1)S(1)}, u32[]{:S(2)}, u32[]{:S(2)}) %collective-permute-start.19) | collective-permute-done | bytes 344096 | tf_op jit(solution)/shard_map/z_far/ppermute | solution.py:126
  90.8 0.9 add_convert_fusion
  (34 shorter events, 0.3 us)
Async XLA Ops:
  0.0 8.9 %collective-permute-start = (bf16[1,1024,768]{2,1,0:T(8,128)(2,1)}, bf16[1,1024,768]{2,1,0:T(8,128)(2,1)S(1)}, u32[]{:S(2)}, u32[]{:S(2)}) collective-permute-start(bf16[1,1024,768]{2,1,0:T(8,128)(2,1)} %v.2), channel_id=1, source_target_pairs={{0,4},{8,12},{16,20},{24,28},{1,5},{9,13},{17,21},{25,29},{2,6},{1... | collective-permute-start | bytes 4718600 | tf_op jit(solution)/shard_map/core_style/ppermute | solution.py:400
  2.5 6.4 %collective-permute-start.1 = (bf16[1,1024,768]{2,1,0:T(8,128)(2,1)}, bf16[1,1024,768]{2,1,0:T(8,128)(2,1)S(1)}, u32[]{:S(2)}, u32[]{:S(2)}) collective-permute-start(bf16[1,1024,768]{2,1,0:T(8,128)(2,1)} %k.2), channel_id=1, source_target_pairs={{4,0},{12,8},{20,16},{28,24},{5,1},{13,9},{21,17},{29,25},{6,2},{1... | collective-permute-start | bytes 4718600 | tf_op jit(solution)/shard_map/core_style/ppermute | solution.py:401
  3.8 1.0 %copy-start.3 = (bf16[224,768]{1,0:T(8,128)(2,1)S(1)}, bf16[224,768]{1,0:T(8,128)(2,1)}, u32[]{:S(2)}) copy-start(bf16[224,768]{1,0:T(8,128)(2,1)} %k.3) | copy-start | bytes 1032196
  4.7 1.0 %copy-start.4 = (bf16[224,768]{1,0:T(8,128)(2,1)S(1)}, bf16[224,768]{1,0:T(8,128)(2,1)}, u32[]{:S(2)}) copy-start(bf16[224,768]{1,0:T(8,128)(2,1)} %v.3) | copy-start | bytes 1032196
  5.8 10.9 %collective-permute-start.3 = (bf16[224,768]{1,0:T(8,128)(2,1)S(1)}, bf16[224,768]{1,0:T(8,128)(2,1)}, u32[]{:S(2)}, u32[]{:S(2)}) collective-permute-start(bf16[224,768]{1,0:T(8,128)(2,1)S(1)} %get-tuple-element.24), channel_id=1, source_target_pairs={{0,8},{4,12},{8,0},{12,4},{16,24},{20,28},{24,16},{28,20},{1,9},{5... | collective-permute-start | bytes 1032200 | tf_op jit(solution)/shard_map/x_kv/ppermute | solution.py:126
  8.9 1.4 %copy-start = (bf16[1,1024,768]{2,1,0:T(8,128)(2,1)S(1)}, bf16[1,1024,768]{2,1,0:T(8,128)(2,1)}, u32[]{:S(2)}) copy-start(bf16[1,1024,768]{2,1,0:T(8,128)(2,1)} %k.2) | copy-start | bytes 4718596
  10.3 1.4 %copy-start.1 = (bf16[1,1024,768]{2,1,0:T(8,128)(2,1)S(1)}, bf16[1,1024,768]{2,1,0:T(8,128)(2,1)}, u32[]{:S(2)}) copy-start(bf16[1,1024,768]{2,1,0:T(8,128)(2,1)} %v.2) | copy-start | bytes 4718596
  11.9 0.8 copy-start.2
  12.7 12.4 %collective-permute-start.2 = (bf16[512,384]{1,0:T(8,128)(2,1)S(1)}, bf16[512,384]{1,0:T(8,128)(2,1)S(1)}, u32[]{:S(2)}, u32[]{:S(2)}) collective-permute-start(bf16[512,384]{1,0:T(8,128)(2,1)S(1)} %get-tuple-element.20), channel_id=1, source_target_pairs={{0,8},{4,12},{8,0},{12,4},{16,24},{20,28},{24,16},{28,20},{1,9},{5... | collective-permute-start | bytes 1179656 | tf_op jit(solution)/shard_map/x_style_0/ppermute | solution.py:126
  14.1 11.0 %collective-permute-start.7 = (bf16[224,768]{1,0:T(8,128)(2,1)S(1)}, bf16[224,768]{1,0:T(8,128)(2,1)S(1)}, u32[]{:S(2)}, u32[]{:S(2)}) collective-permute-start(bf16[224,768]{1,0:T(8,128)(2,1)S(1)} %get-tuple-element.25.rest_0_), channel_id=1, source_target_pairs={{0,16},{4,20},{8,24},{12,28},{16,0},{20,4},{24,8},{28,12},{1,17},{... | collective-permute-start | bytes 1032200 | tf_op jit(solution)/shard_map/y_kv/ppermute | solution.py:126
  15.6 12.4 %collective-permute-start.10 = (bf16[224,768]{1,0:T(8,128)(2,1)S(1)}, bf16[224,768]{1,0:T(8,128)(2,1)S(1)}, u32[]{:S(2)}, u32[]{:S(2)}) collective-permute-start(bf16[224,768]{1,0:T(8,128)(2,1)S(1)} %get-tuple-element.25.rest_0_), channel_id=1, source_target_pairs={{0,4},{4,0},{8,12},{12,8},{16,20},{20,16},{24,28},{28,24},{1,5},{5... | collective-permute-start | bytes 1032200 | tf_op jit(solution)/shard_map/c_kv_0/ppermute | solution.py:126
  16.8 15.6 %collective-permute-start.5 = (bf16[224,768]{1,0:T(8,128)(2,1)}, bf16[224,768]{1,0:T(8,128)(2,1)S(1)}, u32[]{:S(2)}, u32[]{:S(2)}) collective-permute-start(bf16[224,768]{1,0:T(8,128)(2,1)} %collective-permute-done.3.refs_1_.rest_0_.rest_1_), channel_id=1, source_target_pairs={{0,16},{4,20},{8,24},{12,28},{16,0},{20,4},{24,8},{28,12},{1,17},{... | collective-permute-start | bytes 1032200 | tf_op jit(solution)/shard_map/xy_kv/ppermute | solution.py:126
  19.0 14.0 %copy-start.5 = (bf16[224,768]{1,0:T(8,128)(2,1)S(1)}, bf16[224,768]{1,0:T(8,128)(2,1)}, u32[]{:S(2)}) copy-start(bf16[224,768]{1,0:T(8,128)(2,1)} %q.1) | copy-start | bytes 1032196
  19.0 14.0 %copy-start.6 = (s32[1,8]{1,0:T(1,128)S(1)}, s32[1,8]{1,0:T(1,128)}, u32[]{:S(2)}) copy-start(s32[1,8]{1,0:T(1,128)} %lists.5) | copy-start | bytes 100
  19.0 14.8 %collective-permute-start.4 = (bf16[512,384]{1,0:T(8,128)(2,1)}, bf16[512,384]{1,0:T(8,128)(2,1)S(1)}, u32[]{:S(2)}, u32[]{:S(2)}) collective-permute-start(bf16[512,384]{1,0:T(8,128)(2,1)} %shard_map.112), channel_id=1, source_target_pairs={{0,8},{4,12},{8,0},{12,4},{16,24},{20,28},{24,16},{28,20},{1,9},{5... | collective-permute-start | bytes 1179656 | tf_op jit(solution)/shard_map/x_style_1/ppermute | solution.py:126
  25.3 15.7 %collective-permute-start.8 = (bf16[512,384]{1,0:T(8,128)(2,1)S(1)}, bf16[512,384]{1,0:T(8,128)(2,1)S(1)}, u32[]{:S(2)}, u32[]{:S(2)}) collective-permute-start(bf16[512,384]{1,0:T(8,128)(2,1)S(1)} %shard_map.114.here), channel_id=1, source_target_pairs={{0,16},{4,20},{8,24},{12,28},{16,0},{20,4},{24,8},{28,12},{1,17},{... | collective-permute-start | bytes 1179656 | tf_op jit(solution)/shard_map/y_style_0/ppermute | solution.py:126
  27.6 8.3 %collective-permute-start.11 = (bf16[224,768]{1,0:T(8,128)(2,1)}, bf16[224,768]{1,0:T(8,128)(2,1)S(1)}, u32[]{:S(2)}, u32[]{:S(2)}) collective-permute-start(bf16[224,768]{1,0:T(8,128)(2,1)} %collective-permute-done.3.refs_1_.rest_0_.rest_1_), channel_id=1, source_target_pairs={{0,4},{4,0},{8,12},{12,8},{16,20},{20,16},{24,28},{28,24},{1,5},{5... | collective-permute-start | bytes 1032200 | tf_op jit(solution)/shard_map/c_kv_1/ppermute | solution.py:126
  28.0 8.0 %collective-permute-start.12 = (bf16[224,768]{1,0:T(8,128)(2,1)S(1)}, bf16[224,768]{1,0:T(8,128)(2,1)S(1)}, u32[]{:S(2)}, u32[]{:S(2)}) collective-permute-start(bf16[224,768]{1,0:T(8,128)(2,1)S(1)} %collective-permute-done.7.rest_1_.rest_2_), channel_id=1, source_target_pairs={{0,4},{4,0},{8,12},{12,8},{16,20},{20,16},{24,28},{28,24},{1,5},{5... | collective-permute-start | bytes 1032200 | tf_op jit(solution)/shard_map/c_kv_2/ppermute | solution.py:126
  32.4 3.6 %collective-permute-start.13 = (bf16[224,768]{1,0:T(8,128)(2,1)S(1)}, bf16[224,768]{1,0:T(8,128)(2,1)S(1)}, u32[]{:S(2)}, u32[]{:S(2)}) collective-permute-start(bf16[224,768]{1,0:T(8,128)(2,1)S(1)} %collective-permute-done.5.rest_0_.rest_3_), channel_id=1, source_target_pairs={{0,4},{4,0},{8,12},{12,8},{16,20},{20,16},{24,28},{28,24},{1,5},{5... | collective-permute-start | bytes 1032200 | tf_op jit(solution)/shard_map/c_kv_3/ppermute | solution.py:126
  33.8 7.1 %collective-permute-start.9 = (bf16[240,384]{1,0:T(8,128)(2,1)S(1)}, bf16[240,384]{1,0:T(8,128)(2,1)S(1)}, u32[]{:S(2)}, u32[]{:S(2)}) collective-permute-start(bf16[240,384]{1,0:T(8,128)(2,1)S(1)} %get-tuple-element.26), channel_id=1, source_target_pairs={{0,8},{4,12},{8,0},{12,4},{16,24},{20,28},{24,16},{28,20},{1,9},{5... | collective-permute-start | bytes 552968 | tf_op jit(solution)/shard_map/x_q/ppermute | solution.py:126
  36.0 27.0 %slice-start = ((s8[4718592]{0:T(1024)(128)(4,1)}), s8[4194304]{0:T(1024)(128)(4,1)S(1)}, s32[]{:S(2)}) async-start(s8[4718592]{0:T(1024)(128)(4,1)} %bitcast), calls=%async_computation | async-start | bytes 8388608
  41.2 21.8 %slice-start.1 = ((s8[4718592]{0:T(1024)(128)(4,1)}), s8[524288]{0:T(1024)(128)(4,1)S(1)}, s32[]{:S(2)}) async-start(s8[4718592]{0:T(1024)(128)(4,1)} %bitcast), calls=%async_computation.1 | async-start | bytes 1048576
  41.2 6.6 %collective-permute-start.14 = (bf16[512,384]{1,0:T(8,128)(2,1)S(1)}, bf16[512,384]{1,0:T(8,128)(2,1)S(1)}, u32[]{:S(2)}, u32[]{:S(2)}) collective-permute-start(bf16[512,384]{1,0:T(8,128)(2,1)S(1)} %shard_map.116.held), channel_id=1, source_target_pairs={{0,4},{4,0},{8,12},{12,8},{16,20},{20,16},{24,28},{28,24},{1,5},{5... | collective-permute-start | bytes 1179656 | tf_op jit(solution)/shard_map/c_style_0/ppermute | solution.py:126
  41.4 11.5 %collective-permute-start.6 = (bf16[512,384]{1,0:T(8,128)(2,1)S(1)}, bf16[512,384]{1,0:T(8,128)(2,1)S(1)}, u32[]{:S(2)}, u32[]{:S(2)}) collective-permute-start(bf16[512,384]{1,0:T(8,128)(2,1)S(1)} %shard_map.113.rest_0_.here), channel_id=1, source_target_pairs={{0,16},{4,20},{8,24},{12,28},{16,0},{20,4},{24,8},{28,12},{1,17},{... | collective-permute-start | bytes 1179656 | tf_op jit(solution)/shard_map/y_style_1/ppermute | solution.py:126
  53.0 1.8 %collective-permute-start.15 = (bf16[512,384]{1,0:T(8,128)(2,1)S(1)}, bf16[512,384]{1,0:T(8,128)(2,1)S(1)}, u32[]{:S(2)}, u32[]{:S(2)}) collective-permute-start(bf16[512,384]{1,0:T(8,128)(2,1)S(1)} %shard_map.120.held), channel_id=1, source_target_pairs={{0,4},{4,0},{8,12},{12,8},{16,20},{20,16},{24,28},{28,24},{1,5},{5... | collective-permute-start | bytes 1179656 | tf_op jit(solution)/shard_map/c_style_1/ppermute | solution.py:126
  56.6 6.5 %collective-permute-start.16 = (bf16[224,384]{1,0:T(8,128)(2,1)S(1)}, bf16[224,384]{1,0:T(8,128)(2,1)S(1)}, u32[]{:S(2)}, u32[]{:S(2)}) collective-permute-start(bf16[224,384]{1,0:T(8,128)(2,1)S(1)} %shard_map.122), channel_id=1, source_target_pairs={{0,8},{4,12},{8,0},{12,4},{16,24},{20,28},{24,16},{28,20},{1,9},{5... | collective-permute-start | bytes 516104 | tf_op jit(solution)/shard_map/x_back/ppermute | solution.py:126
  63.6 11.1 %collective-permute-start.18 = (bf16[224,768]{1,0:T(8,128)(2,1)S(1)}, bf16[224,768]{1,0:T(8,128)(2,1)S(1)}, u32[]{:S(2)}, u32[]{:S(2)}) collective-permute-start(bf16[224,768]{1,0:T(8,128)(2,1)S(1)} %shard_map.125), channel_id=1, source_target_pairs={{0,1},{1,0},{2,3},{3,2},{4,5},{5,4},{6,7},{7,6},{8,9},{9,8},{10,11... | collective-permute-start | bytes 1032200 | tf_op jit(solution)/shard_map/z_relay/ppermute | solution.py:126
  65.9 20.9 %collective-permute-start.17 = (bf16[224,768]{1,0:T(8,128)(2,1)S(1)}, bf16[224,768]{1,0:T(8,128)(2,1)S(1)}, u32[]{:S(2)}, u32[]{:S(2)}) collective-permute-start(bf16[224,768]{1,0:T(8,128)(2,1)S(1)} %shard_map.124), channel_id=1, source_target_pairs={{0,1},{1,0},{2,3},{3,2},{4,5},{5,4},{6,7},{7,6},{8,9},{9,8},{10,11... | collective-permute-start | bytes 1032200 | tf_op jit(solution)/shard_map/z_near/ppermute | solution.py:126
  75.2 15.6 %copy-start.7 = (bf16[224,768]{1,0:T(8,128)(2,1)S(1)}, bf16[224,768]{1,0:T(8,128)(2,1)}, u32[]{:S(2)}) copy-start(bf16[224,768]{1,0:T(8,128)(2,1)} %param.20) | copy-start | bytes 1032196
  75.2 15.6 %copy-start.8 = (f32[768]{0:T(1024)S(1)}, f32[768]{0:T(1024)}, u32[]{:S(2)}) copy-start(f32[768]{0:T(1024)} %param.21) | copy-start | bytes 9220
  75.2 15.6 %collective-permute-start.19 = (bf16[224,768]{1,0:T(8,128)(2,1)S(1)}, bf16[224,768]{1,0:T(8,128)(2,1)S(1)}, u32[]{:S(2)}, u32[]{:S(2)}) collective-permute-start(bf16[224,768]{1,0:T(8,128)(2,1)S(1)} %shard_map.126), channel_id=1, source_target_pairs={{0,2},{1,3},{2,0},{3,1},{4,6},{5,7},{6,4},{7,5},{8,10},{9,11},{10,... | collective-permute-start | bytes 1032200 | tf_op jit(solution)/shard_map/z_far/ppermute | solution.py:126

commit v3 on v2

--- a/solution.py
+++ b/solution.py
@@ -117,7 +117,6 @@
 
 
 CORE, ROW, COLUMN = 1, 2, 4
-PAD = 256
 SLOTS = (0, 2, 4, 6, 1, 3, 5, 7)
 
 
@@ -201,8 +200,9 @@
     from_owner(owner, k, v, from_even, from_odd, take)
 
 
-def after_kernel(*refs):
-    pass
+def hold_kernel(block, *rest):
+    out, sems = rest[-2:]
+    move(sems, (block, out))
 
 
 def choose_kernel(bit, begin, owner, here, came, *rest):
@@ -219,27 +219,24 @@
 
 
 NT = (((1,), (1,)), ((), ()))
-TN = (((0,), (0,)), ((), ()))
 
 
 def absorb_chunk(query, keys, values, biases, state):
     scale = LOG2E / math.sqrt(HD)
-    scores = [lax.dot_general(k, query, NT, preferred_element_type=jnp.float32) for k in keys]
+    scores = [lax.dot_general(query, k, NT, preferred_element_type=jnp.float32) for k in keys]
     top = None
     for s, b in zip(scores, biases):
-        t = jnp.max(s, axis=0, keepdims=True) * scale
-        t = t if b is None else t + b
+        t = jnp.max(s, axis=1, keepdims=True) * scale + b
         top = t if top is None else jnp.maximum(top, t)
     if state is not None:
         old_top, old_sum, old_acc = state
         top = jnp.maximum(old_top, top)
     total, acc = None, None
     for s, b, v in zip(scores, biases, values):
-        shift = top if b is None else top - b
-        p = jnp.exp2(s * scale - shift)
-        part = jnp.sum(p, axis=0, keepdims=True)
+        p = jnp.exp2(s * scale - (top - b))
+        part = jnp.sum(p, axis=1, keepdims=True)
         total = part if total is None else total + part
-        o = lax.dot_general(v, p.astype(jnp.bfloat16), TN, preferred_element_type=jnp.float32)
+        o = jnp.dot(p.astype(jnp.bfloat16), v, preferred_element_type=jnp.float32)
         acc = o if acc is None else acc + o
     if state is not None:
         factor = jnp.exp2(old_top - top)
@@ -248,14 +245,18 @@
     return top, total, acc
 
 
+def store_state(acc_out, stat_out, h, state):
+    heads = acc_out.shape[1] // HD
+    stat_out[:, h : h + 1] = state[0]
+    stat_out[:, heads + h : heads + h + 1] = state[1]
+    acc_out[:, h * HD : (h + 1) * HD] = state[2]
+
+
 def frames_kernel(remote, lists, counts, q, *rest):
     kv = rest[: len(SLOTS)]
-    acc_out, stat_out, padded = rest[len(SLOTS) :]
+    acc_out, stat_out = rest[len(SLOTS) :]
     rows, width = kv[0].shape[0], kv[0].shape[1] // 2
-    heads = width // HD
     here = lax.axis_index("frame")
-    padded[...] = jnp.zeros_like(padded)
-    padded[:rows, :] = q[:rows, :]
     if remote:
         flags = q[rows : rows + 16, :].astype(jnp.float32)
         lane = lax.broadcasted_iota(jnp.int32, (16, width), 1)
@@ -264,63 +265,45 @@
         frame = here ^ bit
         if remote:
             seen = jnp.max(jnp.where(lane == frame, flags, 0.0), keepdims=True)
-            bias = jnp.where(seen > 0.5, 0.0, -jnp.inf)
+            biases.append(jnp.where(seen > 0.5, 0.0, -jnp.inf))
         else:
-            bias = jnp.where(visible(frame, lists, counts), 0.0, -jnp.inf)
-        biases.append(jnp.broadcast_to(bias, (1, PAD)))
-    stat_out[...] = jnp.zeros_like(stat_out)
-    for h in range(heads):
+            biases.append(jnp.where(visible(frame, lists, counts), 0.0, -jnp.inf))
+    group = 4
+    for h in range(width // HD):
         keys = slice(h * HD, (h + 1) * HD)
         values = slice(width + h * HD, width + (h + 1) * HD)
         state = None
-        for s in range(0, len(SLOTS), 2):
-            pair = kv[s : s + 2]
+        for s in range(0, len(SLOTS), group):
+            blocks = kv[s : s + group]
             state = absorb_chunk(
-                padded[:, keys],
-                [block[:, keys] for block in pair],
-                [block[:, values] for block in pair],
-                biases[s : s + 2],
+                q[:rows, keys],
+                [block[:, keys] for block in blocks],
+                [block[:, values] for block in blocks],
+                biases[s : s + group],
                 state,
             )
-        top, total, acc = state
-        stat_out[h : h + 1, :] = top
-        stat_out[heads + h : heads + h + 1, :] = total
-        acc_out[keys, :] = acc
-
-
-def style_kernel(last, rows, q, held, swapped, acc_in, stat_in, *rest):
-    outs, (keys, values, padded) = rest[:-3], rest[-3:]
-    chunk, width = keys.shape
+        store_state(acc_out, stat_out, h, state)
+
+
+def style_kernel(last, q, held, swapped, acc_in, stat_in, *outs):
+    rows, width = acc_in.shape
     heads = width // HD
     core = lax.axis_index("frame") % 2
-    padded[...] = jnp.zeros_like(padded)
-    padded[:rows, :] = q[:rows, :]
-
-    @pl.when(core == 0)
-    def _():
-        keys[...] = held[...]
-        values[...] = swapped[...]
-
-    @pl.when(core == 1)
-    def _():
-        keys[...] = swapped[...]
-        values[...] = held[...]
-
-    if not last:
-        acc_out, stat_out = outs
-        stat_out[...] = jnp.zeros_like(stat_out)
-    for h in range(heads):
-        cols = slice(h * HD, (h + 1) * HD)
-        state = (stat_in[h : h + 1, :], stat_in[heads + h : heads + h + 1, :], acc_in[cols, :])
-        top, total, acc = absorb_chunk(
-            padded[:, cols], [keys[:, cols]], [values[:, cols]], [None], state
-        )
-        if last:
-            outs[0][:, cols] = (acc / total).T.astype(jnp.bfloat16)[:rows, :]
-        else:
-            stat_out[h : h + 1, :] = top
-            stat_out[heads + h : heads + h + 1, :] = total
-            acc_out[cols, :] = acc
+
+    def run(keys, values):
+        for h in range(heads):
+            cols = slice(h * HD, (h + 1) * HD)
+            state = (stat_in[:, h : h + 1], stat_in[:, heads + h : heads + h + 1], acc_in[:, cols])
+            state = absorb_chunk(
+                q[:rows, cols], [keys[:, cols]], [values[:, cols]], [0.0], state
+            )
+            if last:
+                outs[0][:, cols] = (state[2] / state[1]).astype(jnp.bfloat16)
+            else:
+                store_state(*outs, h, state)
+
+    pl.when(core == 0)(functools.partial(run, held, swapped))
+    pl.when(core == 1)(functools.partial(run, swapped, held))
 
 
 def project_kernel(bit, own, got, weight, *rest):
@@ -347,7 +330,7 @@
 ANY = pl.BlockSpec(memory_space=pl.ANY)
 
 
-def call(kernel, in_specs, outs, scratch=(), out_spec=VMEM, flops=0, moved=0, exps=0):
+def call(kernel, in_specs, outs, scratch=(), out_spec=VMEM):
     shapes = [jax.ShapeDtypeStruct(shape, dtype) for shape, dtype in outs]
     return pl.pallas_call(
         kernel,
@@ -365,13 +348,9 @@
 
 
 def later(block, *after):
-    return pl.pallas_call(
-        after_kernel,
-        out_shape=jax.ShapeDtypeStruct(block.shape, block.dtype),
-        in_specs=[ANY] * (1 + len(after)),
-        out_specs=ANY,
-        input_output_aliases={0: 0},
-    )(block, *after)
+    return call(
+        hold_kernel, [ANY] * (1 + len(after)), [(block.shape, block.dtype)], scratch=[dma(1)]
+    )(block, *after)[0]
 
 
 def paired_device(
@@ -402,7 +381,7 @@
 
     kv = ((rows, 2 * width), bf16)
     kv_keep, kv_send = call(
-        split_kernel, [ANY] * 2, [kv, kv], scratch=[dma(4)], moved=8 * rows * columns
+        split_kernel, [ANY] * 2, [kv, kv], scratch=[dma(4)]
     )(key_rows, value_rows)
     kv_x = swap(kv_send, "frame", ROW, "x_kv")
     kv_y = swap(kv_keep, "frame", COLUMN, "y_kv")
@@ -416,7 +395,6 @@
         [SMEM] + [ANY] * 4,
         parts + [((style, width), bf16)],
         scratch=[dma(3)],
-        moved=8 * style * width,
     )(owner_index, ref_keys, ref_values, from_even, from_odd)
     send_b = later(send_b, kv_x)
 
@@ -426,7 +404,6 @@
             [SMEM] + [ANY] * (2 + len(after)),
             [part],
             scratch=[dma(1)],
-            moved=4 * part[0][0] * width,
         )(owner_index, here, came, *after)[0]
 
     x_came = [swap(sent, "frame", ROW, f"x_style_{j}") for j, sent in enumerate((send_a, send_b))]
@@ -435,24 +412,18 @@
         [SMEM, SMEM, ANY, ANY],
         [((rows, width), bf16), ((rows + 16, width), bf16)],
         scratch=[dma(2)],
-        moved=4 * rows * columns,
-    )(key_lists, list_counts, queries, x_came[0])
+    )(key_lists, list_counts, queries, kv_x)
     q_got = swap(q_send, "frame", ROW, "x_q")
 
     near = [kv_keep, kv_x, kv_y, kv_xy]
     near = near + [swap(block, "frame", CORE, f"c_kv_{n}") for n, block in enumerate(near)]
-    padded = pltpu.VMEM((PAD, width), bf16)
-    state = [((width, PAD), f32), ((8, PAD), f32)]
+    state = [((rows, width), f32), ((rows, HD), f32)]
 
     def frames_of(remote, q):
         return call(
             functools.partial(frames_kernel, remote),
             [SMEM, SMEM] + [VMEM] * 9,
             state,
-            scratch=[padded],
-            flops=4 * PAD * width * 8 * rows,
-            exps=PAD * heads * 8 * rows,
-            moved=16 * rows * width * 2,
         )(key_lists, list_counts, q, *near)
 
     chosen = [
@@ -466,24 +437,19 @@
         return held, swap(held, "frame", CORE, f"c_style_{j}")
 
     def style_of(last, j, q, blocks, held_state):
-        part = parts[j]
-        count = part[0][0]
         return call(
-            functools.partial(style_kernel, last, rows),
+            functools.partial(style_kernel, last),
             [VMEM] * 5,
             [((rows, width), bf16)] if last else state,
-            scratch=[pltpu.VMEM(*part), pltpu.VMEM(*part), padded],
-            flops=4 * PAD * width * count,
-            exps=PAD * heads * count,
-            moved=8 * count * width,
         )(q, *blocks, *held_state)
 
     own_state = frames_of(False, q_keep)
-    blocks = finish(0, chosen[1], q_got, own_state[1])
     their_state = frames_of(True, q_got)
+    seen = own_state[1], their_state[1]
+    blocks = finish(0, chosen[1], q_got)
     own_state = style_of(False, 0, q_keep, blocks, own_state)
     their_state = style_of(False, 0, q_got, blocks, their_state)
-    blocks = finish(1, own_state[1], their_state[1])
+    blocks = finish(1, *seen)
     (theirs,) = style_of(True, 1, q_got, blocks, their_state)
     got = swap(theirs, "frame", ROW, "x_back")
     (own,) = style_of(True, 1, q_keep, blocks, own_state)
@@ -493,8 +459,6 @@
             functools.partial(project_kernel, bit),
             [VMEM] * (3 + len(came)),
             [((rows, columns), dtype)],
-            flops=2 * rows * columns * columns,
-            moved=2 * columns * columns,
         )(own, got, out_weight, *came)[0]
 
     relay = swap(project(3, bf16), "head", 1, "z_relay")
@@ -526,9 +490,8 @@
             mesh.shape["frame"] == 8
             and mesh.shape["head"] == 4
             and columns % (2 * HD) == 0
-            and columns // HD <= 8
+            and columns // HD <= HD
             and rows % 16 == 0
-            and rows <= PAD
             and style % 256 == 0
         )
         return (paired_device if paired else general_device)(*args)

time: 92 us -> 86.6 us (0.941)
  Pallas kernels: 19.8 us -> 16.2 us
  starting transfers between devices: 26.2 us -> 24.4 us
    pallas_call x2, Pallas kernels: 9.7 us -> 6.08 us  [frames_of(): call(functools.partial(frames_kernel, remote), [SMEM, SMEM] + [VMEM] * 9,...]
    ppermute x18, starting transfers between devices: 22.5 us -> 20.6 us  [swap(): lax.ppermute(block, axis, [(i, i ^ bit) for i in range(lax.axis_size(axis...]
    ppermute x18, waiting for transfers between devices: 37.6 us -> 38.5 us  [swap(): lax.ppermute(block, axis, [(i, i ^ bit) for i in range(lax.axis_size(axis...]
    unnamed x22 -> x20, local copies, waits for them, and re-layouts: 5.54 us -> 4.79 us
  transfers between devices with their start and end apart: 20 -> 20, of which waited for: 10 -> 13; matrix products, arithmetic and copies ran while one was open for 0% -> 0% of each run, Pallas kernels for 19% -> 16%
where the time goes in v3:
time: 86.6 us; the launch traced here: 86.3 us
  waiting for transfers between devices  38.5 us (44%)
  starting transfers between devices  24.4 us (28%)
  Pallas kernels  16.2 us (19%)
  local copies, waits for them, and re-layouts  4.79 us (6%)
  between operations  1.59 us (2%)
  other arithmetic  0.9 us (1%)
    ppermute x18, waiting for transfers between devices, swap(): lax.ppermute(block, axis, [(i, i ^ bit) for i in range(lax.axis_size(axis...  38.5 us
    ppermute x18, starting transfers between devices, swap(): lax.ppermute(block, axis, [(i, i ^ bit) for i in range(lax.axis_size(axis...  20.6 us
    pallas_call x2, Pallas kernels, frames_of(): call(functools.partial(frames_kernel, remote), [SMEM, SMEM] + [VMEM] * 9,...  6.08 us
    pallas_call x4, Pallas kernels, style_of(): call(functools.partial(style_kernel, last), [VMEM] * 5, [((rows, width),...  6.03 us
    unnamed x20, local copies, waits for them, and re-layouts  4.79 us
    ppermute x1, starting transfers between devices, paired_device(): from_even = lax.ppermute(ref_values, 'frame', even)  2.45 us
    pallas_call x4, Pallas kernels, project(): call(functools.partial(project_kernel, bit), [VMEM] * (3 + len(came)), [(...  2.05 us
  transfers between devices with their start and end apart: 20, of which 13 were waited for; matrix products, arithmetic and copies ran while one was open for 0% of the time, Pallas kernels for 16%

profile of v3, /device:TPU:0, one launch (start us, length us, event | category | flops | bytes accessed | tf_op | source)
XLA Modules:
  0.0 86.3 jit_solution(11255786558102548188)
XLA Ops:
  0.0 2.4 %collective-permute-start.1 = (bf16[1,1024,768]{2,1,0:T(8,128)(2,1)}, bf16[1,1024,768]{2,1,0:T(8,128)(2,1)S(1)}, u32[]{:S(2)}, u32[]{:S(2)}) collective-permute-start(bf16[1,1024,768]{2,1,0:T(8,128)(2,1)} %v.3), channel_id=1, source_target_pairs={{0,4},{8,12},{16,20},{24,28},{1,5},{9,13},{17,21},{25,29},{2,6},{1... | collective-permute-start | bytes 4718600 | tf_op jit(solution)/shard_map/core_style/ppermute | solution.py:379
  2.5 1.3 %collective-permute-start.2 = (bf16[1,1024,768]{2,1,0:T(8,128)(2,1)}, bf16[1,1024,768]{2,1,0:T(8,128)(2,1)S(1)}, u32[]{:S(2)}, u32[]{:S(2)}) collective-permute-start(bf16[1,1024,768]{2,1,0:T(8,128)(2,1)} %k.3), channel_id=1, source_target_pairs={{4,0},{12,8},{20,16},{28,24},{5,1},{13,9},{21,17},{29,25},{6,2},{1... | collective-permute-start | bytes 4718600 | tf_op jit(solution)/shard_map/core_style/ppermute | solution.py:380
  3.8 1.0 %copy-done.2 = bf16[224,768]{1,0:T(8,128)(2,1)S(1)} copy-done((bf16[224,768]{1,0:T(8,128)(2,1)S(1)}, bf16[224,768]{1,0:T(8,128)(2,1)}, u32[]{:S(2)}) %copy-start.2) | copy-done | bytes 344088
  4.7 1.0 %copy-done.3 = bf16[224,768]{1,0:T(8,128)(2,1)S(1)} copy-done((bf16[224,768]{1,0:T(8,128)(2,1)S(1)}, bf16[224,768]{1,0:T(8,128)(2,1)}, u32[]{:S(2)}) %copy-start.3) | copy-done | bytes 344088
  5.8 2.4 %collective-permute-start = (bf16[224,768]{1,0:T(8,128)(2,1)S(1)}, bf16[224,768]{1,0:T(8,128)(2,1)S(1)}, u32[]{:S(2)}, u32[]{:S(2)}) collective-permute-start(bf16[224,768]{1,0:T(8,128)(2,1)S(1)} %get-tuple-element.20), channel_id=1, source_target_pairs={{0,8},{4,12},{8,0},{12,4},{16,24},{20,28},{24,16},{28,20},{1,9},{5... | collective-permute-start | bytes 1032200 | tf_op jit(solution)/shard_map/x_kv/ppermute | solution.py:125
  8.2 1.5 %collective-permute-start.6 = (bf16[224,768]{1,0:T(8,128)(2,1)S(1)}, bf16[224,768]{1,0:T(8,128)(2,1)S(1)}, u32[]{:S(2)}, u32[]{:S(2)}) collective-permute-start(bf16[224,768]{1,0:T(8,128)(2,1)S(1)} %get-tuple-element.24.rest_0_), channel_id=1, source_target_pairs={{0,16},{4,20},{8,24},{12,28},{16,0},{20,4},{24,8},{28,12},{1,17},{... | collective-permute-start | bytes 1032200 | tf_op jit(solution)/shard_map/y_kv/ppermute | solution.py:125
  10.4 1.4 %copy-done = bf16[1,1024,768]{2,1,0:T(8,128)(2,1)S(1)} copy-done((bf16[1,1024,768]{2,1,0:T(8,128)(2,1)S(1)}, bf16[1,1024,768]{2,1,0:T(8,128)(2,1)}, u32[]{:S(2)}) %copy-start) | copy-done | bytes 1572888
  11.8 1.4 %copy-done.1 = bf16[1,1024,768]{2,1,0:T(8,128)(2,1)S(1)} copy-done((bf16[1,1024,768]{2,1,0:T(8,128)(2,1)S(1)}, bf16[1,1024,768]{2,1,0:T(8,128)(2,1)}, u32[]{:S(2)}) %copy-start.1) | copy-done | bytes 1572888
  13.3 0.2 shard_map.111
  13.5 0.6 collective-permute-start.13
  14.1 2.6 %collective-permute-done.after.rest_0_.rest_1_ = bf16[224,768]{1,0:T(8,128)(2,1)S(1)} collective-permute-done((bf16[224,768]{1,0:T(8,128)(2,1)S(1)}, bf16[224,768]{1,0:T(8,128)(2,1)S(1)}, u32[]{:S(2)}, u32[]{:S(2)}) %collective-permute-start) | collective-permute-done | bytes 344096 | tf_op jit(solution)/shard_map/x_kv/ppermute | solution.py:125
  16.9 2.3 %collective-permute-start.3 = (bf16[512,384]{1,0:T(8,128)(2,1)S(1)}, bf16[512,384]{1,0:T(8,128)(2,1)S(1)}, u32[]{:S(2)}, u32[]{:S(2)}) collective-permute-start(bf16[512,384]{1,0:T(8,128)(2,1)S(1)} %shard_map.112), channel_id=1, source_target_pairs={{0,8},{4,12},{8,0},{12,4},{16,24},{20,28},{24,16},{28,20},{1,9},{5... | collective-permute-start | bytes 1179656 | tf_op jit(solution)/shard_map/x_style_1/ppermute | solution.py:125
  19.2 1.5 %collective-permute-start.4 = (bf16[224,768]{1,0:T(8,128)(2,1)S(1)}, bf16[224,768]{1,0:T(8,128)(2,1)S(1)}, u32[]{:S(2)}, u32[]{:S(2)}) collective-permute-start(bf16[224,768]{1,0:T(8,128)(2,1)S(1)} %collective-permute-done.after.rest_0_.rest_1_), channel_id=1, source_target_pairs={{0,16},{4,20},{8,24},{12,28},{16,0},{20,4},{24,8},{28,12},{1,17},{... | collective-permute-start | bytes 1032200 | tf_op jit(solution)/shard_map/xy_kv/ppermute | solution.py:125
  21.4 0.7 shard_map.110
  22.2 0.6 collective-permute-start.11
  22.8 2.8 %collective-permute-done.13.came = bf16[512,384]{1,0:T(8,128)(2,1)S(1)} collective-permute-done((bf16[512,384]{1,0:T(8,128)(2,1)S(1)}, bf16[512,384]{1,0:T(8,128)(2,1)S(1)}, u32[]{:S(2)}, u32[]{:S(2)}) %collective-permute-start.13) | collective-permute-done | bytes 393248 | tf_op jit(solution)/shard_map/x_style_0/ppermute | solution.py:125
  25.6 0.2 shard_map.117.here
  25.8 1.8 %collective-permute-start.14 = (bf16[512,384]{1,0:T(8,128)(2,1)S(1)}, bf16[512,384]{1,0:T(8,128)(2,1)S(1)}, u32[]{:S(2)}, u32[]{:S(2)}) collective-permute-start(bf16[512,384]{1,0:T(8,128)(2,1)S(1)} %shard_map.117.here), channel_id=1, source_target_pairs={{0,16},{4,20},{8,24},{12,28},{16,0},{20,4},{24,8},{28,12},{1,17},{... | collective-permute-start | bytes 1179656 | tf_op jit(solution)/shard_map/y_style_0/ppermute | solution.py:125
  27.6 2.2 %collective-permute-done.4.rest_0_.rest_3_ = bf16[224,768]{1,0:T(8,128)(2,1)S(1)} collective-permute-done((bf16[224,768]{1,0:T(8,128)(2,1)S(1)}, bf16[224,768]{1,0:T(8,128)(2,1)S(1)}, u32[]{:S(2)}, u32[]{:S(2)}) %collective-permute-start.4) | collective-permute-done | bytes 344096 | tf_op jit(solution)/shard_map/xy_kv/ppermute | solution.py:125
  29.8 4.2 %collective-permute-done.3.came = bf16[512,384]{1,0:T(8,128)(2,1)S(1)} collective-permute-done((bf16[512,384]{1,0:T(8,128)(2,1)S(1)}, bf16[512,384]{1,0:T(8,128)(2,1)S(1)}, u32[]{:S(2)}, u32[]{:S(2)}) %collective-permute-start.3) | collective-permute-done | bytes 393248 | tf_op jit(solution)/shard_map/x_style_1/ppermute | solution.py:125
  34.0 0.2 shard_map.113.here.rest_0_
  34.2 1.8 %collective-permute-start.5 = (bf16[512,384]{1,0:T(8,128)(2,1)S(1)}, bf16[512,384]{1,0:T(8,128)(2,1)S(1)}, u32[]{:S(2)}, u32[]{:S(2)}) collective-permute-start(bf16[512,384]{1,0:T(8,128)(2,1)S(1)} %shard_map.113.here.rest_0_), channel_id=1, source_target_pairs={{0,16},{4,20},{8,24},{12,28},{16,0},{20,4},{24,8},{28,12},{1,17},{... | collective-permute-start | bytes 1179656 | tf_op jit(solution)/shard_map/y_style_1/ppermute | solution.py:125
  36.1 0.3 collective-permute-start.8
  36.6 1.4 %collective-permute-done.11.q.rest_1_ = bf16[240,384]{1,0:T(8,128)(2,1)S(1)} collective-permute-done((bf16[240,384]{1,0:T(8,128)(2,1)S(1)}, bf16[240,384]{1,0:T(8,128)(2,1)S(1)}, u32[]{:S(2)}, u32[]{:S(2)}) %collective-permute-start.11) | collective-permute-done | bytes 184352 | tf_op jit(solution)/shard_map/x_q/ppermute | solution.py:125
  38.2 1.4 %collective-permute-done.10.rest_7_ = bf16[224,768]{1,0:T(8,128)(2,1)S(1)} collective-permute-done((bf16[224,768]{1,0:T(8,128)(2,1)S(1)}, bf16[224,768]{1,0:T(8,128)(2,1)S(1)}, u32[]{:S(2)}, u32[]{:S(2)}) %collective-permute-start.10) | collective-permute-done | bytes 344096 | tf_op jit(solution)/shard_map/c_kv_3/ppermute | solution.py:125
  39.6 3.1 %shard_map.115 = (f32[224,384]{1,0:T(8,128)S(1)}, f32[224,128]{1,0:T(8,128)S(1)}) custom-call(s32[1,8]{1,0:T(1,128)S(1)} %copy-done.5, s32[1]{0:T(128)S(6)} %copy.12.counts, bf16[240,384]{1,0:T(8,128)(2,1)S(1)} %collective-permute-done.11.q.rest_1_, bf16[224,768]{1,0:T(8,128)(2,1)S(1)} %get-tuple-element.24.rest_0_, ...), custom_call_target="tpu_custom_call" | custom-call | flops 1 | bytes 1 | tf_op jit(solution)/shard_map/pallas_call | solution.py:423
  42.7 3.0 %shard_map.114 = (f32[224,384]{1,0:T(8,128)S(1)}, f32[224,128]{1,0:T(8,128)S(1)}) custom-call(s32[1,8]{1,0:T(1,128)S(1)} %copy-done.5, s32[1]{0:T(128)S(6)} %copy.12.counts, bf16[224,384]{1,0:T(8,128)(2,1)S(1)} %get-tuple-element.21.q, bf16[224,768]{1,0:T(8,128)(2,1)S(1)} %get-tuple-element.24.rest_0_, ...), custom_call_target="tpu_custom_call" | custom-call | flops 1 | bytes 1 | tf_op jit(solution)/shard_map/pallas_call | solution.py:423
  45.7 0.2 shard_map.118.held
  46.0 0.2 collective-permute-start.15
  46.5 0.3 collective-permute-start.12
  46.8 0.9 %collective-permute-done.15.swapped = bf16[512,384]{1,0:T(8,128)(2,1)S(1)} collective-permute-done((bf16[512,384]{1,0:T(8,128)(2,1)S(1)}, bf16[512,384]{1,0:T(8,128)(2,1)S(1)}, u32[]{:S(2)}, u32[]{:S(2)}) %collective-permute-start.15) | collective-permute-done | bytes 393248 | tf_op jit(solution)/shard_map/c_style_0/ppermute | solution.py:125
  47.7 1.4 %shard_map.121 = (f32[224,384]{1,0:T(8,128)S(1)}, f32[224,128]{1,0:T(8,128)S(1)}) custom-call(bf16[240,384]{1,0:T(8,128)(2,1)S(1)} %collective-permute-done.11.q.rest_1_, bf16[512,384]{1,0:T(8,128)(2,1)S(1)} %shard_map.118.held, bf16[512,384]{1,0:T(8,128)(2,1)S(1)} %collective-permute-done.15.swapped, f32[224,384]{1,0:T(8,128)S(1)} %get-tuple-element.32.acc_in, ...), custom_call_target="tpu_custom_call" | custom-call | flops 1 | bytes 1 | tf_op jit(solution)/shard_map/pallas_call | solution.py:440
  49.2 1.7 %shard_map.122 = bf16[224,384]{1,0:T(8,128)(2,1)S(1)} custom-call(bf16[240,384]{1,0:T(8,128)(2,1)S(1)} %collective-permute-done.11.q.rest_1_, bf16[512,384]{1,0:T(8,128)(2,1)S(1)} %shard_map.116.held, bf16[512,384]{1,0:T(8,128)(2,1)S(1)} %collective-permute-done.12.swapped, f32[224,384]{1,0:T(8,128)S(1)} %get-tuple-element.33.acc_in, ...), custom_call_target="tpu_custom_call" | custom-call | flops 1 | bytes 1 | tf_op jit(solution)/shard_map/pallas_call | solution.py:440
  50.9 1.8 %collective-permute-start.16 = (bf16[224,384]{1,0:T(8,128)(2,1)S(1)}, bf16[224,384]{1,0:T(8,128)(2,1)S(1)}, u32[]{:S(2)}, u32[]{:S(2)}) collective-permute-start(bf16[224,384]{1,0:T(8,128)(2,1)S(1)} %shard_map.122), channel_id=1, source_target_pairs={{0,8},{4,12},{8,0},{12,4},{16,24},{20,28},{24,16},{28,20},{1,9},{5... | collective-permute-start | bytes 516104 | tf_op jit(solution)/shard_map/x_back/ppermute | solution.py:125
  52.7 1.4 %shard_map.119 = (f32[224,384]{1,0:T(8,128)S(1)}, f32[224,128]{1,0:T(8,128)S(1)}) custom-call(bf16[224,384]{1,0:T(8,128)(2,1)S(1)} %get-tuple-element.21.q, bf16[512,384]{1,0:T(8,128)(2,1)S(1)} %shard_map.118.held, bf16[512,384]{1,0:T(8,128)(2,1)S(1)} %collective-permute-done.15.swapped, f32[224,384]{1,0:T(8,128)S(1)} %get-tuple-element.29.acc_in, ...), custom_call_target="tpu_custom_call" | custom-call | flops 1 | bytes 1 | tf_op jit(solution)/shard_map/pallas_call | solution.py:440
  54.1 1.5 %shard_map.120.own = bf16[224,384]{1,0:T(8,128)(2,1)S(1)} custom-call(bf16[224,384]{1,0:T(8,128)(2,1)S(1)} %get-tuple-element.21.q, bf16[512,384]{1,0:T(8,128)(2,1)S(1)} %shard_map.116.held, bf16[512,384]{1,0:T(8,128)(2,1)S(1)} %collective-permute-done.12.swapped, f32[224,384]{1,0:T(8,128)S(1)} %get-tuple-element.30.acc_in, ...), custom_call_target="tpu_custom_call" | custom-call | flops 1 | bytes 1 | tf_op jit(solution)/shard_map/pallas_call | solution.py:440
  55.6 2.0 %collective-permute-done.16.got = bf16[224,384]{1,0:T(8,128)(2,1)S(1)} collective-permute-done((bf16[224,384]{1,0:T(8,128)(2,1)S(1)}, bf16[224,384]{1,0:T(8,128)(2,1)S(1)}, u32[]{:S(2)}, u32[]{:S(2)}) %collective-permute-start.16) | collective-permute-done | bytes 172064 | tf_op jit(solution)/shard_map/x_back/ppermute | solution.py:125
  57.6 0.5 shard_map.125
  58.2 1.9 %collective-permute-start.18 = (bf16[224,768]{1,0:T(8,128)(2,1)S(1)}, bf16[224,768]{1,0:T(8,128)(2,1)S(1)}, u32[]{:S(2)}, u32[]{:S(2)}) collective-permute-start(bf16[224,768]{1,0:T(8,128)(2,1)S(1)} %shard_map.125), channel_id=1, source_target_pairs={{0,1},{1,0},{2,3},{3,2},{4,5},{5,4},{6,7},{7,6},{8,9},{9,8},{10,11... | collective-permute-start | bytes 1032200 | tf_op jit(solution)/shard_map/z_relay/ppermute | solution.py:125
  60.0 0.5 shard_map.124
  60.5 0.3 collective-permute-start.17
  60.8 8.4 %collective-permute-done.18.rest_0_ = bf16[224,768]{1,0:T(8,128)(2,1)S(1)} collective-permute-done((bf16[224,768]{1,0:T(8,128)(2,1)S(1)}, bf16[224,768]{1,0:T(8,128)(2,1)S(1)}, u32[]{:S(2)}, u32[]{:S(2)}) %collective-permute-start.18) | collective-permute-done | bytes 344096 | tf_op jit(solution)/shard_map/z_relay/ppermute | solution.py:125
  69.2 0.5 shard_map.126
  69.7 2.9 %collective-permute-start.19 = (bf16[224,768]{1,0:T(8,128)(2,1)S(1)}, bf16[224,768]{1,0:T(8,128)(2,1)S(1)}, u32[]{:S(2)}, u32[]{:S(2)}) collective-permute-start(bf16[224,768]{1,0:T(8,128)(2,1)S(1)} %shard_map.126), channel_id=1, source_target_pairs={{0,2},{1,3},{2,0},{3,1},{4,6},{5,7},{6,4},{7,5},{8,10},{9,11},{10,... | collective-permute-start | bytes 1032200 | tf_op jit(solution)/shard_map/z_far/ppermute | solution.py:125
  72.6 0.5 shard_map.123
  73.2 8.8 %collective-permute-done.17 = bf16[224,768]{1,0:T(8,128)(2,1)S(1)} collective-permute-done((bf16[224,768]{1,0:T(8,128)(2,1)S(1)}, bf16[224,768]{1,0:T(8,128)(2,1)S(1)}, u32[]{:S(2)}, u32[]{:S(2)}) %collective-permute-start.17) | collective-permute-done | bytes 344096 | tf_op jit(solution)/shard_map/z_near/ppermute | solution.py:125
  82.0 3.5 %collective-permute-done.19 = bf16[224,768]{1,0:T(8,128)(2,1)S(1)} collective-permute-done((bf16[224,768]{1,0:T(8,128)(2,1)S(1)}, bf16[224,768]{1,0:T(8,128)(2,1)S(1)}, u32[]{:S(2)}, u32[]{:S(2)}) %collective-permute-start.19) | collective-permute-done | bytes 344096 | tf_op jit(solution)/shard_map/z_far/ppermute | solution.py:125
  85.4 0.9 %add_convert_fusion = bf16[224,768]{1,0:T(8,128)(2,1)} fusion(bf16[224,768]{1,0:T(8,128)(2,1)S(1)} %collective-permute-done.19, f32[224,768]{1,0:T(8,128)S(1)} %shard_map.123, bf16[224,768]{1,0:T(8,128)(2,1)S(1)} %collective-permute-done.17, bf16[224,768]{1,0:T(8,128)(2,1)S(1)} %copy-done.6, f32[768]{0:T(1024)S(1)} %copy-done.7), kind=kLoop, calls=%fused_computation | loop fusion | flops 1376256 | bytes 2067456 | tf_op jit(solution)/shard_map/convert_element_type | solution.py:468
  (32 shorter events, 1.2 us)
Async XLA Ops:
  0.0 10.4 %collective-permute-start.1 = (bf16[1,1024,768]{2,1,0:T(8,128)(2,1)}, bf16[1,1024,768]{2,1,0:T(8,128)(2,1)S(1)}, u32[]{:S(2)}, u32[]{:S(2)}) collective-permute-start(bf16[1,1024,768]{2,1,0:T(8,128)(2,1)} %v.3), channel_id=1, source_target_pairs={{0,4},{8,12},{16,20},{24,28},{1,5},{9,13},{17,21},{25,29},{2,6},{1... | collective-permute-start | bytes 4718600 | tf_op jit(solution)/shard_map/core_style/ppermute | solution.py:379
  2.5 8.0 %collective-permute-start.2 = (bf16[1,1024,768]{2,1,0:T(8,128)(2,1)}, bf16[1,1024,768]{2,1,0:T(8,128)(2,1)S(1)}, u32[]{:S(2)}, u32[]{:S(2)}) collective-permute-start(bf16[1,1024,768]{2,1,0:T(8,128)(2,1)} %k.3), channel_id=1, source_target_pairs={{4,0},{12,8},{20,16},{28,24},{5,1},{13,9},{21,17},{29,25},{6,2},{1... | collective-permute-start | bytes 4718600 | tf_op jit(solution)/shard_map/core_style/ppermute | solution.py:380
  3.8 1.0 %copy-start.2 = (bf16[224,768]{1,0:T(8,128)(2,1)S(1)}, bf16[224,768]{1,0:T(8,128)(2,1)}, u32[]{:S(2)}) copy-start(bf16[224,768]{1,0:T(8,128)(2,1)} %k.2) | copy-start | bytes 1032196
  4.7 1.0 %copy-start.3 = (bf16[224,768]{1,0:T(8,128)(2,1)S(1)}, bf16[224,768]{1,0:T(8,128)(2,1)}, u32[]{:S(2)}) copy-start(bf16[224,768]{1,0:T(8,128)(2,1)} %v.2) | copy-start | bytes 1032196
  5.8 10.8 %collective-permute-start = (bf16[224,768]{1,0:T(8,128)(2,1)S(1)}, bf16[224,768]{1,0:T(8,128)(2,1)S(1)}, u32[]{:S(2)}, u32[]{:S(2)}) collective-permute-start(bf16[224,768]{1,0:T(8,128)(2,1)S(1)} %get-tuple-element.20), channel_id=1, source_target_pairs={{0,8},{4,12},{8,0},{12,4},{16,24},{20,28},{24,16},{28,20},{1,9},{5... | collective-permute-start | bytes 1032200 | tf_op jit(solution)/shard_map/x_kv/ppermute | solution.py:125
  8.2 13.9 %collective-permute-start.6 = (bf16[224,768]{1,0:T(8,128)(2,1)S(1)}, bf16[224,768]{1,0:T(8,128)(2,1)S(1)}, u32[]{:S(2)}, u32[]{:S(2)}) collective-permute-start(bf16[224,768]{1,0:T(8,128)(2,1)S(1)} %get-tuple-element.24.rest_0_), channel_id=1, source_target_pairs={{0,16},{4,20},{8,24},{12,28},{16,0},{20,4},{24,8},{28,12},{1,17},{... | collective-permute-start | bytes 1032200 | tf_op jit(solution)/shard_map/y_kv/ppermute | solution.py:125
  9.7 11.7 %copy-start.5 = (s32[1,8]{1,0:T(1,128)S(1)}, s32[1,8]{1,0:T(1,128)}, u32[]{:S(2)}) copy-start(s32[1,8]{1,0:T(1,128)} %lists.5) | copy-start | bytes 100
  10.4 1.4 %copy-start = (bf16[1,1024,768]{2,1,0:T(8,128)(2,1)S(1)}, bf16[1,1024,768]{2,1,0:T(8,128)(2,1)}, u32[]{:S(2)}) copy-start(bf16[1,1024,768]{2,1,0:T(8,128)(2,1)} %k.3) | copy-start | bytes 4718596
  11.8 1.4 %copy-start.1 = (bf16[1,1024,768]{2,1,0:T(8,128)(2,1)S(1)}, bf16[1,1024,768]{2,1,0:T(8,128)(2,1)}, u32[]{:S(2)}) copy-start(bf16[1,1024,768]{2,1,0:T(8,128)(2,1)} %v.3) | copy-start | bytes 4718596
  13.3 8.2 %copy-start.4 = (bf16[224,768]{1,0:T(8,128)(2,1)S(1)}, bf16[224,768]{1,0:T(8,128)(2,1)}, u32[]{:S(2)}) copy-start(bf16[224,768]{1,0:T(8,128)(2,1)} %q.1) | copy-start | bytes 1032196
  13.5 12.1 %collective-permute-start.13 = (bf16[512,384]{1,0:T(8,128)(2,1)S(1)}, bf16[512,384]{1,0:T(8,128)(2,1)S(1)}, u32[]{:S(2)}, u32[]{:S(2)}) collective-permute-start(bf16[512,384]{1,0:T(8,128)(2,1)S(1)} %get-tuple-element.28), channel_id=1, source_target_pairs={{0,8},{4,12},{8,0},{12,4},{16,24},{20,28},{24,16},{28,20},{1,9},{5... | collective-permute-start | bytes 1179656 | tf_op jit(solution)/shard_map/x_style_0/ppermute | solution.py:125
  16.9 17.1 %collective-permute-start.3 = (bf16[512,384]{1,0:T(8,128)(2,1)S(1)}, bf16[512,384]{1,0:T(8,128)(2,1)S(1)}, u32[]{:S(2)}, u32[]{:S(2)}) collective-permute-start(bf16[512,384]{1,0:T(8,128)(2,1)S(1)} %shard_map.112), channel_id=1, source_target_pairs={{0,8},{4,12},{8,0},{12,4},{16,24},{20,28},{24,16},{28,20},{1,9},{5... | collective-permute-start | bytes 1179656 | tf_op jit(solution)/shard_map/x_style_1/ppermute | solution.py:125
  19.2 10.6 %collective-permute-start.4 = (bf16[224,768]{1,0:T(8,128)(2,1)S(1)}, bf16[224,768]{1,0:T(8,128)(2,1)S(1)}, u32[]{:S(2)}, u32[]{:S(2)}) collective-permute-start(bf16[224,768]{1,0:T(8,128)(2,1)S(1)} %collective-permute-done.after.rest_0_.rest_1_), channel_id=1, source_target_pairs={{0,16},{4,20},{8,24},{12,28},{16,0},{20,4},{24,8},{28,12},{1,17},{... | collective-permute-start | bytes 1032200 | tf_op jit(solution)/shard_map/xy_kv/ppermute | solution.py:125
  20.7 15.7 %collective-permute-start.7 = (bf16[224,768]{1,0:T(8,128)(2,1)S(1)}, bf16[224,768]{1,0:T(8,128)(2,1)S(1)}, u32[]{:S(2)}, u32[]{:S(2)}) collective-permute-start(bf16[224,768]{1,0:T(8,128)(2,1)S(1)} %get-tuple-element.24.rest_0_), channel_id=1, source_target_pairs={{0,4},{4,0},{8,12},{12,8},{16,20},{20,16},{24,28},{28,24},{1,5},{5... | collective-permute-start | bytes 1032200 | tf_op jit(solution)/shard_map/c_kv_0/ppermute | solution.py:125
  22.2 15.8 %collective-permute-start.11 = (bf16[240,384]{1,0:T(8,128)(2,1)S(1)}, bf16[240,384]{1,0:T(8,128)(2,1)S(1)}, u32[]{:S(2)}, u32[]{:S(2)}) collective-permute-start(bf16[240,384]{1,0:T(8,128)(2,1)S(1)} %get-tuple-element.26), channel_id=1, source_target_pairs={{0,8},{4,12},{8,0},{12,4},{16,24},{20,28},{24,16},{28,20},{1,9},{5... | collective-permute-start | bytes 552968 | tf_op jit(solution)/shard_map/x_q/ppermute | solution.py:125
  25.8 19.9 %collective-permute-start.14 = (bf16[512,384]{1,0:T(8,128)(2,1)S(1)}, bf16[512,384]{1,0:T(8,128)(2,1)S(1)}, u32[]{:S(2)}, u32[]{:S(2)}) collective-permute-start(bf16[512,384]{1,0:T(8,128)(2,1)S(1)} %shard_map.117.here), channel_id=1, source_target_pairs={{0,16},{4,20},{8,24},{12,28},{16,0},{20,4},{24,8},{28,12},{1,17},{... | collective-permute-start | bytes 1179656 | tf_op jit(solution)/shard_map/y_style_0/ppermute | solution.py:125
  34.2 12.1 %collective-permute-start.5 = (bf16[512,384]{1,0:T(8,128)(2,1)S(1)}, bf16[512,384]{1,0:T(8,128)(2,1)S(1)}, u32[]{:S(2)}, u32[]{:S(2)}) collective-permute-start(bf16[512,384]{1,0:T(8,128)(2,1)S(1)} %shard_map.113.here.rest_0_), channel_id=1, source_target_pairs={{0,16},{4,20},{8,24},{12,28},{16,0},{20,4},{24,8},{28,12},{1,17},{... | collective-permute-start | bytes 1179656 | tf_op jit(solution)/shard_map/y_style_1/ppermute | solution.py:125
  36.1 2.0 %collective-permute-start.8 = (bf16[224,768]{1,0:T(8,128)(2,1)S(1)}, bf16[224,768]{1,0:T(8,128)(2,1)S(1)}, u32[]{:S(2)}, u32[]{:S(2)}) collective-permute-start(bf16[224,768]{1,0:T(8,128)(2,1)S(1)} %collective-permute-done.after.rest_0_.rest_1_), channel_id=1, source_target_pairs={{0,4},{4,0},{8,12},{12,8},{16,20},{20,16},{24,28},{28,24},{1,5},{5... | collective-permute-start | bytes 1032200 | tf_op jit(solution)/shard_map/c_kv_1/ppermute | solution.py:125
  36.4 1.8 %collective-permute-start.9 = (bf16[224,768]{1,0:T(8,128)(2,1)S(1)}, bf16[224,768]{1,0:T(8,128)(2,1)S(1)}, u32[]{:S(2)}, u32[]{:S(2)}) collective-permute-start(bf16[224,768]{1,0:T(8,128)(2,1)S(1)} %collective-permute-done.6.rest_2_.rest_1_), channel_id=1, source_target_pairs={{0,4},{4,0},{8,12},{12,8},{16,20},{20,16},{24,28},{28,24},{1,5},{5... | collective-permute-start | bytes 1032200 | tf_op jit(solution)/shard_map/c_kv_2/ppermute | solution.py:125
  37.9 1.7 %collective-permute-start.10 = (bf16[224,768]{1,0:T(8,128)(2,1)S(1)}, bf16[224,768]{1,0:T(8,128)(2,1)S(1)}, u32[]{:S(2)}, u32[]{:S(2)}) collective-permute-start(bf16[224,768]{1,0:T(8,128)(2,1)S(1)} %collective-permute-done.4.rest_0_.rest_3_), channel_id=1, source_target_pairs={{0,4},{4,0},{8,12},{12,8},{16,20},{20,16},{24,28},{28,24},{1,5},{5... | collective-permute-start | bytes 1032200 | tf_op jit(solution)/shard_map/c_kv_3/ppermute | solution.py:125
  39.6 18.0 %slice-start = ((s8[4718592]{0:T(1024)(128)(4,1)}), s8[4194304]{0:T(1024)(128)(4,1)S(1)}, s32[]{:S(2)}) async-start(s8[4718592]{0:T(1024)(128)(4,1)} %bitcast), calls=%async_computation | async-start | bytes 8388608
  45.7 11.9 %slice-start.1 = ((s8[4718592]{0:T(1024)(128)(4,1)}), s8[524288]{0:T(1024)(128)(4,1)S(1)}, s32[]{:S(2)}) async-start(s8[4718592]{0:T(1024)(128)(4,1)} %bitcast), calls=%async_computation.1 | async-start | bytes 1048576
  46.0 1.8 %collective-permute-start.15 = (bf16[512,384]{1,0:T(8,128)(2,1)S(1)}, bf16[512,384]{1,0:T(8,128)(2,1)S(1)}, u32[]{:S(2)}, u32[]{:S(2)}) collective-permute-start(bf16[512,384]{1,0:T(8,128)(2,1)S(1)} %shard_map.118.held), channel_id=1, source_target_pairs={{0,4},{4,0},{8,12},{12,8},{16,20},{20,16},{24,28},{28,24},{1,5},{5... | collective-permute-start | bytes 1179656 | tf_op jit(solution)/shard_map/c_style_0/ppermute | solution.py:125
  46.5 2.6 %collective-permute-start.12 = (bf16[512,384]{1,0:T(8,128)(2,1)S(1)}, bf16[512,384]{1,0:T(8,128)(2,1)S(1)}, u32[]{:S(2)}, u32[]{:S(2)}) collective-permute-start(bf16[512,384]{1,0:T(8,128)(2,1)S(1)} %shard_map.116.held), channel_id=1, source_target_pairs={{0,4},{4,0},{8,12},{12,8},{16,20},{20,16},{24,28},{28,24},{1,5},{5... | collective-permute-start | bytes 1179656 | tf_op jit(solution)/shard_map/c_style_1/ppermute | solution.py:125
  50.9 6.7 %collective-permute-start.16 = (bf16[224,384]{1,0:T(8,128)(2,1)S(1)}, bf16[224,384]{1,0:T(8,128)(2,1)S(1)}, u32[]{:S(2)}, u32[]{:S(2)}) collective-permute-start(bf16[224,384]{1,0:T(8,128)(2,1)S(1)} %shard_map.122), channel_id=1, source_target_pairs={{0,8},{4,12},{8,0},{12,4},{16,24},{20,28},{24,16},{28,20},{1,9},{5... | collective-permute-start | bytes 516104 | tf_op jit(solution)/shard_map/x_back/ppermute | solution.py:125
  58.2 11.0 %collective-permute-start.18 = (bf16[224,768]{1,0:T(8,128)(2,1)S(1)}, bf16[224,768]{1,0:T(8,128)(2,1)S(1)}, u32[]{:S(2)}, u32[]{:S(2)}) collective-permute-start(bf16[224,768]{1,0:T(8,128)(2,1)S(1)} %shard_map.125), channel_id=1, source_target_pairs={{0,1},{1,0},{2,3},{3,2},{4,5},{5,4},{6,7},{7,6},{8,9},{9,8},{10,11... | collective-permute-start | bytes 1032200 | tf_op jit(solution)/shard_map/z_relay/ppermute | solution.py:125
  60.5 21.4 %collective-permute-start.17 = (bf16[224,768]{1,0:T(8,128)(2,1)S(1)}, bf16[224,768]{1,0:T(8,128)(2,1)S(1)}, u32[]{:S(2)}, u32[]{:S(2)}) collective-permute-start(bf16[224,768]{1,0:T(8,128)(2,1)S(1)} %shard_map.124), channel_id=1, source_target_pairs={{0,1},{1,0},{2,3},{3,2},{4,5},{5,4},{6,7},{7,6},{8,9},{9,8},{10,11... | collective-permute-start | bytes 1032200 | tf_op jit(solution)/shard_map/z_near/ppermute | solution.py:125
  69.7 15.7 %copy-start.6 = (bf16[224,768]{1,0:T(8,128)(2,1)S(1)}, bf16[224,768]{1,0:T(8,128)(2,1)}, u32[]{:S(2)}) copy-start(bf16[224,768]{1,0:T(8,128)(2,1)} %param.20) | copy-start | bytes 1032196
  69.7 15.7 %copy-start.7 = (f32[768]{0:T(1024)S(1)}, f32[768]{0:T(1024)}, u32[]{:S(2)}) copy-start(f32[768]{0:T(1024)} %param.21) | copy-start | bytes 9220
  69.7 15.7 %collective-permute-start.19 = (bf16[224,768]{1,0:T(8,128)(2,1)S(1)}, bf16[224,768]{1,0:T(8,128)(2,1)S(1)}, u32[]{:S(2)}, u32[]{:S(2)}) collective-permute-start(bf16[224,768]{1,0:T(8,128)(2,1)S(1)} %shard_map.126), channel_id=1, source_target_pairs={{0,2},{1,3},{2,0},{3,1},{4,6},{5,7},{6,4},{7,5},{8,10},{9,11},{10,... | collective-permute-start | bytes 1032200 | tf_op jit(solution)/shard_map/z_far/ppermute | solution.py:125

commit v4 on v3

--- a/solution.py
+++ b/solution.py
@@ -184,7 +184,7 @@
         copy.wait()
 
 
-def pick_kernel(owner, k, v, from_even, from_odd, send_a, send_b, keep, sems):
+def pick_kernel(owner, k, v, from_even, from_odd, after, send_a, send_b, keep, sems):
     first, width = send_a.shape
     second = send_b.shape[0]
     mine, other = halves(width)
@@ -330,7 +330,7 @@
 ANY = pl.BlockSpec(memory_space=pl.ANY)
 
 
-def call(kernel, in_specs, outs, scratch=(), out_spec=VMEM):
+def call(kernel, in_specs, outs, scratch=(), out_spec=VMEM, flops=1):
     shapes = [jax.ShapeDtypeStruct(shape, dtype) for shape, dtype in outs]
     return pl.pallas_call(
         kernel,
@@ -339,7 +339,7 @@
         out_specs=[out_spec] * len(shapes),
         scratch_shapes=list(scratch),
         compiler_params=pltpu.CompilerParams(vmem_limit_bytes=VMEM_LIMIT),
-        cost_estimate=pl.CostEstimate(flops=1, bytes_accessed=1, transcendentals=0),
+        cost_estimate=pl.CostEstimate(flops=flops, bytes_accessed=1, transcendentals=0),
     )
 
 
@@ -347,9 +347,9 @@
     return pltpu.SemaphoreType.DMA((count,))
 
 
-def later(block, *after):
+def later(block, *after, flops=1):
     return call(
-        hold_kernel, [ANY] * (1 + len(after)), [(block.shape, block.dtype)], scratch=[dma(1)]
+        hold_kernel, [ANY] * (1 + len(after)), [(block.shape, block.dtype)], scratch=[dma(1)], flops=flops
     )(block, *after)[0]
 
 
@@ -379,24 +379,32 @@
         from_even = lax.ppermute(ref_values, "frame", even)
         from_odd = lax.ppermute(ref_keys, "frame", odd)
 
-    kv = ((rows, 2 * width), bf16)
-    kv_keep, kv_send = call(
-        split_kernel, [ANY] * 2, [kv, kv], scratch=[dma(4)]
-    )(key_rows, value_rows)
+    right = (lax.axis_index("frame") // ROW) % 2 == 1
+
+    def half_of(block, flag):
+        return jnp.where(flag, block[:, width:], block[:, :width])
+
+    kv_send, kv_keep = [
+        jnp.concatenate([half_of(key_rows, flag), half_of(value_rows, flag)], axis=1)
+        for flag in (jnp.logical_not(right), right)
+    ]
     kv_x = swap(kv_send, "frame", ROW, "x_kv")
     kv_y = swap(kv_keep, "frame", COLUMN, "y_kv")
     kv_xy = swap(kv_x, "frame", COLUMN, "xy_kv")
 
-    second = style // 2
-    first = style - second
+    near = [kv_keep, kv_x, kv_y, kv_xy]
+    near = near + [swap(block, "frame", CORE, f"c_kv_{n}") for n, block in enumerate(near)]
+    ready = later(kv_x[:16], kv_x, kv_y, flops=4 * 10**10)
+    first = style * 16 // 32
+    second = style - first
     parts = [((first, width), bf16), ((second, width), bf16)]
     send_a, send_b, keep = call(
         pick_kernel,
-        [SMEM] + [ANY] * 4,
+        [SMEM] + [ANY] * 5,
         parts + [((style, width), bf16)],
         scratch=[dma(3)],
-    )(owner_index, ref_keys, ref_values, from_even, from_odd)
-    send_b = later(send_b, kv_x)
+    )(owner_index, ref_keys, ref_values, from_even, from_odd, ready)
+    send_b = later(send_b, near[4])
 
     def choose(part, bit, begin, here, came, *after):
         return call(
@@ -404,6 +412,7 @@
             [SMEM] + [ANY] * (2 + len(after)),
             [part],
             scratch=[dma(1)],
+            flops=1,
         )(owner_index, here, came, *after)[0]
 
     x_came = [swap(sent, "frame", ROW, f"x_style_{j}") for j, sent in enumerate((send_a, send_b))]
@@ -412,11 +421,9 @@
         [SMEM, SMEM, ANY, ANY],
         [((rows, width), bf16), ((rows + 16, width), bf16)],
         scratch=[dma(2)],
-    )(key_lists, list_counts, queries, kv_x)
+    )(key_lists, list_counts, queries, kv_y)
     q_got = swap(q_send, "frame", ROW, "x_q")
 
-    near = [kv_keep, kv_x, kv_y, kv_xy]
-    near = near + [swap(block, "frame", CORE, f"c_kv_{n}") for n, block in enumerate(near)]
     state = [((rows, width), f32), ((rows, HD), f32)]
 
     def frames_of(remote, q):
@@ -424,11 +431,12 @@
             functools.partial(frames_kernel, remote),
             [SMEM, SMEM] + [VMEM] * 9,
             state,
+            flops=3 * 10**9,
         )(key_lists, list_counts, q, *near)
 
     chosen = [
         choose(parts[j], ROW, j * first, keep, x_came[j], *after)
-        for j, after in enumerate(((kv_x, kv_y), (kv_xy,)))
+        for j, after in enumerate(((kv_x,), (kv_xy, *near[4:],)))
     ]
     y_came = [swap(block, "frame", COLUMN, f"y_style_{j}") for j, block in enumerate(chosen)]
 
@@ -441,12 +449,13 @@
             functools.partial(style_kernel, last),
             [VMEM] * 5,
             [((rows, width), bf16)] if last else state,
+            flops=10**9,
         )(q, *blocks, *held_state)
 
     own_state = frames_of(False, q_keep)
     their_state = frames_of(True, q_got)
     seen = own_state[1], their_state[1]
-    blocks = finish(0, chosen[1], q_got)
+    blocks = finish(0, seen[0])
     own_state = style_of(False, 0, q_keep, blocks, own_state)
     their_state = style_of(False, 0, q_got, blocks, their_state)
     blocks = finish(1, *seen)

time: 86.6 us -> 82.9 us (0.957)
  local copies, waits for them, and re-layouts: 4.79 us -> 0.05 us
  other arithmetic: 0.9 us -> 2.32 us
  starting transfers between devices: 24.4 us -> 23 us
  waiting for transfers between devices: 38.5 us -> 39.6 us
    unnamed x20 -> x16, local copies, waits for them, and re-layouts: 4.79 us -> 0.05 us
    ppermute x18, starting transfers between devices: 20.6 us -> 19.2 us  [swap(): lax.ppermute(block, axis, [(i, i ^ bit) for i in range(lax.axis_size(axis...]
    select_n x0 -> x1, other arithmetic: none -> 1.35 us  [half_of(): return jnp.where(flag, block[:, width:], block[:, :width])]
    ppermute x18, waiting for transfers between devices: 38.5 us -> 39.6 us  [swap(): lax.ppermute(block, axis, [(i, i ^ bit) for i in range(lax.axis_size(axis...]
  transfers between devices with their start and end apart: 20 -> 20, of which waited for: 13 -> 10; matrix products, arithmetic and copies ran while one was open for 0% -> 0% of each run, Pallas kernels for 16% -> 17%
where the time goes in v4:
time: 82.9 us; the launch traced here: 82.7 us
  waiting for transfers between devices  39.6 us (48%)
  starting transfers between devices  23 us (28%)
  Pallas kernels  16.1 us (19%)
  other arithmetic  2.32 us (3%)
  between operations  1.62 us (2%)
    ppermute x18, waiting for transfers between devices, swap(): lax.ppermute(block, axis, [(i, i ^ bit) for i in range(lax.axis_size(axis...  39.6 us
    ppermute x18, starting transfers between devices, swap(): lax.ppermute(block, axis, [(i, i ^ bit) for i in range(lax.axis_size(axis...  19.2 us
    pallas_call x2, Pallas kernels, frames_of(): call(functools.partial(frames_kernel, remote), [SMEM, SMEM] + [VMEM] * 9,...  6.04 us
    pallas_call x4, Pallas kernels, style_of(): call(functools.partial(style_kernel, last), [VMEM] * 5, [((rows, width),...  6.01 us
    ppermute x1, starting transfers between devices, paired_device(): from_even = lax.ppermute(ref_values, 'frame', even)  2.5 us
    pallas_call x4, Pallas kernels, project(): call(functools.partial(project_kernel, bit), [VMEM] * (3 + len(came)), [(...  2.05 us
  transfers between devices with their start and end apart: 20, of which 10 were waited for; matrix products, arithmetic and copies ran while one was open for 0% of the time, Pallas kernels for 17%

profile of v4, /device:TPU:0, one launch (start us, length us, event | category | flops | bytes accessed | tf_op | source)
XLA Modules:
  0.0 82.7 jit_solution(221616177932882854)
XLA Ops:
  0.0 1.4 %broadcast_select_fusion = (bf16[224,384]{1,0:T(8,128)(2,1)S(1)}, bf16[224,384]{1,0:T(8,128)(2,1)S(1)}, bf16[224,384]{1,0:T(8,128)(2,1)S(1)}, bf16[224,384]{1,0:T(8,128)(2,1)S(1)}) fusion(pred[]{:T(512)S(6)} %not.3, bf16[224,768]{1,0:T(8,128)(2,1)} %param.13, pred[]{:T(512)S(6)} %eq.5, bf16[224,768]{1,0:T(8,128)(2,1)} %param.12), kind=kLoop, calls=%fused_computation.3 | loop fusion | flops 344064 | bytes 1376258 | tf_op jit(solution)/shard_map/jit(_where)/select_n | solution.py:385
  1.4 3.0 %collective-permute-start.3 = (bf16[224,768]{1,0:T(8,128)(2,1)S(1)}, bf16[224,768]{1,0:T(8,128)(2,1)S(1)}, u32[]{:S(2)}, u32[]{:S(2)}) collective-permute-start(bf16[224,768]{1,0:T(8,128)(2,1)S(1)} %pad_maximum_fusion.1), channel_id=1, source_target_pairs={{0,8},{4,12},{8,0},{12,4},{16,24},{20,28},{24,16},{28,20},{1,9},{5... | collective-permute-start | bytes 1032200 | tf_op jit(solution)/shard_map/x_kv/ppermute | solution.py:125
  4.4 1.6 %collective-permute-start = (bf16[224,768]{1,0:T(8,128)(2,1)S(1)}, bf16[224,768]{1,0:T(8,128)(2,1)S(1)}, u32[]{:S(2)}, u32[]{:S(2)}) collective-permute-start(bf16[224,768]{1,0:T(8,128)(2,1)S(1)} %pad_maximum_fusion.rest_0_), channel_id=1, source_target_pairs={{0,16},{4,20},{8,24},{12,28},{16,0},{20,4},{24,8},{28,12},{1,17},{... | collective-permute-start | bytes 1032200 | tf_op jit(solution)/shard_map/y_kv/ppermute | solution.py:125
  6.0 2.5 %collective-permute-start.1 = (bf16[1,1024,768]{2,1,0:T(8,128)(2,1)}, bf16[1,1024,768]{2,1,0:T(8,128)(2,1)S(1)}, u32[]{:S(2)}, u32[]{:S(2)}) collective-permute-start(bf16[1,1024,768]{2,1,0:T(8,128)(2,1)} %v.1), channel_id=1, source_target_pairs={{0,4},{8,12},{16,20},{24,28},{1,5},{9,13},{17,21},{25,29},{2,6},{1... | collective-permute-start | bytes 4718600 | tf_op jit(solution)/shard_map/core_style/ppermute | solution.py:379
  8.5 1.3 %collective-permute-start.2 = (bf16[1,1024,768]{2,1,0:T(8,128)(2,1)S(1)}, bf16[1,1024,768]{2,1,0:T(8,128)(2,1)S(1)}, u32[]{:S(2)}, u32[]{:S(2)}) collective-permute-start(bf16[1,1024,768]{2,1,0:T(8,128)(2,1)S(1)} %copy-done), channel_id=1, source_target_pairs={{4,0},{12,8},{20,16},{28,24},{5,1},{13,9},{21,17},{29,25},{6,2},{1... | collective-permute-start | bytes 4718600 | tf_op jit(solution)/shard_map/core_style/ppermute | solution.py:380
  10.5 2.0 %collective-permute-done.3.rest_0_.rest_1_ = bf16[224,768]{1,0:T(8,128)(2,1)S(1)} collective-permute-done((bf16[224,768]{1,0:T(8,128)(2,1)S(1)}, bf16[224,768]{1,0:T(8,128)(2,1)S(1)}, u32[]{:S(2)}, u32[]{:S(2)}) %collective-permute-start.3) | collective-permute-done | bytes 344096 | tf_op jit(solution)/shard_map/x_kv/ppermute | solution.py:125
  12.5 1.8 %collective-permute-start.6 = (bf16[224,768]{1,0:T(8,128)(2,1)S(1)}, bf16[224,768]{1,0:T(8,128)(2,1)S(1)}, u32[]{:S(2)}, u32[]{:S(2)}) collective-permute-start(bf16[224,768]{1,0:T(8,128)(2,1)S(1)} %collective-permute-done.3.rest_0_.rest_1_), channel_id=1, source_target_pairs={{0,16},{4,20},{8,24},{12,28},{16,0},{20,4},{24,8},{28,12},{1,17},{... | collective-permute-start | bytes 1032200 | tf_op jit(solution)/shard_map/xy_kv/ppermute | solution.py:125
  14.3 0.2 shard_map.111
  14.6 1.6 %collective-permute-start.13 = (bf16[512,384]{1,0:T(8,128)(2,1)S(1)}, bf16[512,384]{1,0:T(8,128)(2,1)S(1)}, u32[]{:S(2)}, u32[]{:S(2)}) collective-permute-start(bf16[512,384]{1,0:T(8,128)(2,1)S(1)} %get-tuple-element.24), channel_id=1, source_target_pairs={{0,8},{4,12},{8,0},{12,4},{16,24},{20,28},{24,16},{28,20},{1,9},{5... | collective-permute-start | bytes 1179656 | tf_op jit(solution)/shard_map/x_style_0/ppermute | solution.py:125
  16.1 0.2 shard_map.112
  16.3 0.6 collective-permute-start.5
  16.9 0.5 collective-permute-start.8
  17.4 4.3 %collective-permute-done.6.rest_0_.rest_3_ = bf16[224,768]{1,0:T(8,128)(2,1)S(1)} collective-permute-done((bf16[224,768]{1,0:T(8,128)(2,1)S(1)}, bf16[224,768]{1,0:T(8,128)(2,1)S(1)}, u32[]{:S(2)}, u32[]{:S(2)}) %collective-permute-start.6) | collective-permute-done | bytes 344096 | tf_op jit(solution)/shard_map/xy_kv/ppermute | solution.py:125
  21.8 4.9 %collective-permute-done.13.came = bf16[512,384]{1,0:T(8,128)(2,1)S(1)} collective-permute-done((bf16[512,384]{1,0:T(8,128)(2,1)S(1)}, bf16[512,384]{1,0:T(8,128)(2,1)S(1)}, u32[]{:S(2)}, u32[]{:S(2)}) %collective-permute-start.13) | collective-permute-done | bytes 393248 | tf_op jit(solution)/shard_map/x_style_0/ppermute | solution.py:125
  26.7 0.2 shard_map.117.here
  26.9 1.4 %collective-permute-start.14 = (bf16[512,384]{1,0:T(8,128)(2,1)S(1)}, bf16[512,384]{1,0:T(8,128)(2,1)S(1)}, u32[]{:S(2)}, u32[]{:S(2)}) collective-permute-start(bf16[512,384]{1,0:T(8,128)(2,1)S(1)} %shard_map.117.here), channel_id=1, source_target_pairs={{0,16},{4,20},{8,24},{12,28},{16,0},{20,4},{24,8},{28,12},{1,17},{... | collective-permute-start | bytes 1179656 | tf_op jit(solution)/shard_map/y_style_0/ppermute | solution.py:125
  28.9 0.7 shard_map.109
  29.7 1.6 %collective-permute-start.11 = (bf16[240,384]{1,0:T(8,128)(2,1)S(1)}, bf16[240,384]{1,0:T(8,128)(2,1)S(1)}, u32[]{:S(2)}, u32[]{:S(2)}) collective-permute-start(bf16[240,384]{1,0:T(8,128)(2,1)S(1)} %get-tuple-element.22), channel_id=1, source_target_pairs={{0,8},{4,12},{8,0},{12,4},{16,24},{20,28},{24,16},{28,20},{1,9},{5... | collective-permute-start | bytes 552968 | tf_op jit(solution)/shard_map/x_q/ppermute | solution.py:125
  31.2 3.9 %collective-permute-done.5.came = bf16[512,384]{1,0:T(8,128)(2,1)S(1)} collective-permute-done((bf16[512,384]{1,0:T(8,128)(2,1)S(1)}, bf16[512,384]{1,0:T(8,128)(2,1)S(1)}, u32[]{:S(2)}, u32[]{:S(2)}) %collective-permute-start.5) | collective-permute-done | bytes 393248 | tf_op jit(solution)/shard_map/x_style_1/ppermute | solution.py:125
  35.1 0.2 shard_map.113.here
  35.3 1.3 %collective-permute-start.10 = (bf16[512,384]{1,0:T(8,128)(2,1)S(1)}, bf16[512,384]{1,0:T(8,128)(2,1)S(1)}, u32[]{:S(2)}, u32[]{:S(2)}) collective-permute-start(bf16[512,384]{1,0:T(8,128)(2,1)S(1)} %shard_map.113.here), channel_id=1, source_target_pairs={{0,16},{4,20},{8,24},{12,28},{16,0},{20,4},{24,8},{28,12},{1,17},{... | collective-permute-start | bytes 1179656 | tf_op jit(solution)/shard_map/y_style_1/ppermute | solution.py:125
  36.6 3.0 %shard_map.114 = (f32[224,384]{1,0:T(8,128)S(1)}, f32[224,128]{1,0:T(8,128)S(1)}) custom-call(s32[1,8]{1,0:T(1,128)S(1)} %copy-done.3, s32[1]{0:T(128)S(6)} %copy.12.counts, bf16[224,384]{1,0:T(8,128)(2,1)S(1)} %get-tuple-element.18.q, bf16[224,768]{1,0:T(8,128)(2,1)S(1)} %pad_maximum_fusion.rest_0_, ...), custom_call_target="tpu_custom_call" | custom-call | flops 3000000000 | bytes 1 | tf_op jit(solution)/shard_map/pallas_call | solution.py:430
  39.6 0.2 shard_map.118.held
  39.9 0.1 collective-permute-start.15
  40.0 0.0 slice-start
  40.0 3.0 %shard_map.115 = (f32[224,384]{1,0:T(8,128)S(1)}, f32[224,128]{1,0:T(8,128)S(1)}) custom-call(s32[1,8]{1,0:T(1,128)S(1)} %copy-done.3, s32[1]{0:T(128)S(6)} %copy.12.counts, bf16[240,384]{1,0:T(8,128)(2,1)S(1)} %collective-permute-done.11.q, bf16[224,768]{1,0:T(8,128)(2,1)S(1)} %pad_maximum_fusion.rest_0_, ...), custom_call_target="tpu_custom_call" | custom-call | flops 3000000000 | bytes 1 | tf_op jit(solution)/shard_map/pallas_call | solution.py:430
  43.0 0.8 collective-permute-done.10.came
  43.8 0.2 shard_map.116.held
  44.0 0.1 collective-permute-start.12
  44.1 0.0 slice-start.1
  44.1 1.4 %shard_map.121 = (f32[224,384]{1,0:T(8,128)S(1)}, f32[224,128]{1,0:T(8,128)S(1)}) custom-call(bf16[240,384]{1,0:T(8,128)(2,1)S(1)} %collective-permute-done.11.q, bf16[512,384]{1,0:T(8,128)(2,1)S(1)} %shard_map.118.held, bf16[512,384]{1,0:T(8,128)(2,1)S(1)} %collective-permute-done.15.swapped, f32[224,384]{1,0:T(8,128)S(1)} %get-tuple-element.28.acc_in, ...), custom_call_target="tpu_custom_call" | custom-call | flops 1000000000 | bytes 1 | tf_op jit(solution)/shard_map/pallas_call | solution.py:448
  45.5 0.2 collective-permute-done.12.swapped
  45.8 1.7 %shard_map.122 = bf16[224,384]{1,0:T(8,128)(2,1)S(1)} custom-call(bf16[240,384]{1,0:T(8,128)(2,1)S(1)} %collective-permute-done.11.q, bf16[512,384]{1,0:T(8,128)(2,1)S(1)} %shard_map.116.held, bf16[512,384]{1,0:T(8,128)(2,1)S(1)} %collective-permute-done.12.swapped, f32[224,384]{1,0:T(8,128)S(1)} %get-tuple-element.29.acc_in, ...), custom_call_target="tpu_custom_call" | custom-call | flops 1000000000 | bytes 1 | tf_op jit(solution)/shard_map/pallas_call | solution.py:448
  47.4 1.0 %collective-permute-start.16 = (bf16[224,384]{1,0:T(8,128)(2,1)S(1)}, bf16[224,384]{1,0:T(8,128)(2,1)S(1)}, u32[]{:S(2)}, u32[]{:S(2)}) collective-permute-start(bf16[224,384]{1,0:T(8,128)(2,1)S(1)} %shard_map.122), channel_id=1, source_target_pairs={{0,8},{4,12},{8,0},{12,4},{16,24},{20,28},{24,16},{28,20},{1,9},{5... | collective-permute-start | bytes 516104 | tf_op jit(solution)/shard_map/x_back/ppermute | solution.py:125
  48.5 1.4 %shard_map.119 = (f32[224,384]{1,0:T(8,128)S(1)}, f32[224,128]{1,0:T(8,128)S(1)}) custom-call(bf16[224,384]{1,0:T(8,128)(2,1)S(1)} %get-tuple-element.18.q, bf16[512,384]{1,0:T(8,128)(2,1)S(1)} %shard_map.118.held, bf16[512,384]{1,0:T(8,128)(2,1)S(1)} %collective-permute-done.15.swapped, f32[224,384]{1,0:T(8,128)S(1)} %get-tuple-element.25.acc_in, ...), custom_call_target="tpu_custom_call" | custom-call | flops 1000000000 | bytes 1 | tf_op jit(solution)/shard_map/pallas_call | solution.py:448
  49.9 1.5 %shard_map.120.own = bf16[224,384]{1,0:T(8,128)(2,1)S(1)} custom-call(bf16[224,384]{1,0:T(8,128)(2,1)S(1)} %get-tuple-element.18.q, bf16[512,384]{1,0:T(8,128)(2,1)S(1)} %shard_map.116.held, bf16[512,384]{1,0:T(8,128)(2,1)S(1)} %collective-permute-done.12.swapped, f32[224,384]{1,0:T(8,128)S(1)} %get-tuple-element.26.acc_in, ...), custom_call_target="tpu_custom_call" | custom-call | flops 1000000000 | bytes 1 | tf_op jit(solution)/shard_map/pallas_call | solution.py:448
  51.4 2.6 %collective-permute-done.16.got = bf16[224,384]{1,0:T(8,128)(2,1)S(1)} collective-permute-done((bf16[224,384]{1,0:T(8,128)(2,1)S(1)}, bf16[224,384]{1,0:T(8,128)(2,1)S(1)}, u32[]{:S(2)}, u32[]{:S(2)}) %collective-permute-start.16) | collective-permute-done | bytes 172064 | tf_op jit(solution)/shard_map/x_back/ppermute | solution.py:125
  54.0 0.5 shard_map.125
  54.6 1.6 %collective-permute-start.18 = (bf16[224,768]{1,0:T(8,128)(2,1)S(1)}, bf16[224,768]{1,0:T(8,128)(2,1)S(1)}, u32[]{:S(2)}, u32[]{:S(2)}) collective-permute-start(bf16[224,768]{1,0:T(8,128)(2,1)S(1)} %shard_map.125), channel_id=1, source_target_pairs={{0,1},{1,0},{2,3},{3,2},{4,5},{5,4},{6,7},{7,6},{8,9},{9,8},{10,11... | collective-permute-start | bytes 1032200 | tf_op jit(solution)/shard_map/z_relay/ppermute | solution.py:125
  56.2 0.5 shard_map.124
  56.7 0.5 collective-permute-start.17
  57.2 8.4 %collective-permute-done.18.rest_0_ = bf16[224,768]{1,0:T(8,128)(2,1)S(1)} collective-permute-done((bf16[224,768]{1,0:T(8,128)(2,1)S(1)}, bf16[224,768]{1,0:T(8,128)(2,1)S(1)}, u32[]{:S(2)}, u32[]{:S(2)}) %collective-permute-start.18) | collective-permute-done | bytes 344096 | tf_op jit(solution)/shard_map/z_relay/ppermute | solution.py:125
  65.6 0.5 shard_map.126
  66.2 2.7 %collective-permute-start.19 = (bf16[224,768]{1,0:T(8,128)(2,1)S(1)}, bf16[224,768]{1,0:T(8,128)(2,1)S(1)}, u32[]{:S(2)}, u32[]{:S(2)}) collective-permute-start(bf16[224,768]{1,0:T(8,128)(2,1)S(1)} %shard_map.126), channel_id=1, source_target_pairs={{0,2},{1,3},{2,0},{3,1},{4,6},{5,7},{6,4},{7,5},{8,10},{9,11},{10,... | collective-permute-start | bytes 1032200 | tf_op jit(solution)/shard_map/z_far/ppermute | solution.py:125
  68.8 0.5 shard_map.123
  69.3 8.6 %collective-permute-done.17 = bf16[224,768]{1,0:T(8,128)(2,1)S(1)} collective-permute-done((bf16[224,768]{1,0:T(8,128)(2,1)S(1)}, bf16[224,768]{1,0:T(8,128)(2,1)S(1)}, u32[]{:S(2)}, u32[]{:S(2)}) %collective-permute-start.17) | collective-permute-done | bytes 344096 | tf_op jit(solution)/shard_map/z_near/ppermute | solution.py:125
  77.9 3.8 %collective-permute-done.19 = bf16[224,768]{1,0:T(8,128)(2,1)S(1)} collective-permute-done((bf16[224,768]{1,0:T(8,128)(2,1)S(1)}, bf16[224,768]{1,0:T(8,128)(2,1)S(1)}, u32[]{:S(2)}, u32[]{:S(2)}) %collective-permute-start.19) | collective-permute-done | bytes 344096 | tf_op jit(solution)/shard_map/z_far/ppermute | solution.py:125
  81.8 0.9 %add_convert_fusion = bf16[224,768]{1,0:T(8,128)(2,1)} fusion(bf16[224,768]{1,0:T(8,128)(2,1)S(1)} %collective-permute-done.19, f32[224,768]{1,0:T(8,128)S(1)} %shard_map.123, bf16[224,768]{1,0:T(8,128)(2,1)S(1)} %collective-permute-done.17, bf16[224,768]{1,0:T(8,128)(2,1)S(1)} %copy-done.4, f32[768]{0:T(1024)S(1)} %copy-done.5), kind=kLoop, calls=%fused_computation | loop fusion | flops 1376256 | bytes 2067456 | tf_op jit(solution)/shard_map/convert_element_type | solution.py:477
  (32 shorter events, 0.2 us)
Async XLA Ops:
  0.0 8.5 %copy-start = (bf16[1,1024,768]{2,1,0:T(8,128)(2,1)S(1)}, bf16[1,1024,768]{2,1,0:T(8,128)(2,1)}, u32[]{:S(2)}) copy-start(bf16[1,1024,768]{2,1,0:T(8,128)(2,1)} %k.1) | copy-start | bytes 4718596
  1.4 11.1 %collective-permute-start.3 = (bf16[224,768]{1,0:T(8,128)(2,1)S(1)}, bf16[224,768]{1,0:T(8,128)(2,1)S(1)}, u32[]{:S(2)}, u32[]{:S(2)}) collective-permute-start(bf16[224,768]{1,0:T(8,128)(2,1)S(1)} %pad_maximum_fusion.1), channel_id=1, source_target_pairs={{0,8},{4,12},{8,0},{12,4},{16,24},{20,28},{24,16},{28,20},{1,9},{5... | collective-permute-start | bytes 1032200 | tf_op jit(solution)/shard_map/x_kv/ppermute | solution.py:125
  4.4 9.8 %collective-permute-start = (bf16[224,768]{1,0:T(8,128)(2,1)S(1)}, bf16[224,768]{1,0:T(8,128)(2,1)S(1)}, u32[]{:S(2)}, u32[]{:S(2)}) collective-permute-start(bf16[224,768]{1,0:T(8,128)(2,1)S(1)} %pad_maximum_fusion.rest_0_), channel_id=1, source_target_pairs={{0,16},{4,20},{8,24},{12,28},{16,0},{20,4},{24,8},{28,12},{1,17},{... | collective-permute-start | bytes 1032200 | tf_op jit(solution)/shard_map/y_kv/ppermute | solution.py:125
  6.0 10.1 %collective-permute-start.4 = (bf16[224,768]{1,0:T(8,128)(2,1)S(1)}, bf16[224,768]{1,0:T(8,128)(2,1)S(1)}, u32[]{:S(2)}, u32[]{:S(2)}) collective-permute-start(bf16[224,768]{1,0:T(8,128)(2,1)S(1)} %pad_maximum_fusion.rest_0_), channel_id=1, source_target_pairs={{0,4},{4,0},{8,12},{12,8},{16,20},{20,16},{24,28},{28,24},{1,5},{5... | collective-permute-start | bytes 1032200 | tf_op jit(solution)/shard_map/c_kv_0/ppermute | solution.py:125
  6.0 8.2 %collective-permute-start.1 = (bf16[1,1024,768]{2,1,0:T(8,128)(2,1)}, bf16[1,1024,768]{2,1,0:T(8,128)(2,1)S(1)}, u32[]{:S(2)}, u32[]{:S(2)}) collective-permute-start(bf16[1,1024,768]{2,1,0:T(8,128)(2,1)} %v.1), channel_id=1, source_target_pairs={{0,4},{8,12},{16,20},{24,28},{1,5},{9,13},{17,21},{25,29},{2,6},{1... | collective-permute-start | bytes 4718600 | tf_op jit(solution)/shard_map/core_style/ppermute | solution.py:379
  8.5 5.7 %collective-permute-start.2 = (bf16[1,1024,768]{2,1,0:T(8,128)(2,1)S(1)}, bf16[1,1024,768]{2,1,0:T(8,128)(2,1)S(1)}, u32[]{:S(2)}, u32[]{:S(2)}) collective-permute-start(bf16[1,1024,768]{2,1,0:T(8,128)(2,1)S(1)} %copy-done), channel_id=1, source_target_pairs={{4,0},{12,8},{20,16},{28,24},{5,1},{13,9},{21,17},{29,25},{6,2},{1... | collective-permute-start | bytes 4718600 | tf_op jit(solution)/shard_map/core_style/ppermute | solution.py:380
  12.5 1.8 %copy-start.1 = (bf16[1,1024,768]{2,1,0:T(8,128)(2,1)S(1)}, bf16[1,1024,768]{2,1,0:T(8,128)(2,1)}, u32[]{:S(2)}) copy-start(bf16[1,1024,768]{2,1,0:T(8,128)(2,1)} %v.1) | copy-start | bytes 4718596
  12.5 9.3 %collective-permute-start.6 = (bf16[224,768]{1,0:T(8,128)(2,1)S(1)}, bf16[224,768]{1,0:T(8,128)(2,1)S(1)}, u32[]{:S(2)}, u32[]{:S(2)}) collective-permute-start(bf16[224,768]{1,0:T(8,128)(2,1)S(1)} %collective-permute-done.3.rest_0_.rest_1_), channel_id=1, source_target_pairs={{0,16},{4,20},{8,24},{12,28},{16,0},{20,4},{24,8},{28,12},{1,17},{... | collective-permute-start | bytes 1032200 | tf_op jit(solution)/shard_map/xy_kv/ppermute | solution.py:125
  14.5 14.4 %copy-start.2 = (bf16[224,768]{1,0:T(8,128)(2,1)S(1)}, bf16[224,768]{1,0:T(8,128)(2,1)}, u32[]{:S(2)}) copy-start(bf16[224,768]{1,0:T(8,128)(2,1)} %q.1) | copy-start | bytes 1032196
  14.6 14.4 %copy-start.3 = (s32[1,8]{1,0:T(1,128)S(1)}, s32[1,8]{1,0:T(1,128)}, u32[]{:S(2)}) copy-start(s32[1,8]{1,0:T(1,128)} %lists.5) | copy-start | bytes 100
  14.6 12.1 %collective-permute-start.13 = (bf16[512,384]{1,0:T(8,128)(2,1)S(1)}, bf16[512,384]{1,0:T(8,128)(2,1)S(1)}, u32[]{:S(2)}, u32[]{:S(2)}) collective-permute-start(bf16[512,384]{1,0:T(8,128)(2,1)S(1)} %get-tuple-element.24), channel_id=1, source_target_pairs={{0,8},{4,12},{8,0},{12,4},{16,24},{20,28},{24,16},{28,20},{1,9},{5... | collective-permute-start | bytes 1179656 | tf_op jit(solution)/shard_map/x_style_0/ppermute | solution.py:125
  16.3 18.8 %collective-permute-start.5 = (bf16[512,384]{1,0:T(8,128)(2,1)S(1)}, bf16[512,384]{1,0:T(8,128)(2,1)S(1)}, u32[]{:S(2)}, u32[]{:S(2)}) collective-permute-start(bf16[512,384]{1,0:T(8,128)(2,1)S(1)} %shard_map.112), channel_id=1, source_target_pairs={{0,8},{4,12},{8,0},{12,4},{16,24},{20,28},{24,16},{28,20},{1,9},{5... | collective-permute-start | bytes 1179656 | tf_op jit(solution)/shard_map/x_style_1/ppermute | solution.py:125
  16.9 12.7 %collective-permute-start.7 = (bf16[224,768]{1,0:T(8,128)(2,1)S(1)}, bf16[224,768]{1,0:T(8,128)(2,1)S(1)}, u32[]{:S(2)}, u32[]{:S(2)}) collective-permute-start(bf16[224,768]{1,0:T(8,128)(2,1)S(1)} %collective-permute-done.3.rest_0_.rest_1_), channel_id=1, source_target_pairs={{0,4},{4,0},{8,12},{12,8},{16,20},{20,16},{24,28},{28,24},{1,5},{5... | collective-permute-start | bytes 1032200 | tf_op jit(solution)/shard_map/c_kv_1/ppermute | solution.py:125
  16.9 14.3 %collective-permute-start.8 = (bf16[224,768]{1,0:T(8,128)(2,1)S(1)}, bf16[224,768]{1,0:T(8,128)(2,1)S(1)}, u32[]{:S(2)}, u32[]{:S(2)}) collective-permute-start(bf16[224,768]{1,0:T(8,128)(2,1)S(1)} %collective-permute-done.after.rest_1_.rest_2_), channel_id=1, source_target_pairs={{0,4},{4,0},{8,12},{12,8},{16,20},{20,16},{24,28},{28,24},{1,5},{5... | collective-permute-start | bytes 1032200 | tf_op jit(solution)/shard_map/c_kv_2/ppermute | solution.py:125
  21.8 9.4 %collective-permute-start.9 = (bf16[224,768]{1,0:T(8,128)(2,1)S(1)}, bf16[224,768]{1,0:T(8,128)(2,1)S(1)}, u32[]{:S(2)}, u32[]{:S(2)}) collective-permute-start(bf16[224,768]{1,0:T(8,128)(2,1)S(1)} %collective-permute-done.6.rest_0_.rest_3_), channel_id=1, source_target_pairs={{0,4},{4,0},{8,12},{12,8},{16,20},{20,16},{24,28},{28,24},{1,5},{5... | collective-permute-start | bytes 1032200 | tf_op jit(solution)/shard_map/c_kv_3/ppermute | solution.py:125
  26.9 12.7 %collective-permute-start.14 = (bf16[512,384]{1,0:T(8,128)(2,1)S(1)}, bf16[512,384]{1,0:T(8,128)(2,1)S(1)}, u32[]{:S(2)}, u32[]{:S(2)}) collective-permute-start(bf16[512,384]{1,0:T(8,128)(2,1)S(1)} %shard_map.117.here), channel_id=1, source_target_pairs={{0,16},{4,20},{8,24},{12,28},{16,0},{20,4},{24,8},{28,12},{1,17},{... | collective-permute-start | bytes 1179656 | tf_op jit(solution)/shard_map/y_style_0/ppermute | solution.py:125
  29.7 10.3 %collective-permute-start.11 = (bf16[240,384]{1,0:T(8,128)(2,1)S(1)}, bf16[240,384]{1,0:T(8,128)(2,1)S(1)}, u32[]{:S(2)}, u32[]{:S(2)}) collective-permute-start(bf16[240,384]{1,0:T(8,128)(2,1)S(1)} %get-tuple-element.22), channel_id=1, source_target_pairs={{0,8},{4,12},{8,0},{12,4},{16,24},{20,28},{24,16},{28,20},{1,9},{5... | collective-permute-start | bytes 552968 | tf_op jit(solution)/shard_map/x_q/ppermute | solution.py:125
  35.3 8.5 %collective-permute-start.10 = (bf16[512,384]{1,0:T(8,128)(2,1)S(1)}, bf16[512,384]{1,0:T(8,128)(2,1)S(1)}, u32[]{:S(2)}, u32[]{:S(2)}) collective-permute-start(bf16[512,384]{1,0:T(8,128)(2,1)S(1)} %shard_map.113.here), channel_id=1, source_target_pairs={{0,16},{4,20},{8,24},{12,28},{16,0},{20,4},{24,8},{28,12},{1,17},{... | collective-permute-start | bytes 1179656 | tf_op jit(solution)/shard_map/y_style_1/ppermute | solution.py:125
  39.9 4.2 %collective-permute-start.15 = (bf16[512,384]{1,0:T(8,128)(2,1)S(1)}, bf16[512,384]{1,0:T(8,128)(2,1)S(1)}, u32[]{:S(2)}, u32[]{:S(2)}) collective-permute-start(bf16[512,384]{1,0:T(8,128)(2,1)S(1)} %shard_map.118.held), channel_id=1, source_target_pairs={{0,4},{4,0},{8,12},{12,8},{16,20},{20,16},{24,28},{28,24},{1,5},{5... | collective-permute-start | bytes 1179656 | tf_op jit(solution)/shard_map/c_style_0/ppermute | solution.py:125
  40.0 14.1 %slice-start = ((s8[4718592]{0:T(1024)(128)(4,1)}), s8[4194304]{0:T(1024)(128)(4,1)S(1)}, s32[]{:S(2)}) async-start(s8[4718592]{0:T(1024)(128)(4,1)} %bitcast), calls=%async_computation | async-start | bytes 8388608
  44.0 1.8 %collective-permute-start.12 = (bf16[512,384]{1,0:T(8,128)(2,1)S(1)}, bf16[512,384]{1,0:T(8,128)(2,1)S(1)}, u32[]{:S(2)}, u32[]{:S(2)}) collective-permute-start(bf16[512,384]{1,0:T(8,128)(2,1)S(1)} %shard_map.116.held), channel_id=1, source_target_pairs={{0,4},{4,0},{8,12},{12,8},{16,20},{20,16},{24,28},{28,24},{1,5},{5... | collective-permute-start | bytes 1179656 | tf_op jit(solution)/shard_map/c_style_1/ppermute | solution.py:125
  44.1 10.0 %slice-start.1 = ((s8[4718592]{0:T(1024)(128)(4,1)}), s8[524288]{0:T(1024)(128)(4,1)S(1)}, s32[]{:S(2)}) async-start(s8[4718592]{0:T(1024)(128)(4,1)} %bitcast), calls=%async_computation.1 | async-start | bytes 1048576
  47.4 6.6 %collective-permute-start.16 = (bf16[224,384]{1,0:T(8,128)(2,1)S(1)}, bf16[224,384]{1,0:T(8,128)(2,1)S(1)}, u32[]{:S(2)}, u32[]{:S(2)}) collective-permute-start(bf16[224,384]{1,0:T(8,128)(2,1)S(1)} %shard_map.122), channel_id=1, source_target_pairs={{0,8},{4,12},{8,0},{12,4},{16,24},{20,28},{24,16},{28,20},{1,9},{5... | collective-permute-start | bytes 516104 | tf_op jit(solution)/shard_map/x_back/ppermute | solution.py:125
  54.6 11.1 %collective-permute-start.18 = (bf16[224,768]{1,0:T(8,128)(2,1)S(1)}, bf16[224,768]{1,0:T(8,128)(2,1)S(1)}, u32[]{:S(2)}, u32[]{:S(2)}) collective-permute-start(bf16[224,768]{1,0:T(8,128)(2,1)S(1)} %shard_map.125), channel_id=1, source_target_pairs={{0,1},{1,0},{2,3},{3,2},{4,5},{5,4},{6,7},{7,6},{8,9},{9,8},{10,11... | collective-permute-start | bytes 1032200 | tf_op jit(solution)/shard_map/z_relay/ppermute | solution.py:125
  56.7 21.2 %collective-permute-start.17 = (bf16[224,768]{1,0:T(8,128)(2,1)S(1)}, bf16[224,768]{1,0:T(8,128)(2,1)S(1)}, u32[]{:S(2)}, u32[]{:S(2)}) collective-permute-start(bf16[224,768]{1,0:T(8,128)(2,1)S(1)} %shard_map.124), channel_id=1, source_target_pairs={{0,1},{1,0},{2,3},{3,2},{4,5},{5,4},{6,7},{7,6},{8,9},{9,8},{10,11... | collective-permute-start | bytes 1032200 | tf_op jit(solution)/shard_map/z_near/ppermute | solution.py:125
  66.2 15.6 %copy-start.4 = (bf16[224,768]{1,0:T(8,128)(2,1)S(1)}, bf16[224,768]{1,0:T(8,128)(2,1)}, u32[]{:S(2)}) copy-start(bf16[224,768]{1,0:T(8,128)(2,1)} %param.20) | copy-start | bytes 1032196
  66.2 15.6 %copy-start.5 = (f32[768]{0:T(1024)S(1)}, f32[768]{0:T(1024)}, u32[]{:S(2)}) copy-start(f32[768]{0:T(1024)} %param.21) | copy-start | bytes 9220
  66.2 15.6 %collective-permute-start.19 = (bf16[224,768]{1,0:T(8,128)(2,1)S(1)}, bf16[224,768]{1,0:T(8,128)(2,1)S(1)}, u32[]{:S(2)}, u32[]{:S(2)}) collective-permute-start(bf16[224,768]{1,0:T(8,128)(2,1)S(1)} %shard_map.126), channel_id=1, source_target_pairs={{0,2},{1,3},{2,0},{3,1},{4,6},{5,7},{6,4},{7,5},{8,10},{9,11},{10,... | collective-permute-start | bytes 1032200 | tf_op jit(solution)/shard_map/z_far/ppermute | solution.py:125

commit v5 on v4

--- a/solution.py
+++ b/solution.py
@@ -325,6 +325,11 @@
     out[...] = share.astype(out.dtype)
 
 
+def base_kernel(own, near, residual, gate, out):
+    summed = own[...] + near[...].astype(jnp.float32)
+    out[...] = residual[...].astype(jnp.float32) + gate[...] * summed
+
+
 SMEM = pl.BlockSpec(memory_space=pltpu.SMEM)
 VMEM = pl.BlockSpec(memory_space=pltpu.VMEM)
 ANY = pl.BlockSpec(memory_space=pl.ANY)
@@ -473,8 +478,11 @@
     relay = swap(project(3, bf16), "head", 1, "z_relay")
     near_share = swap(project(1, bf16), "head", 1, "z_near")
     far_share = swap(project(2, bf16, relay), "head", 2, "z_far")
-    projected = project(0, f32) + near_share.astype(f32) + far_share.astype(f32)
-    return (residual.astype(f32) + gate_scale[None, :] * projected).astype(bf16)
+    gate = gate_scale[None, :]
+    (base,) = call(
+        base_kernel, [VMEM] * 4, [((rows, columns), f32)]
+    )(project(0, f32), near_share, residual, gate)
+    return (base + gate * far_share.astype(f32)).astype(bf16)
 
 
 def solution(mesh):

time: 82.9 us -> 82.7 us (level)
  no operation moved by 1% of the time
where the time goes in v5:
time: 82.7 us; the launch traced here: 82.6 us
  waiting for transfers between devices  39.4 us (48%)
  starting transfers between devices  23 us (28%)
  Pallas kernels  16.2 us (20%)
  other arithmetic  2.24 us (3%)
  between operations  1.62 us (2%)
    ppermute x18, waiting for transfers between devices, swap(): lax.ppermute(block, axis, [(i, i ^ bit) for i in range(lax.axis_size(axis...  39.4 us
    ppermute x18, starting transfers between devices, swap(): lax.ppermute(block, axis, [(i, i ^ bit) for i in range(lax.axis_size(axis...  19.2 us
    pallas_call x2, Pallas kernels, frames_of(): call(functools.partial(frames_kernel, remote), [SMEM, SMEM] + [VMEM] * 9,...  6.04 us
    pallas_call x4, Pallas kernels, style_of(): call(functools.partial(style_kernel, last), [VMEM] * 5, [((rows, width),...  6 us
    ppermute x1, starting transfers between devices, paired_device(): from_even = lax.ppermute(ref_values, 'frame', even)  2.5 us
    pallas_call x4, Pallas kernels, project(): call(functools.partial(project_kernel, bit), [VMEM] * (3 + len(came)), [(...  2.08 us
  transfers between devices with their start and end apart: 20, of which 10 were waited for; matrix products, arithmetic and copies ran while one was open for 0% of the time, Pallas kernels for 17%

profile of v5, /device:TPU:0, one launch (start us, length us, event | category | flops | bytes accessed | tf_op | source)
XLA Modules:
  0.0 82.6 jit_solution(3526231822498012688)
XLA Ops:
  0.0 1.4 %broadcast_select_fusion = (bf16[224,384]{1,0:T(8,128)(2,1)S(1)}, bf16[224,384]{1,0:T(8,128)(2,1)S(1)}, bf16[224,384]{1,0:T(8,128)(2,1)S(1)}, bf16[224,384]{1,0:T(8,128)(2,1)S(1)}) fusion(pred[]{:T(512)S(6)} %not.3, bf16[224,768]{1,0:T(8,128)(2,1)} %param.13, pred[]{:T(512)S(6)} %eq.5, bf16[224,768]{1,0:T(8,128)(2,1)} %param.12), kind=kLoop, calls=%fused_computation.3 | loop fusion | flops 344064 | bytes 1376258 | tf_op jit(solution)/shard_map/jit(_where)/select_n | solution.py:390
  1.4 3.0 %collective-permute-start.3 = (bf16[224,768]{1,0:T(8,128)(2,1)S(1)}, bf16[224,768]{1,0:T(8,128)(2,1)S(1)}, u32[]{:S(2)}, u32[]{:S(2)}) collective-permute-start(bf16[224,768]{1,0:T(8,128)(2,1)S(1)} %pad_maximum_fusion.1), channel_id=1, source_target_pairs={{0,8},{4,12},{8,0},{12,4},{16,24},{20,28},{24,16},{28,20},{1,9},{5... | collective-permute-start | bytes 1032200 | tf_op jit(solution)/shard_map/x_kv/ppermute | solution.py:125
  4.4 1.6 %collective-permute-start = (bf16[224,768]{1,0:T(8,128)(2,1)S(1)}, bf16[224,768]{1,0:T(8,128)(2,1)S(1)}, u32[]{:S(2)}, u32[]{:S(2)}) collective-permute-start(bf16[224,768]{1,0:T(8,128)(2,1)S(1)} %pad_maximum_fusion.rest_0_), channel_id=1, source_target_pairs={{0,16},{4,20},{8,24},{12,28},{16,0},{20,4},{24,8},{28,12},{1,17},{... | collective-permute-start | bytes 1032200 | tf_op jit(solution)/shard_map/y_kv/ppermute | solution.py:125
  6.0 2.5 %collective-permute-start.1 = (bf16[1,1024,768]{2,1,0:T(8,128)(2,1)}, bf16[1,1024,768]{2,1,0:T(8,128)(2,1)S(1)}, u32[]{:S(2)}, u32[]{:S(2)}) collective-permute-start(bf16[1,1024,768]{2,1,0:T(8,128)(2,1)} %v.1), channel_id=1, source_target_pairs={{0,4},{8,12},{16,20},{24,28},{1,5},{9,13},{17,21},{25,29},{2,6},{1... | collective-permute-start | bytes 4718600 | tf_op jit(solution)/shard_map/core_style/ppermute | solution.py:384
  8.5 1.3 %collective-permute-start.2 = (bf16[1,1024,768]{2,1,0:T(8,128)(2,1)S(1)}, bf16[1,1024,768]{2,1,0:T(8,128)(2,1)S(1)}, u32[]{:S(2)}, u32[]{:S(2)}) collective-permute-start(bf16[1,1024,768]{2,1,0:T(8,128)(2,1)S(1)} %copy-done), channel_id=1, source_target_pairs={{4,0},{12,8},{20,16},{28,24},{5,1},{13,9},{21,17},{29,25},{6,2},{1... | collective-permute-start | bytes 4718600 | tf_op jit(solution)/shard_map/core_style/ppermute | solution.py:385
  10.5 2.0 %collective-permute-done.3.rest_0_.rest_1_ = bf16[224,768]{1,0:T(8,128)(2,1)S(1)} collective-permute-done((bf16[224,768]{1,0:T(8,128)(2,1)S(1)}, bf16[224,768]{1,0:T(8,128)(2,1)S(1)}, u32[]{:S(2)}, u32[]{:S(2)}) %collective-permute-start.3) | collective-permute-done | bytes 344096 | tf_op jit(solution)/shard_map/x_kv/ppermute | solution.py:125
  12.5 1.8 %collective-permute-start.6 = (bf16[224,768]{1,0:T(8,128)(2,1)S(1)}, bf16[224,768]{1,0:T(8,128)(2,1)S(1)}, u32[]{:S(2)}, u32[]{:S(2)}) collective-permute-start(bf16[224,768]{1,0:T(8,128)(2,1)S(1)} %collective-permute-done.3.rest_0_.rest_1_), channel_id=1, source_target_pairs={{0,16},{4,20},{8,24},{12,28},{16,0},{20,4},{24,8},{28,12},{1,17},{... | collective-permute-start | bytes 1032200 | tf_op jit(solution)/shard_map/xy_kv/ppermute | solution.py:125
  14.3 0.2 shard_map.111
  14.6 1.6 %collective-permute-start.13 = (bf16[512,384]{1,0:T(8,128)(2,1)S(1)}, bf16[512,384]{1,0:T(8,128)(2,1)S(1)}, u32[]{:S(2)}, u32[]{:S(2)}) collective-permute-start(bf16[512,384]{1,0:T(8,128)(2,1)S(1)} %get-tuple-element.24), channel_id=1, source_target_pairs={{0,8},{4,12},{8,0},{12,4},{16,24},{20,28},{24,16},{28,20},{1,9},{5... | collective-permute-start | bytes 1179656 | tf_op jit(solution)/shard_map/x_style_0/ppermute | solution.py:125
  16.1 0.2 shard_map.112
  16.3 0.6 collective-permute-start.5
  16.9 0.5 collective-permute-start.8
  17.4 4.3 %collective-permute-done.6.rest_0_.rest_3_ = bf16[224,768]{1,0:T(8,128)(2,1)S(1)} collective-permute-done((bf16[224,768]{1,0:T(8,128)(2,1)S(1)}, bf16[224,768]{1,0:T(8,128)(2,1)S(1)}, u32[]{:S(2)}, u32[]{:S(2)}) %collective-permute-start.6) | collective-permute-done | bytes 344096 | tf_op jit(solution)/shard_map/xy_kv/ppermute | solution.py:125
  21.8 4.9 %collective-permute-done.13.came = bf16[512,384]{1,0:T(8,128)(2,1)S(1)} collective-permute-done((bf16[512,384]{1,0:T(8,128)(2,1)S(1)}, bf16[512,384]{1,0:T(8,128)(2,1)S(1)}, u32[]{:S(2)}, u32[]{:S(2)}) %collective-permute-start.13) | collective-permute-done | bytes 393248 | tf_op jit(solution)/shard_map/x_style_0/ppermute | solution.py:125
  26.7 0.2 shard_map.117.here
  26.9 1.4 %collective-permute-start.14 = (bf16[512,384]{1,0:T(8,128)(2,1)S(1)}, bf16[512,384]{1,0:T(8,128)(2,1)S(1)}, u32[]{:S(2)}, u32[]{:S(2)}) collective-permute-start(bf16[512,384]{1,0:T(8,128)(2,1)S(1)} %shard_map.117.here), channel_id=1, source_target_pairs={{0,16},{4,20},{8,24},{12,28},{16,0},{20,4},{24,8},{28,12},{1,17},{... | collective-permute-start | bytes 1179656 | tf_op jit(solution)/shard_map/y_style_0/ppermute | solution.py:125
  28.9 0.7 shard_map.109
  29.7 1.6 %collective-permute-start.11 = (bf16[240,384]{1,0:T(8,128)(2,1)S(1)}, bf16[240,384]{1,0:T(8,128)(2,1)S(1)}, u32[]{:S(2)}, u32[]{:S(2)}) collective-permute-start(bf16[240,384]{1,0:T(8,128)(2,1)S(1)} %get-tuple-element.22), channel_id=1, source_target_pairs={{0,8},{4,12},{8,0},{12,4},{16,24},{20,28},{24,16},{28,20},{1,9},{5... | collective-permute-start | bytes 552968 | tf_op jit(solution)/shard_map/x_q/ppermute | solution.py:125
  31.2 3.9 %collective-permute-done.5.came = bf16[512,384]{1,0:T(8,128)(2,1)S(1)} collective-permute-done((bf16[512,384]{1,0:T(8,128)(2,1)S(1)}, bf16[512,384]{1,0:T(8,128)(2,1)S(1)}, u32[]{:S(2)}, u32[]{:S(2)}) %collective-permute-start.5) | collective-permute-done | bytes 393248 | tf_op jit(solution)/shard_map/x_style_1/ppermute | solution.py:125
  35.1 0.2 shard_map.113.here
  35.3 1.3 %collective-permute-start.10 = (bf16[512,384]{1,0:T(8,128)(2,1)S(1)}, bf16[512,384]{1,0:T(8,128)(2,1)S(1)}, u32[]{:S(2)}, u32[]{:S(2)}) collective-permute-start(bf16[512,384]{1,0:T(8,128)(2,1)S(1)} %shard_map.113.here), channel_id=1, source_target_pairs={{0,16},{4,20},{8,24},{12,28},{16,0},{20,4},{24,8},{28,12},{1,17},{... | collective-permute-start | bytes 1179656 | tf_op jit(solution)/shard_map/y_style_1/ppermute | solution.py:125
  36.6 3.0 %shard_map.114 = (f32[224,384]{1,0:T(8,128)S(1)}, f32[224,128]{1,0:T(8,128)S(1)}) custom-call(s32[1,8]{1,0:T(1,128)S(1)} %copy-done.4, s32[1]{0:T(128)S(6)} %copy.12.counts, bf16[224,384]{1,0:T(8,128)(2,1)S(1)} %get-tuple-element.18.q, bf16[224,768]{1,0:T(8,128)(2,1)S(1)} %pad_maximum_fusion.rest_0_, ...), custom_call_target="tpu_custom_call" | custom-call | flops 3000000000 | bytes 1 | tf_op jit(solution)/shard_map/pallas_call | solution.py:435
  39.6 0.2 shard_map.118.held
  39.9 0.1 collective-permute-start.15
  40.0 3.0 %shard_map.115 = (f32[224,384]{1,0:T(8,128)S(1)}, f32[224,128]{1,0:T(8,128)S(1)}) custom-call(s32[1,8]{1,0:T(1,128)S(1)} %copy-done.4, s32[1]{0:T(128)S(6)} %copy.12.counts, bf16[240,384]{1,0:T(8,128)(2,1)S(1)} %collective-permute-done.11.q, bf16[224,768]{1,0:T(8,128)(2,1)S(1)} %pad_maximum_fusion.rest_0_, ...), custom_call_target="tpu_custom_call" | custom-call | flops 3000000000 | bytes 1 | tf_op jit(solution)/shard_map/pallas_call | solution.py:435
  43.0 0.8 collective-permute-done.10.came
  43.8 0.2 shard_map.116.held
  44.0 0.1 collective-permute-start.12
  44.1 0.0 slice-start.1
  44.1 1.4 %shard_map.121 = (f32[224,384]{1,0:T(8,128)S(1)}, f32[224,128]{1,0:T(8,128)S(1)}) custom-call(bf16[240,384]{1,0:T(8,128)(2,1)S(1)} %collective-permute-done.11.q, bf16[512,384]{1,0:T(8,128)(2,1)S(1)} %shard_map.118.held, bf16[512,384]{1,0:T(8,128)(2,1)S(1)} %collective-permute-done.15.swapped, f32[224,384]{1,0:T(8,128)S(1)} %get-tuple-element.28.acc_in, ...), custom_call_target="tpu_custom_call" | custom-call | flops 1000000000 | bytes 1 | tf_op jit(solution)/shard_map/pallas_call | solution.py:453
  45.5 0.2 collective-permute-done.12.swapped
  45.8 1.7 %shard_map.122 = bf16[224,384]{1,0:T(8,128)(2,1)S(1)} custom-call(bf16[240,384]{1,0:T(8,128)(2,1)S(1)} %collective-permute-done.11.q, bf16[512,384]{1,0:T(8,128)(2,1)S(1)} %shard_map.116.held, bf16[512,384]{1,0:T(8,128)(2,1)S(1)} %collective-permute-done.12.swapped, f32[224,384]{1,0:T(8,128)S(1)} %get-tuple-element.29.acc_in, ...), custom_call_target="tpu_custom_call" | custom-call | flops 1000000000 | bytes 1 | tf_op jit(solution)/shard_map/pallas_call | solution.py:453
  47.4 1.0 %collective-permute-start.16 = (bf16[224,384]{1,0:T(8,128)(2,1)S(1)}, bf16[224,384]{1,0:T(8,128)(2,1)S(1)}, u32[]{:S(2)}, u32[]{:S(2)}) collective-permute-start(bf16[224,384]{1,0:T(8,128)(2,1)S(1)} %shard_map.122), channel_id=1, source_target_pairs={{0,8},{4,12},{8,0},{12,4},{16,24},{20,28},{24,16},{28,20},{1,9},{5... | collective-permute-start | bytes 516104 | tf_op jit(solution)/shard_map/x_back/ppermute | solution.py:125
  48.5 1.4 %shard_map.119 = (f32[224,384]{1,0:T(8,128)S(1)}, f32[224,128]{1,0:T(8,128)S(1)}) custom-call(bf16[224,384]{1,0:T(8,128)(2,1)S(1)} %get-tuple-element.18.q, bf16[512,384]{1,0:T(8,128)(2,1)S(1)} %shard_map.118.held, bf16[512,384]{1,0:T(8,128)(2,1)S(1)} %collective-permute-done.15.swapped, f32[224,384]{1,0:T(8,128)S(1)} %get-tuple-element.25.acc_in, ...), custom_call_target="tpu_custom_call" | custom-call | flops 1000000000 | bytes 1 | tf_op jit(solution)/shard_map/pallas_call | solution.py:453
  49.9 1.5 %shard_map.120.own = bf16[224,384]{1,0:T(8,128)(2,1)S(1)} custom-call(bf16[224,384]{1,0:T(8,128)(2,1)S(1)} %get-tuple-element.18.q, bf16[512,384]{1,0:T(8,128)(2,1)S(1)} %shard_map.116.held, bf16[512,384]{1,0:T(8,128)(2,1)S(1)} %collective-permute-done.12.swapped, f32[224,384]{1,0:T(8,128)S(1)} %get-tuple-element.26.acc_in, ...), custom_call_target="tpu_custom_call" | custom-call | flops 1000000000 | bytes 1 | tf_op jit(solution)/shard_map/pallas_call | solution.py:453
  51.4 2.6 %collective-permute-done.16.got = bf16[224,384]{1,0:T(8,128)(2,1)S(1)} collective-permute-done((bf16[224,384]{1,0:T(8,128)(2,1)S(1)}, bf16[224,384]{1,0:T(8,128)(2,1)S(1)}, u32[]{:S(2)}, u32[]{:S(2)}) %collective-permute-start.16) | collective-permute-done | bytes 172064 | tf_op jit(solution)/shard_map/x_back/ppermute | solution.py:125
  54.0 0.5 shard_map.126
  54.6 1.6 %collective-permute-start.18 = (bf16[224,768]{1,0:T(8,128)(2,1)S(1)}, bf16[224,768]{1,0:T(8,128)(2,1)S(1)}, u32[]{:S(2)}, u32[]{:S(2)}) collective-permute-start(bf16[224,768]{1,0:T(8,128)(2,1)S(1)} %shard_map.126), channel_id=1, source_target_pairs={{0,1},{1,0},{2,3},{3,2},{4,5},{5,4},{6,7},{7,6},{8,9},{9,8},{10,11... | collective-permute-start | bytes 1032200 | tf_op jit(solution)/shard_map/z_relay/ppermute | solution.py:125
  56.2 0.5 shard_map.124
  56.7 0.5 collective-permute-start.17
  57.2 8.4 %collective-permute-done.18.rest_0_ = bf16[224,768]{1,0:T(8,128)(2,1)S(1)} collective-permute-done((bf16[224,768]{1,0:T(8,128)(2,1)S(1)}, bf16[224,768]{1,0:T(8,128)(2,1)S(1)}, u32[]{:S(2)}, u32[]{:S(2)}) %collective-permute-start.18) | collective-permute-done | bytes 344096 | tf_op jit(solution)/shard_map/z_relay/ppermute | solution.py:125
  65.6 0.5 shard_map.127
  66.1 2.7 %collective-permute-start.19 = (bf16[224,768]{1,0:T(8,128)(2,1)S(1)}, bf16[224,768]{1,0:T(8,128)(2,1)S(1)}, u32[]{:S(2)}, u32[]{:S(2)}) collective-permute-start(bf16[224,768]{1,0:T(8,128)(2,1)S(1)} %shard_map.127), channel_id=1, source_target_pairs={{0,2},{1,3},{2,0},{3,1},{4,6},{5,7},{6,4},{7,5},{8,10},{9,11},{10,... | collective-permute-start | bytes 1032200 | tf_op jit(solution)/shard_map/z_far/ppermute | solution.py:125
  68.8 0.5 shard_map.123.own
  69.3 8.6 %collective-permute-done.17.near = bf16[224,768]{1,0:T(8,128)(2,1)S(1)} collective-permute-done((bf16[224,768]{1,0:T(8,128)(2,1)S(1)}, bf16[224,768]{1,0:T(8,128)(2,1)S(1)}, u32[]{:S(2)}, u32[]{:S(2)}) %collective-permute-start.17) | collective-permute-done | bytes 344096 | tf_op jit(solution)/shard_map/z_near/ppermute | solution.py:125
  77.9 0.1 shard_map.125
  78.1 3.6 %collective-permute-done.19 = bf16[224,768]{1,0:T(8,128)(2,1)S(1)} collective-permute-done((bf16[224,768]{1,0:T(8,128)(2,1)S(1)}, bf16[224,768]{1,0:T(8,128)(2,1)S(1)}, u32[]{:S(2)}, u32[]{:S(2)}) %collective-permute-start.19) | collective-permute-done | bytes 344096 | tf_op jit(solution)/shard_map/z_far/ppermute | solution.py:125
  81.7 0.8 add_convert_fusion
  (34 shorter events, 0.2 us)
Async XLA Ops:
  0.0 8.5 %copy-start = (bf16[1,1024,768]{2,1,0:T(8,128)(2,1)S(1)}, bf16[1,1024,768]{2,1,0:T(8,128)(2,1)}, u32[]{:S(2)}) copy-start(bf16[1,1024,768]{2,1,0:T(8,128)(2,1)} %k.1) | copy-start | bytes 4718596
  1.4 11.1 %collective-permute-start.3 = (bf16[224,768]{1,0:T(8,128)(2,1)S(1)}, bf16[224,768]{1,0:T(8,128)(2,1)S(1)}, u32[]{:S(2)}, u32[]{:S(2)}) collective-permute-start(bf16[224,768]{1,0:T(8,128)(2,1)S(1)} %pad_maximum_fusion.1), channel_id=1, source_target_pairs={{0,8},{4,12},{8,0},{12,4},{16,24},{20,28},{24,16},{28,20},{1,9},{5... | collective-permute-start | bytes 1032200 | tf_op jit(solution)/shard_map/x_kv/ppermute | solution.py:125
  4.4 9.8 %collective-permute-start = (bf16[224,768]{1,0:T(8,128)(2,1)S(1)}, bf16[224,768]{1,0:T(8,128)(2,1)S(1)}, u32[]{:S(2)}, u32[]{:S(2)}) collective-permute-start(bf16[224,768]{1,0:T(8,128)(2,1)S(1)} %pad_maximum_fusion.rest_0_), channel_id=1, source_target_pairs={{0,16},{4,20},{8,24},{12,28},{16,0},{20,4},{24,8},{28,12},{1,17},{... | collective-permute-start | bytes 1032200 | tf_op jit(solution)/shard_map/y_kv/ppermute | solution.py:125
  6.0 10.1 %collective-permute-start.4 = (bf16[224,768]{1,0:T(8,128)(2,1)S(1)}, bf16[224,768]{1,0:T(8,128)(2,1)S(1)}, u32[]{:S(2)}, u32[]{:S(2)}) collective-permute-start(bf16[224,768]{1,0:T(8,128)(2,1)S(1)} %pad_maximum_fusion.rest_0_), channel_id=1, source_target_pairs={{0,4},{4,0},{8,12},{12,8},{16,20},{20,16},{24,28},{28,24},{1,5},{5... | collective-permute-start | bytes 1032200 | tf_op jit(solution)/shard_map/c_kv_0/ppermute | solution.py:125
  6.0 8.2 %collective-permute-start.1 = (bf16[1,1024,768]{2,1,0:T(8,128)(2,1)}, bf16[1,1024,768]{2,1,0:T(8,128)(2,1)S(1)}, u32[]{:S(2)}, u32[]{:S(2)}) collective-permute-start(bf16[1,1024,768]{2,1,0:T(8,128)(2,1)} %v.1), channel_id=1, source_target_pairs={{0,4},{8,12},{16,20},{24,28},{1,5},{9,13},{17,21},{25,29},{2,6},{1... | collective-permute-start | bytes 4718600 | tf_op jit(solution)/shard_map/core_style/ppermute | solution.py:384
  8.5 5.7 %collective-permute-start.2 = (bf16[1,1024,768]{2,1,0:T(8,128)(2,1)S(1)}, bf16[1,1024,768]{2,1,0:T(8,128)(2,1)S(1)}, u32[]{:S(2)}, u32[]{:S(2)}) collective-permute-start(bf16[1,1024,768]{2,1,0:T(8,128)(2,1)S(1)} %copy-done), channel_id=1, source_target_pairs={{4,0},{12,8},{20,16},{28,24},{5,1},{13,9},{21,17},{29,25},{6,2},{1... | collective-permute-start | bytes 4718600 | tf_op jit(solution)/shard_map/core_style/ppermute | solution.py:385
  12.5 1.8 %copy-start.1 = (bf16[1,1024,768]{2,1,0:T(8,128)(2,1)S(1)}, bf16[1,1024,768]{2,1,0:T(8,128)(2,1)}, u32[]{:S(2)}) copy-start(bf16[1,1024,768]{2,1,0:T(8,128)(2,1)} %v.1) | copy-start | bytes 4718596
  12.5 9.3 %collective-permute-start.6 = (bf16[224,768]{1,0:T(8,128)(2,1)S(1)}, bf16[224,768]{1,0:T(8,128)(2,1)S(1)}, u32[]{:S(2)}, u32[]{:S(2)}) collective-permute-start(bf16[224,768]{1,0:T(8,128)(2,1)S(1)} %collective-permute-done.3.rest_0_.rest_1_), channel_id=1, source_target_pairs={{0,16},{4,20},{8,24},{12,28},{16,0},{20,4},{24,8},{28,12},{1,17},{... | collective-permute-start | bytes 1032200 | tf_op jit(solution)/shard_map/xy_kv/ppermute | solution.py:125
  14.5 14.4 %copy-start.2 = (bf16[224,768]{1,0:T(8,128)(2,1)S(1)}, bf16[224,768]{1,0:T(8,128)(2,1)}, u32[]{:S(2)}) copy-start(bf16[224,768]{1,0:T(8,128)(2,1)} %q.1) | copy-start | bytes 1032196
  14.6 14.4 %copy-start.4 = (s32[1,8]{1,0:T(1,128)S(1)}, s32[1,8]{1,0:T(1,128)}, u32[]{:S(2)}) copy-start(s32[1,8]{1,0:T(1,128)} %lists.5) | copy-start | bytes 100
  14.6 12.1 %collective-permute-start.13 = (bf16[512,384]{1,0:T(8,128)(2,1)S(1)}, bf16[512,384]{1,0:T(8,128)(2,1)S(1)}, u32[]{:S(2)}, u32[]{:S(2)}) collective-permute-start(bf16[512,384]{1,0:T(8,128)(2,1)S(1)} %get-tuple-element.24), channel_id=1, source_target_pairs={{0,8},{4,12},{8,0},{12,4},{16,24},{20,28},{24,16},{28,20},{1,9},{5... | collective-permute-start | bytes 1179656 | tf_op jit(solution)/shard_map/x_style_0/ppermute | solution.py:125
  16.3 18.8 %collective-permute-start.5 = (bf16[512,384]{1,0:T(8,128)(2,1)S(1)}, bf16[512,384]{1,0:T(8,128)(2,1)S(1)}, u32[]{:S(2)}, u32[]{:S(2)}) collective-permute-start(bf16[512,384]{1,0:T(8,128)(2,1)S(1)} %shard_map.112), channel_id=1, source_target_pairs={{0,8},{4,12},{8,0},{12,4},{16,24},{20,28},{24,16},{28,20},{1,9},{5... | collective-permute-start | bytes 1179656 | tf_op jit(solution)/shard_map/x_style_1/ppermute | solution.py:125
  16.9 12.7 %collective-permute-start.7 = (bf16[224,768]{1,0:T(8,128)(2,1)S(1)}, bf16[224,768]{1,0:T(8,128)(2,1)S(1)}, u32[]{:S(2)}, u32[]{:S(2)}) collective-permute-start(bf16[224,768]{1,0:T(8,128)(2,1)S(1)} %collective-permute-done.3.rest_0_.rest_1_), channel_id=1, source_target_pairs={{0,4},{4,0},{8,12},{12,8},{16,20},{20,16},{24,28},{28,24},{1,5},{5... | collective-permute-start | bytes 1032200 | tf_op jit(solution)/shard_map/c_kv_1/ppermute | solution.py:125
  16.9 14.3 %collective-permute-start.8 = (bf16[224,768]{1,0:T(8,128)(2,1)S(1)}, bf16[224,768]{1,0:T(8,128)(2,1)S(1)}, u32[]{:S(2)}, u32[]{:S(2)}) collective-permute-start(bf16[224,768]{1,0:T(8,128)(2,1)S(1)} %collective-permute-done.after.rest_1_.rest_2_), channel_id=1, source_target_pairs={{0,4},{4,0},{8,12},{12,8},{16,20},{20,16},{24,28},{28,24},{1,5},{5... | collective-permute-start | bytes 1032200 | tf_op jit(solution)/shard_map/c_kv_2/ppermute | solution.py:125
  21.8 9.4 %collective-permute-start.9 = (bf16[224,768]{1,0:T(8,128)(2,1)S(1)}, bf16[224,768]{1,0:T(8,128)(2,1)S(1)}, u32[]{:S(2)}, u32[]{:S(2)}) collective-permute-start(bf16[224,768]{1,0:T(8,128)(2,1)S(1)} %collective-permute-done.6.rest_0_.rest_3_), channel_id=1, source_target_pairs={{0,4},{4,0},{8,12},{12,8},{16,20},{20,16},{24,28},{28,24},{1,5},{5... | collective-permute-start | bytes 1032200 | tf_op jit(solution)/shard_map/c_kv_3/ppermute | solution.py:125
  26.9 12.7 %collective-permute-start.14 = (bf16[512,384]{1,0:T(8,128)(2,1)S(1)}, bf16[512,384]{1,0:T(8,128)(2,1)S(1)}, u32[]{:S(2)}, u32[]{:S(2)}) collective-permute-start(bf16[512,384]{1,0:T(8,128)(2,1)S(1)} %shard_map.117.here), channel_id=1, source_target_pairs={{0,16},{4,20},{8,24},{12,28},{16,0},{20,4},{24,8},{28,12},{1,17},{... | collective-permute-start | bytes 1179656 | tf_op jit(solution)/shard_map/y_style_0/ppermute | solution.py:125
  29.7 10.3 %collective-permute-start.11 = (bf16[240,384]{1,0:T(8,128)(2,1)S(1)}, bf16[240,384]{1,0:T(8,128)(2,1)S(1)}, u32[]{:S(2)}, u32[]{:S(2)}) collective-permute-start(bf16[240,384]{1,0:T(8,128)(2,1)S(1)} %get-tuple-element.22), channel_id=1, source_target_pairs={{0,8},{4,12},{8,0},{12,4},{16,24},{20,28},{24,16},{28,20},{1,9},{5... | collective-permute-start | bytes 552968 | tf_op jit(solution)/shard_map/x_q/ppermute | solution.py:125
  35.3 8.5 %collective-permute-start.10 = (bf16[512,384]{1,0:T(8,128)(2,1)S(1)}, bf16[512,384]{1,0:T(8,128)(2,1)S(1)}, u32[]{:S(2)}, u32[]{:S(2)}) collective-permute-start(bf16[512,384]{1,0:T(8,128)(2,1)S(1)} %shard_map.113.here), channel_id=1, source_target_pairs={{0,16},{4,20},{8,24},{12,28},{16,0},{20,4},{24,8},{28,12},{1,17},{... | collective-permute-start | bytes 1179656 | tf_op jit(solution)/shard_map/y_style_1/ppermute | solution.py:125
  39.9 4.2 %collective-permute-start.15 = (bf16[512,384]{1,0:T(8,128)(2,1)S(1)}, bf16[512,384]{1,0:T(8,128)(2,1)S(1)}, u32[]{:S(2)}, u32[]{:S(2)}) collective-permute-start(bf16[512,384]{1,0:T(8,128)(2,1)S(1)} %shard_map.118.held), channel_id=1, source_target_pairs={{0,4},{4,0},{8,12},{12,8},{16,20},{20,16},{24,28},{28,24},{1,5},{5... | collective-permute-start | bytes 1179656 | tf_op jit(solution)/shard_map/c_style_0/ppermute | solution.py:125
  40.0 14.1 %slice-start = ((s8[4718592]{0:T(1024)(128)(4,1)}), s8[4194304]{0:T(1024)(128)(4,1)S(1)}, s32[]{:S(2)}) async-start(s8[4718592]{0:T(1024)(128)(4,1)} %bitcast), calls=%async_computation | async-start | bytes 8388608
  44.0 1.8 %collective-permute-start.12 = (bf16[512,384]{1,0:T(8,128)(2,1)S(1)}, bf16[512,384]{1,0:T(8,128)(2,1)S(1)}, u32[]{:S(2)}, u32[]{:S(2)}) collective-permute-start(bf16[512,384]{1,0:T(8,128)(2,1)S(1)} %shard_map.116.held), channel_id=1, source_target_pairs={{0,4},{4,0},{8,12},{12,8},{16,20},{20,16},{24,28},{28,24},{1,5},{5... | collective-permute-start | bytes 1179656 | tf_op jit(solution)/shard_map/c_style_1/ppermute | solution.py:125
  44.1 10.0 %slice-start.1 = ((s8[4718592]{0:T(1024)(128)(4,1)}), s8[524288]{0:T(1024)(128)(4,1)S(1)}, s32[]{:S(2)}) async-start(s8[4718592]{0:T(1024)(128)(4,1)} %bitcast), calls=%async_computation.1 | async-start | bytes 1048576
  47.4 6.6 %collective-permute-start.16 = (bf16[224,384]{1,0:T(8,128)(2,1)S(1)}, bf16[224,384]{1,0:T(8,128)(2,1)S(1)}, u32[]{:S(2)}, u32[]{:S(2)}) collective-permute-start(bf16[224,384]{1,0:T(8,128)(2,1)S(1)} %shard_map.122), channel_id=1, source_target_pairs={{0,8},{4,12},{8,0},{12,4},{16,24},{20,28},{24,16},{28,20},{1,9},{5... | collective-permute-start | bytes 516104 | tf_op jit(solution)/shard_map/x_back/ppermute | solution.py:125
  54.6 11.1 %collective-permute-start.18 = (bf16[224,768]{1,0:T(8,128)(2,1)S(1)}, bf16[224,768]{1,0:T(8,128)(2,1)S(1)}, u32[]{:S(2)}, u32[]{:S(2)}) collective-permute-start(bf16[224,768]{1,0:T(8,128)(2,1)S(1)} %shard_map.126), channel_id=1, source_target_pairs={{0,1},{1,0},{2,3},{3,2},{4,5},{5,4},{6,7},{7,6},{8,9},{9,8},{10,11... | collective-permute-start | bytes 1032200 | tf_op jit(solution)/shard_map/z_relay/ppermute | solution.py:125
  56.7 12.1 %copy-start.5 = (f32[768]{0:T(1024)S(1)}, f32[768]{0:T(1024)}, u32[]{:S(2)}) copy-start(f32[768]{0:T(1024)} %param.21) | copy-start | bytes 9220
  56.7 21.2 %collective-permute-start.17 = (bf16[224,768]{1,0:T(8,128)(2,1)S(1)}, bf16[224,768]{1,0:T(8,128)(2,1)S(1)}, u32[]{:S(2)}, u32[]{:S(2)}) collective-permute-start(bf16[224,768]{1,0:T(8,128)(2,1)S(1)} %shard_map.124), channel_id=1, source_target_pairs={{0,1},{1,0},{2,3},{3,2},{4,5},{5,4},{6,7},{7,6},{8,9},{9,8},{10,11... | collective-permute-start | bytes 1032200 | tf_op jit(solution)/shard_map/z_near/ppermute | solution.py:125
  66.1 15.6 %collective-permute-start.19 = (bf16[224,768]{1,0:T(8,128)(2,1)S(1)}, bf16[224,768]{1,0:T(8,128)(2,1)S(1)}, u32[]{:S(2)}, u32[]{:S(2)}) collective-permute-start(bf16[224,768]{1,0:T(8,128)(2,1)S(1)} %shard_map.127), channel_id=1, source_target_pairs={{0,2},{1,3},{2,0},{3,1},{4,6},{5,7},{6,4},{7,5},{8,10},{9,11},{10,... | collective-permute-start | bytes 1032200 | tf_op jit(solution)/shard_map/z_far/ppermute | solution.py:125
  68.8 9.1 %copy-start.3 = (bf16[224,768]{1,0:T(8,128)(2,1)S(1)}, bf16[224,768]{1,0:T(8,128)(2,1)}, u32[]{:S(2)}) copy-start(bf16[224,768]{1,0:T(8,128)(2,1)} %residual.1) | copy-start | bytes 1032196

commit v6 on v5

--- a/solution.py
+++ b/solution.py
@@ -441,7 +441,7 @@
 
     chosen = [
         choose(parts[j], ROW, j * first, keep, x_came[j], *after)
-        for j, after in enumerate(((kv_x,), (kv_xy, *near[4:],)))
+        for j, after in enumerate(((kv_x, kv_y), (kv_xy, *near[4:])))
     ]
     y_came = [swap(block, "frame", COLUMN, f"y_style_{j}") for j, block in enumerate(chosen)]
 

time: 82.7 us -> 82.7 us (level)
  no operation moved by 1% of the time
where the time goes in v6:
time: 82.7 us; the launch traced here: 82.5 us
  waiting for transfers between devices  39.2 us (47%)
  starting transfers between devices  23.1 us (28%)
  Pallas kernels  16.3 us (20%)
  other arithmetic  2.24 us (3%)
  between operations  1.61 us (2%)
    ppermute x18, waiting for transfers between devices, swap(): lax.ppermute(block, axis, [(i, i ^ bit) for i in range(lax.axis_size(axis...  39.2 us
    ppermute x18, starting transfers between devices, swap(): lax.ppermute(block, axis, [(i, i ^ bit) for i in range(lax.axis_size(axis...  19.3 us
    pallas_call x2, Pallas kernels, frames_of(): call(functools.partial(frames_kernel, remote), [SMEM, SMEM] + [VMEM] * 9,...  6.07 us
    pallas_call x4, Pallas kernels, style_of(): call(functools.partial(style_kernel, last), [VMEM] * 5, [((rows, width),...  6.04 us
    ppermute x1, starting transfers between devices, paired_device(): from_even = lax.ppermute(ref_values, 'frame', even)  2.5 us
    pallas_call x4, Pallas kernels, project(): call(functools.partial(project_kernel, bit), [VMEM] * (3 + len(came)), [(...  2.07 us
  transfers between devices with their start and end apart: 20, of which 10 were waited for; matrix products, arithmetic and copies ran while one was open for 0% of the time, Pallas kernels for 17%

profile of v6, /device:TPU:0, one launch (start us, length us, event | category | flops | bytes accessed | tf_op | source)
XLA Modules:
  0.0 82.5 jit_solution(837948467559922445)
XLA Ops:
  0.0 1.4 %broadcast_select_fusion = (bf16[224,384]{1,0:T(8,128)(2,1)S(1)}, bf16[224,384]{1,0:T(8,128)(2,1)S(1)}, bf16[224,384]{1,0:T(8,128)(2,1)S(1)}, bf16[224,384]{1,0:T(8,128)(2,1)S(1)}) fusion(pred[]{:T(512)S(6)} %not.3, bf16[224,768]{1,0:T(8,128)(2,1)} %param.13, pred[]{:T(512)S(6)} %eq.5, bf16[224,768]{1,0:T(8,128)(2,1)} %param.12), kind=kLoop, calls=%fused_computation.3 | loop fusion | flops 344064 | bytes 1376258 | tf_op jit(solution)/shard_map/jit(_where)/select_n | solution.py:390
  1.4 3.0 %collective-permute-start.3 = (bf16[224,768]{1,0:T(8,128)(2,1)S(1)}, bf16[224,768]{1,0:T(8,128)(2,1)S(1)}, u32[]{:S(2)}, u32[]{:S(2)}) collective-permute-start(bf16[224,768]{1,0:T(8,128)(2,1)S(1)} %pad_maximum_fusion.1), channel_id=1, source_target_pairs={{0,8},{4,12},{8,0},{12,4},{16,24},{20,28},{24,16},{28,20},{1,9},{5... | collective-permute-start | bytes 1032200 | tf_op jit(solution)/shard_map/x_kv/ppermute | solution.py:125
  4.4 1.6 %collective-permute-start = (bf16[224,768]{1,0:T(8,128)(2,1)S(1)}, bf16[224,768]{1,0:T(8,128)(2,1)S(1)}, u32[]{:S(2)}, u32[]{:S(2)}) collective-permute-start(bf16[224,768]{1,0:T(8,128)(2,1)S(1)} %pad_maximum_fusion.rest_0_), channel_id=1, source_target_pairs={{0,16},{4,20},{8,24},{12,28},{16,0},{20,4},{24,8},{28,12},{1,17},{... | collective-permute-start | bytes 1032200 | tf_op jit(solution)/shard_map/y_kv/ppermute | solution.py:125
  6.0 2.5 %collective-permute-start.1 = (bf16[1,1024,768]{2,1,0:T(8,128)(2,1)}, bf16[1,1024,768]{2,1,0:T(8,128)(2,1)S(1)}, u32[]{:S(2)}, u32[]{:S(2)}) collective-permute-start(bf16[1,1024,768]{2,1,0:T(8,128)(2,1)} %v.1), channel_id=1, source_target_pairs={{0,4},{8,12},{16,20},{24,28},{1,5},{9,13},{17,21},{25,29},{2,6},{1... | collective-permute-start | bytes 4718600 | tf_op jit(solution)/shard_map/core_style/ppermute | solution.py:384
  8.5 1.3 %collective-permute-start.2 = (bf16[1,1024,768]{2,1,0:T(8,128)(2,1)S(1)}, bf16[1,1024,768]{2,1,0:T(8,128)(2,1)S(1)}, u32[]{:S(2)}, u32[]{:S(2)}) collective-permute-start(bf16[1,1024,768]{2,1,0:T(8,128)(2,1)S(1)} %copy-done), channel_id=1, source_target_pairs={{4,0},{12,8},{20,16},{28,24},{5,1},{13,9},{21,17},{29,25},{6,2},{1... | collective-permute-start | bytes 4718600 | tf_op jit(solution)/shard_map/core_style/ppermute | solution.py:385
  10.5 2.0 %collective-permute-done.3.rest_0_.rest_1_ = bf16[224,768]{1,0:T(8,128)(2,1)S(1)} collective-permute-done((bf16[224,768]{1,0:T(8,128)(2,1)S(1)}, bf16[224,768]{1,0:T(8,128)(2,1)S(1)}, u32[]{:S(2)}, u32[]{:S(2)}) %collective-permute-start.3) | collective-permute-done | bytes 344096 | tf_op jit(solution)/shard_map/x_kv/ppermute | solution.py:125
  12.5 1.8 %collective-permute-start.6 = (bf16[224,768]{1,0:T(8,128)(2,1)S(1)}, bf16[224,768]{1,0:T(8,128)(2,1)S(1)}, u32[]{:S(2)}, u32[]{:S(2)}) collective-permute-start(bf16[224,768]{1,0:T(8,128)(2,1)S(1)} %collective-permute-done.3.rest_0_.rest_1_), channel_id=1, source_target_pairs={{0,16},{4,20},{8,24},{12,28},{16,0},{20,4},{24,8},{28,12},{1,17},{... | collective-permute-start | bytes 1032200 | tf_op jit(solution)/shard_map/xy_kv/ppermute | solution.py:125
  14.3 0.2 shard_map.111
  14.5 1.6 %collective-permute-start.13 = (bf16[512,384]{1,0:T(8,128)(2,1)S(1)}, bf16[512,384]{1,0:T(8,128)(2,1)S(1)}, u32[]{:S(2)}, u32[]{:S(2)}) collective-permute-start(bf16[512,384]{1,0:T(8,128)(2,1)S(1)} %get-tuple-element.24), channel_id=1, source_target_pairs={{0,8},{4,12},{8,0},{12,4},{16,24},{20,28},{24,16},{28,20},{1,9},{5... | collective-permute-start | bytes 1179656 | tf_op jit(solution)/shard_map/x_style_0/ppermute | solution.py:125
  16.1 0.2 shard_map.112
  16.3 0.6 collective-permute-start.5
  16.9 0.5 collective-permute-start.8
  17.4 4.4 %collective-permute-done.6.rest_0_.rest_3_ = bf16[224,768]{1,0:T(8,128)(2,1)S(1)} collective-permute-done((bf16[224,768]{1,0:T(8,128)(2,1)S(1)}, bf16[224,768]{1,0:T(8,128)(2,1)S(1)}, u32[]{:S(2)}, u32[]{:S(2)}) %collective-permute-start.6) | collective-permute-done | bytes 344096 | tf_op jit(solution)/shard_map/xy_kv/ppermute | solution.py:125
  21.8 4.9 %collective-permute-done.13.came = bf16[512,384]{1,0:T(8,128)(2,1)S(1)} collective-permute-done((bf16[512,384]{1,0:T(8,128)(2,1)S(1)}, bf16[512,384]{1,0:T(8,128)(2,1)S(1)}, u32[]{:S(2)}, u32[]{:S(2)}) %collective-permute-start.13) | collective-permute-done | bytes 393248 | tf_op jit(solution)/shard_map/x_style_0/ppermute | solution.py:125
  26.6 0.2 shard_map.117.here
  26.8 1.4 %collective-permute-start.14 = (bf16[512,384]{1,0:T(8,128)(2,1)S(1)}, bf16[512,384]{1,0:T(8,128)(2,1)S(1)}, u32[]{:S(2)}, u32[]{:S(2)}) collective-permute-start(bf16[512,384]{1,0:T(8,128)(2,1)S(1)} %shard_map.117.here), channel_id=1, source_target_pairs={{0,16},{4,20},{8,24},{12,28},{16,0},{20,4},{24,8},{28,12},{1,17},{... | collective-permute-start | bytes 1179656 | tf_op jit(solution)/shard_map/y_style_0/ppermute | solution.py:125
  28.9 0.7 shard_map.109
  29.6 1.6 %collective-permute-start.11 = (bf16[240,384]{1,0:T(8,128)(2,1)S(1)}, bf16[240,384]{1,0:T(8,128)(2,1)S(1)}, u32[]{:S(2)}, u32[]{:S(2)}) collective-permute-start(bf16[240,384]{1,0:T(8,128)(2,1)S(1)} %get-tuple-element.22), channel_id=1, source_target_pairs={{0,8},{4,12},{8,0},{12,4},{16,24},{20,28},{24,16},{28,20},{1,9},{5... | collective-permute-start | bytes 552968 | tf_op jit(solution)/shard_map/x_q/ppermute | solution.py:125
  31.2 3.9 %collective-permute-done.5.came = bf16[512,384]{1,0:T(8,128)(2,1)S(1)} collective-permute-done((bf16[512,384]{1,0:T(8,128)(2,1)S(1)}, bf16[512,384]{1,0:T(8,128)(2,1)S(1)}, u32[]{:S(2)}, u32[]{:S(2)}) %collective-permute-start.5) | collective-permute-done | bytes 393248 | tf_op jit(solution)/shard_map/x_style_1/ppermute | solution.py:125
  35.1 0.2 shard_map.113.here
  35.3 1.3 %collective-permute-start.10 = (bf16[512,384]{1,0:T(8,128)(2,1)S(1)}, bf16[512,384]{1,0:T(8,128)(2,1)S(1)}, u32[]{:S(2)}, u32[]{:S(2)}) collective-permute-start(bf16[512,384]{1,0:T(8,128)(2,1)S(1)} %shard_map.113.here), channel_id=1, source_target_pairs={{0,16},{4,20},{8,24},{12,28},{16,0},{20,4},{24,8},{28,12},{1,17},{... | collective-permute-start | bytes 1179656 | tf_op jit(solution)/shard_map/y_style_1/ppermute | solution.py:125
  36.6 3.0 %shard_map.114 = (f32[224,384]{1,0:T(8,128)S(1)}, f32[224,128]{1,0:T(8,128)S(1)}) custom-call(s32[1,8]{1,0:T(1,128)S(1)} %copy-done.4, s32[1]{0:T(128)S(6)} %copy.12.counts, bf16[224,384]{1,0:T(8,128)(2,1)S(1)} %get-tuple-element.18.q, bf16[224,768]{1,0:T(8,128)(2,1)S(1)} %pad_maximum_fusion.rest_0_, ...), custom_call_target="tpu_custom_call" | custom-call | flops 3000000000 | bytes 1 | tf_op jit(solution)/shard_map/pallas_call | solution.py:435
  39.6 0.2 shard_map.118.held
  39.8 0.1 collective-permute-start.15
  39.9 3.1 %shard_map.115 = (f32[224,384]{1,0:T(8,128)S(1)}, f32[224,128]{1,0:T(8,128)S(1)}) custom-call(s32[1,8]{1,0:T(1,128)S(1)} %copy-done.4, s32[1]{0:T(128)S(6)} %copy.12.counts, bf16[240,384]{1,0:T(8,128)(2,1)S(1)} %collective-permute-done.11.q, bf16[224,768]{1,0:T(8,128)(2,1)S(1)} %pad_maximum_fusion.rest_0_, ...), custom_call_target="tpu_custom_call" | custom-call | flops 3000000000 | bytes 1 | tf_op jit(solution)/shard_map/pallas_call | solution.py:435
  43.0 0.7 collective-permute-done.10.came
  43.7 0.2 shard_map.116.held
  44.0 0.1 collective-permute-start.12
  44.0 0.0 slice-start.1
  44.1 1.4 %shard_map.121 = (f32[224,384]{1,0:T(8,128)S(1)}, f32[224,128]{1,0:T(8,128)S(1)}) custom-call(bf16[240,384]{1,0:T(8,128)(2,1)S(1)} %collective-permute-done.11.q, bf16[512,384]{1,0:T(8,128)(2,1)S(1)} %shard_map.118.held, bf16[512,384]{1,0:T(8,128)(2,1)S(1)} %collective-permute-done.15.swapped, f32[224,384]{1,0:T(8,128)S(1)} %get-tuple-element.28.acc_in, ...), custom_call_target="tpu_custom_call" | custom-call | flops 1000000000 | bytes 1 | tf_op jit(solution)/shard_map/pallas_call | solution.py:453
  45.5 0.2 collective-permute-done.12.swapped
  45.7 1.7 %shard_map.122 = bf16[224,384]{1,0:T(8,128)(2,1)S(1)} custom-call(bf16[240,384]{1,0:T(8,128)(2,1)S(1)} %collective-permute-done.11.q, bf16[512,384]{1,0:T(8,128)(2,1)S(1)} %shard_map.116.held, bf16[512,384]{1,0:T(8,128)(2,1)S(1)} %collective-permute-done.12.swapped, f32[224,384]{1,0:T(8,128)S(1)} %get-tuple-element.29.acc_in, ...), custom_call_target="tpu_custom_call" | custom-call | flops 1000000000 | bytes 1 | tf_op jit(solution)/shard_map/pallas_call | solution.py:453
  47.4 1.1 %collective-permute-start.16 = (bf16[224,384]{1,0:T(8,128)(2,1)S(1)}, bf16[224,384]{1,0:T(8,128)(2,1)S(1)}, u32[]{:S(2)}, u32[]{:S(2)}) collective-permute-start(bf16[224,384]{1,0:T(8,128)(2,1)S(1)} %shard_map.122), channel_id=1, source_target_pairs={{0,8},{4,12},{8,0},{12,4},{16,24},{20,28},{24,16},{28,20},{1,9},{5... | collective-permute-start | bytes 516104 | tf_op jit(solution)/shard_map/x_back/ppermute | solution.py:125
  48.5 1.4 %shard_map.119 = (f32[224,384]{1,0:T(8,128)S(1)}, f32[224,128]{1,0:T(8,128)S(1)}) custom-call(bf16[224,384]{1,0:T(8,128)(2,1)S(1)} %get-tuple-element.18.q, bf16[512,384]{1,0:T(8,128)(2,1)S(1)} %shard_map.118.held, bf16[512,384]{1,0:T(8,128)(2,1)S(1)} %collective-permute-done.15.swapped, f32[224,384]{1,0:T(8,128)S(1)} %get-tuple-element.25.acc_in, ...), custom_call_target="tpu_custom_call" | custom-call | flops 1000000000 | bytes 1 | tf_op jit(solution)/shard_map/pallas_call | solution.py:453
  49.9 1.5 %shard_map.120.own = bf16[224,384]{1,0:T(8,128)(2,1)S(1)} custom-call(bf16[224,384]{1,0:T(8,128)(2,1)S(1)} %get-tuple-element.18.q, bf16[512,384]{1,0:T(8,128)(2,1)S(1)} %shard_map.116.held, bf16[512,384]{1,0:T(8,128)(2,1)S(1)} %collective-permute-done.12.swapped, f32[224,384]{1,0:T(8,128)S(1)} %get-tuple-element.26.acc_in, ...), custom_call_target="tpu_custom_call" | custom-call | flops 1000000000 | bytes 1 | tf_op jit(solution)/shard_map/pallas_call | solution.py:453
  51.4 2.6 %collective-permute-done.16.got = bf16[224,384]{1,0:T(8,128)(2,1)S(1)} collective-permute-done((bf16[224,384]{1,0:T(8,128)(2,1)S(1)}, bf16[224,384]{1,0:T(8,128)(2,1)S(1)}, u32[]{:S(2)}, u32[]{:S(2)}) %collective-permute-start.16) | collective-permute-done | bytes 172064 | tf_op jit(solution)/shard_map/x_back/ppermute | solution.py:125
  54.0 0.5 shard_map.126
  54.5 1.7 %collective-permute-start.18 = (bf16[224,768]{1,0:T(8,128)(2,1)S(1)}, bf16[224,768]{1,0:T(8,128)(2,1)S(1)}, u32[]{:S(2)}, u32[]{:S(2)}) collective-permute-start(bf16[224,768]{1,0:T(8,128)(2,1)S(1)} %shard_map.126), channel_id=1, source_target_pairs={{0,1},{1,0},{2,3},{3,2},{4,5},{5,4},{6,7},{7,6},{8,9},{9,8},{10,11... | collective-permute-start | bytes 1032200 | tf_op jit(solution)/shard_map/z_relay/ppermute | solution.py:125
  56.2 0.5 shard_map.124
  56.7 0.5 collective-permute-start.17
  57.2 8.4 %collective-permute-done.18.rest_0_ = bf16[224,768]{1,0:T(8,128)(2,1)S(1)} collective-permute-done((bf16[224,768]{1,0:T(8,128)(2,1)S(1)}, bf16[224,768]{1,0:T(8,128)(2,1)S(1)}, u32[]{:S(2)}, u32[]{:S(2)}) %collective-permute-start.18) | collective-permute-done | bytes 344096 | tf_op jit(solution)/shard_map/z_relay/ppermute | solution.py:125
  65.6 0.5 shard_map.127
  66.1 2.7 %collective-permute-start.19 = (bf16[224,768]{1,0:T(8,128)(2,1)S(1)}, bf16[224,768]{1,0:T(8,128)(2,1)S(1)}, u32[]{:S(2)}, u32[]{:S(2)}) collective-permute-start(bf16[224,768]{1,0:T(8,128)(2,1)S(1)} %shard_map.127), channel_id=1, source_target_pairs={{0,2},{1,3},{2,0},{3,1},{4,6},{5,7},{6,4},{7,5},{8,10},{9,11},{10,... | collective-permute-start | bytes 1032200 | tf_op jit(solution)/shard_map/z_far/ppermute | solution.py:125
  68.8 0.5 shard_map.123.own
  69.3 8.6 %collective-permute-done.17.near = bf16[224,768]{1,0:T(8,128)(2,1)S(1)} collective-permute-done((bf16[224,768]{1,0:T(8,128)(2,1)S(1)}, bf16[224,768]{1,0:T(8,128)(2,1)S(1)}, u32[]{:S(2)}, u32[]{:S(2)}) %collective-permute-start.17) | collective-permute-done | bytes 344096 | tf_op jit(solution)/shard_map/z_near/ppermute | solution.py:125
  77.9 0.1 shard_map.125
  78.0 3.7 %collective-permute-done.19 = bf16[224,768]{1,0:T(8,128)(2,1)S(1)} collective-permute-done((bf16[224,768]{1,0:T(8,128)(2,1)S(1)}, bf16[224,768]{1,0:T(8,128)(2,1)S(1)}, u32[]{:S(2)}, u32[]{:S(2)}) %collective-permute-start.19) | collective-permute-done | bytes 344096 | tf_op jit(solution)/shard_map/z_far/ppermute | solution.py:125
  81.7 0.8 add_convert_fusion
  (34 shorter events, 0.2 us)
Async XLA Ops:
  0.0 8.5 %copy-start = (bf16[1,1024,768]{2,1,0:T(8,128)(2,1)S(1)}, bf16[1,1024,768]{2,1,0:T(8,128)(2,1)}, u32[]{:S(2)}) copy-start(bf16[1,1024,768]{2,1,0:T(8,128)(2,1)} %k.1) | copy-start | bytes 4718596
  1.4 11.1 %collective-permute-start.3 = (bf16[224,768]{1,0:T(8,128)(2,1)S(1)}, bf16[224,768]{1,0:T(8,128)(2,1)S(1)}, u32[]{:S(2)}, u32[]{:S(2)}) collective-permute-start(bf16[224,768]{1,0:T(8,128)(2,1)S(1)} %pad_maximum_fusion.1), channel_id=1, source_target_pairs={{0,8},{4,12},{8,0},{12,4},{16,24},{20,28},{24,16},{28,20},{1,9},{5... | collective-permute-start | bytes 1032200 | tf_op jit(solution)/shard_map/x_kv/ppermute | solution.py:125
  4.4 9.8 %collective-permute-start = (bf16[224,768]{1,0:T(8,128)(2,1)S(1)}, bf16[224,768]{1,0:T(8,128)(2,1)S(1)}, u32[]{:S(2)}, u32[]{:S(2)}) collective-permute-start(bf16[224,768]{1,0:T(8,128)(2,1)S(1)} %pad_maximum_fusion.rest_0_), channel_id=1, source_target_pairs={{0,16},{4,20},{8,24},{12,28},{16,0},{20,4},{24,8},{28,12},{1,17},{... | collective-permute-start | bytes 1032200 | tf_op jit(solution)/shard_map/y_kv/ppermute | solution.py:125
  6.0 10.1 %collective-permute-start.4 = (bf16[224,768]{1,0:T(8,128)(2,1)S(1)}, bf16[224,768]{1,0:T(8,128)(2,1)S(1)}, u32[]{:S(2)}, u32[]{:S(2)}) collective-permute-start(bf16[224,768]{1,0:T(8,128)(2,1)S(1)} %pad_maximum_fusion.rest_0_), channel_id=1, source_target_pairs={{0,4},{4,0},{8,12},{12,8},{16,20},{20,16},{24,28},{28,24},{1,5},{5... | collective-permute-start | bytes 1032200 | tf_op jit(solution)/shard_map/c_kv_0/ppermute | solution.py:125
  6.0 8.2 %collective-permute-start.1 = (bf16[1,1024,768]{2,1,0:T(8,128)(2,1)}, bf16[1,1024,768]{2,1,0:T(8,128)(2,1)S(1)}, u32[]{:S(2)}, u32[]{:S(2)}) collective-permute-start(bf16[1,1024,768]{2,1,0:T(8,128)(2,1)} %v.1), channel_id=1, source_target_pairs={{0,4},{8,12},{16,20},{24,28},{1,5},{9,13},{17,21},{25,29},{2,6},{1... | collective-permute-start | bytes 4718600 | tf_op jit(solution)/shard_map/core_style/ppermute | solution.py:384
  8.5 5.7 %collective-permute-start.2 = (bf16[1,1024,768]{2,1,0:T(8,128)(2,1)S(1)}, bf16[1,1024,768]{2,1,0:T(8,128)(2,1)S(1)}, u32[]{:S(2)}, u32[]{:S(2)}) collective-permute-start(bf16[1,1024,768]{2,1,0:T(8,128)(2,1)S(1)} %copy-done), channel_id=1, source_target_pairs={{4,0},{12,8},{20,16},{28,24},{5,1},{13,9},{21,17},{29,25},{6,2},{1... | collective-permute-start | bytes 4718600 | tf_op jit(solution)/shard_map/core_style/ppermute | solution.py:385
  12.5 1.8 %copy-start.1 = (bf16[1,1024,768]{2,1,0:T(8,128)(2,1)S(1)}, bf16[1,1024,768]{2,1,0:T(8,128)(2,1)}, u32[]{:S(2)}) copy-start(bf16[1,1024,768]{2,1,0:T(8,128)(2,1)} %v.1) | copy-start | bytes 4718596
  12.5 9.3 %collective-permute-start.6 = (bf16[224,768]{1,0:T(8,128)(2,1)S(1)}, bf16[224,768]{1,0:T(8,128)(2,1)S(1)}, u32[]{:S(2)}, u32[]{:S(2)}) collective-permute-start(bf16[224,768]{1,0:T(8,128)(2,1)S(1)} %collective-permute-done.3.rest_0_.rest_1_), channel_id=1, source_target_pairs={{0,16},{4,20},{8,24},{12,28},{16,0},{20,4},{24,8},{28,12},{1,17},{... | collective-permute-start | bytes 1032200 | tf_op jit(solution)/shard_map/xy_kv/ppermute | solution.py:125
  14.5 12.1 %collective-permute-start.13 = (bf16[512,384]{1,0:T(8,128)(2,1)S(1)}, bf16[512,384]{1,0:T(8,128)(2,1)S(1)}, u32[]{:S(2)}, u32[]{:S(2)}) collective-permute-start(bf16[512,384]{1,0:T(8,128)(2,1)S(1)} %get-tuple-element.24), channel_id=1, source_target_pairs={{0,8},{4,12},{8,0},{12,4},{16,24},{20,28},{24,16},{28,20},{1,9},{5... | collective-permute-start | bytes 1179656 | tf_op jit(solution)/shard_map/x_style_0/ppermute | solution.py:125
  16.1 12.8 %copy-start.2 = (bf16[224,768]{1,0:T(8,128)(2,1)S(1)}, bf16[224,768]{1,0:T(8,128)(2,1)}, u32[]{:S(2)}) copy-start(bf16[224,768]{1,0:T(8,128)(2,1)} %q.1) | copy-start | bytes 1032196
  16.1 12.8 %copy-start.4 = (s32[1,8]{1,0:T(1,128)S(1)}, s32[1,8]{1,0:T(1,128)}, u32[]{:S(2)}) copy-start(s32[1,8]{1,0:T(1,128)} %lists.5) | copy-start | bytes 100
  16.3 18.8 %collective-permute-start.5 = (bf16[512,384]{1,0:T(8,128)(2,1)S(1)}, bf16[512,384]{1,0:T(8,128)(2,1)S(1)}, u32[]{:S(2)}, u32[]{:S(2)}) collective-permute-start(bf16[512,384]{1,0:T(8,128)(2,1)S(1)} %shard_map.112), channel_id=1, source_target_pairs={{0,8},{4,12},{8,0},{12,4},{16,24},{20,28},{24,16},{28,20},{1,9},{5... | collective-permute-start | bytes 1179656 | tf_op jit(solution)/shard_map/x_style_1/ppermute | solution.py:125
  16.9 12.7 %collective-permute-start.7 = (bf16[224,768]{1,0:T(8,128)(2,1)S(1)}, bf16[224,768]{1,0:T(8,128)(2,1)S(1)}, u32[]{:S(2)}, u32[]{:S(2)}) collective-permute-start(bf16[224,768]{1,0:T(8,128)(2,1)S(1)} %collective-permute-done.3.rest_0_.rest_1_), channel_id=1, source_target_pairs={{0,4},{4,0},{8,12},{12,8},{16,20},{20,16},{24,28},{28,24},{1,5},{5... | collective-permute-start | bytes 1032200 | tf_op jit(solution)/shard_map/c_kv_1/ppermute | solution.py:125
  16.9 14.3 %collective-permute-start.8 = (bf16[224,768]{1,0:T(8,128)(2,1)S(1)}, bf16[224,768]{1,0:T(8,128)(2,1)S(1)}, u32[]{:S(2)}, u32[]{:S(2)}) collective-permute-start(bf16[224,768]{1,0:T(8,128)(2,1)S(1)} %collective-permute-done.after.rest_1_.rest_2_), channel_id=1, source_target_pairs={{0,4},{4,0},{8,12},{12,8},{16,20},{20,16},{24,28},{28,24},{1,5},{5... | collective-permute-start | bytes 1032200 | tf_op jit(solution)/shard_map/c_kv_2/ppermute | solution.py:125
  21.8 9.4 %collective-permute-start.9 = (bf16[224,768]{1,0:T(8,128)(2,1)S(1)}, bf16[224,768]{1,0:T(8,128)(2,1)S(1)}, u32[]{:S(2)}, u32[]{:S(2)}) collective-permute-start(bf16[224,768]{1,0:T(8,128)(2,1)S(1)} %collective-permute-done.6.rest_0_.rest_3_), channel_id=1, source_target_pairs={{0,4},{4,0},{8,12},{12,8},{16,20},{20,16},{24,28},{28,24},{1,5},{5... | collective-permute-start | bytes 1032200 | tf_op jit(solution)/shard_map/c_kv_3/ppermute | solution.py:125
  26.8 12.7 %collective-permute-start.14 = (bf16[512,384]{1,0:T(8,128)(2,1)S(1)}, bf16[512,384]{1,0:T(8,128)(2,1)S(1)}, u32[]{:S(2)}, u32[]{:S(2)}) collective-permute-start(bf16[512,384]{1,0:T(8,128)(2,1)S(1)} %shard_map.117.here), channel_id=1, source_target_pairs={{0,16},{4,20},{8,24},{12,28},{16,0},{20,4},{24,8},{28,12},{1,17},{... | collective-permute-start | bytes 1179656 | tf_op jit(solution)/shard_map/y_style_0/ppermute | solution.py:125
  29.6 10.3 %collective-permute-start.11 = (bf16[240,384]{1,0:T(8,128)(2,1)S(1)}, bf16[240,384]{1,0:T(8,128)(2,1)S(1)}, u32[]{:S(2)}, u32[]{:S(2)}) collective-permute-start(bf16[240,384]{1,0:T(8,128)(2,1)S(1)} %get-tuple-element.22), channel_id=1, source_target_pairs={{0,8},{4,12},{8,0},{12,4},{16,24},{20,28},{24,16},{28,20},{1,9},{5... | collective-permute-start | bytes 552968 | tf_op jit(solution)/shard_map/x_q/ppermute | solution.py:125
  35.3 8.5 %collective-permute-start.10 = (bf16[512,384]{1,0:T(8,128)(2,1)S(1)}, bf16[512,384]{1,0:T(8,128)(2,1)S(1)}, u32[]{:S(2)}, u32[]{:S(2)}) collective-permute-start(bf16[512,384]{1,0:T(8,128)(2,1)S(1)} %shard_map.113.here), channel_id=1, source_target_pairs={{0,16},{4,20},{8,24},{12,28},{16,0},{20,4},{24,8},{28,12},{1,17},{... | collective-permute-start | bytes 1179656 | tf_op jit(solution)/shard_map/y_style_1/ppermute | solution.py:125
  39.8 4.2 %collective-permute-start.15 = (bf16[512,384]{1,0:T(8,128)(2,1)S(1)}, bf16[512,384]{1,0:T(8,128)(2,1)S(1)}, u32[]{:S(2)}, u32[]{:S(2)}) collective-permute-start(bf16[512,384]{1,0:T(8,128)(2,1)S(1)} %shard_map.118.held), channel_id=1, source_target_pairs={{0,4},{4,0},{8,12},{12,8},{16,20},{20,16},{24,28},{28,24},{1,5},{5... | collective-permute-start | bytes 1179656 | tf_op jit(solution)/shard_map/c_style_0/ppermute | solution.py:125
  39.9 14.1 %slice-start = ((s8[4718592]{0:T(1024)(128)(4,1)}), s8[4194304]{0:T(1024)(128)(4,1)S(1)}, s32[]{:S(2)}) async-start(s8[4718592]{0:T(1024)(128)(4,1)} %bitcast), calls=%async_computation | async-start | bytes 8388608
  44.0 1.8 %collective-permute-start.12 = (bf16[512,384]{1,0:T(8,128)(2,1)S(1)}, bf16[512,384]{1,0:T(8,128)(2,1)S(1)}, u32[]{:S(2)}, u32[]{:S(2)}) collective-permute-start(bf16[512,384]{1,0:T(8,128)(2,1)S(1)} %shard_map.116.held), channel_id=1, source_target_pairs={{0,4},{4,0},{8,12},{12,8},{16,20},{20,16},{24,28},{28,24},{1,5},{5... | collective-permute-start | bytes 1179656 | tf_op jit(solution)/shard_map/c_style_1/ppermute | solution.py:125
  44.0 10.0 %slice-start.1 = ((s8[4718592]{0:T(1024)(128)(4,1)}), s8[524288]{0:T(1024)(128)(4,1)S(1)}, s32[]{:S(2)}) async-start(s8[4718592]{0:T(1024)(128)(4,1)} %bitcast), calls=%async_computation.1 | async-start | bytes 1048576
  47.4 6.6 %collective-permute-start.16 = (bf16[224,384]{1,0:T(8,128)(2,1)S(1)}, bf16[224,384]{1,0:T(8,128)(2,1)S(1)}, u32[]{:S(2)}, u32[]{:S(2)}) collective-permute-start(bf16[224,384]{1,0:T(8,128)(2,1)S(1)} %shard_map.122), channel_id=1, source_target_pairs={{0,8},{4,12},{8,0},{12,4},{16,24},{20,28},{24,16},{28,20},{1,9},{5... | collective-permute-start | bytes 516104 | tf_op jit(solution)/shard_map/x_back/ppermute | solution.py:125
  54.5 11.1 %collective-permute-start.18 = (bf16[224,768]{1,0:T(8,128)(2,1)S(1)}, bf16[224,768]{1,0:T(8,128)(2,1)S(1)}, u32[]{:S(2)}, u32[]{:S(2)}) collective-permute-start(bf16[224,768]{1,0:T(8,128)(2,1)S(1)} %shard_map.126), channel_id=1, source_target_pairs={{0,1},{1,0},{2,3},{3,2},{4,5},{5,4},{6,7},{7,6},{8,9},{9,8},{10,11... | collective-permute-start | bytes 1032200 | tf_op jit(solution)/shard_map/z_relay/ppermute | solution.py:125
  56.7 12.1 %copy-start.5 = (f32[768]{0:T(1024)S(1)}, f32[768]{0:T(1024)}, u32[]{:S(2)}) copy-start(f32[768]{0:T(1024)} %param.21) | copy-start | bytes 9220
  56.7 21.2 %collective-permute-start.17 = (bf16[224,768]{1,0:T(8,128)(2,1)S(1)}, bf16[224,768]{1,0:T(8,128)(2,1)S(1)}, u32[]{:S(2)}, u32[]{:S(2)}) collective-permute-start(bf16[224,768]{1,0:T(8,128)(2,1)S(1)} %shard_map.124), channel_id=1, source_target_pairs={{0,1},{1,0},{2,3},{3,2},{4,5},{5,4},{6,7},{7,6},{8,9},{9,8},{10,11... | collective-permute-start | bytes 1032200 | tf_op jit(solution)/shard_map/z_near/ppermute | solution.py:125
  66.1 15.6 %collective-permute-start.19 = (bf16[224,768]{1,0:T(8,128)(2,1)S(1)}, bf16[224,768]{1,0:T(8,128)(2,1)S(1)}, u32[]{:S(2)}, u32[]{:S(2)}) collective-permute-start(bf16[224,768]{1,0:T(8,128)(2,1)S(1)} %shard_map.127), channel_id=1, source_target_pairs={{0,2},{1,3},{2,0},{3,1},{4,6},{5,7},{6,4},{7,5},{8,10},{9,11},{10,... | collective-permute-start | bytes 1032200 | tf_op jit(solution)/shard_map/z_far/ppermute | solution.py:125
  68.8 9.1 %copy-start.3 = (bf16[224,768]{1,0:T(8,128)(2,1)S(1)}, bf16[224,768]{1,0:T(8,128)(2,1)}, u32[]{:S(2)}) copy-start(bf16[224,768]{1,0:T(8,128)(2,1)} %residual.1) | copy-start | bytes 1032196
